TPU v7x, 256 devices: a whole 4x4x8 slice. The times are simulated.
256 devices in a mesh: seq: 64 (over z, x, core), head: 4 (over y).
Axes of the slice: x: 4, y: 4, z: 8, core: 2. Of those that a mesh axis runs over, the one named last changes fastest.
Arguments:
- queries: bfloat16 [8704, 1024], P('seq', 'head'), may hold values from -5 to 5
- key_rows: bfloat16 [8704, 1024], P('seq', 'head'), may hold values from -5 to 5
- value_rows: bfloat16 [8704, 1024], P('seq', 'head'), may hold values from -6 to 6
- scale_of: int32 [8704], P('seq'), may hold values from -1 to 12, as said below
- wo: bfloat16 [1024, 2048], P('head'), may hold values from -0.1875 to 0.1875
- dy: bfloat16 [8704, 2048], P('seq', 'head'), may hold values from -16 to 16
Outputs:
- block_out: bfloat16 [8704, 2048], P('seq', 'head')
- dq: bfloat16 [8704, 1024], P('seq', 'head')
- dk: bfloat16 [8704, 1024], P('seq', 'head')
- dv: bfloat16 [8704, 1024], P('seq', 'head')
- dwo: float32 [1024, 2048], P('head', 'seq')
Inputs may be any that keep to these rules, and one draw needn't show every extreme that they name: `scale_of`: in each aligned block of 136 rows (one index of seq) the first 128 rows hold ids 13 - 3 to 12, not falling over these rows of all blocks taken in order, each of the three ids present; the last 8 rows of a block are all -1 except in exactly 4 blocks, whose last rows hold ids 0 to 9, not falling within the block.
All inputs are finite; a program needn't handle non-finite values.
Results may differ from a plain program's by a relative error of at most 0.035.
Values may be sent and summed in bfloat16 or wider, within the bound.
No kernel may reach another device: no remote copies, remote signals or barrier semaphores. Data moves between devices by JAX's collectives and lax.ppermute only.
A program may use at most 192 MiB of HBM per device.

v0:
```python
import functools
import math

import jax
import jax.numpy as jnp
from jax import lax
from jax.experimental import pallas as pl
from jax.experimental.pallas import tpu as pltpu
from jax.sharding import Mesh, PartitionSpec as P

DH = 128
ROWS = 136
PAD = 144
FINE = 128
REST = PAD - FINE
PAIR = 2 * PAD
NH = 4
QHALF = 8
NQ = QHALF * PAD
NK = 2 * NQ
QREST = QHALF * FINE
SUMS = 80
LOAD = PAIR + SUMS
FEATS = 2 * DH
MODEL = 2048
WIDE = MODEL // NH
COLS = 32
BLOCK = 384
BIG = -1e30
SCALE = DH ** (-0.5)
UNIT = SCALE * math.log2(math.e)
F32 = jnp.float32
BF16 = jnp.bfloat16
LAST = (((1,), (1,)), ((), ()))
FIRST = (((0,), (0,)), ((), ()))
PARAMS = pltpu.CompilerParams(vmem_limit_bytes=48 << 20)
VMEM = pl.BlockSpec(memory_space=pltpu.VMEM)
SMEM = pl.BlockSpec(memory_space=pltpu.SMEM)


def shape(dims, kind=BF16):
    return jax.ShapeDtypeStruct(dims, kind)


def call(kernel, name, ins, outs, scratch=(), scalars=0, flops=0):
    cost = pl.CostEstimate(flops=flops, bytes_accessed=1 << 20, transcendentals=0) if flops else None
    return pl.pallas_call(
        kernel,
        in_specs=[SMEM] * scalars + [VMEM] * (len(ins) - scalars),
        out_shape=outs,
        scratch_shapes=list(scratch),
        compiler_params=PARAMS,
        cost_estimate=cost,
        name=name,
    )(*ins)


def by_parity(e, first, second, keep_ref, send_ref):
    @pl.when(e == 0)
    def _():
        keep_ref[...] = first
        send_ref[...] = second

    @pl.when(e == 1)
    def _():
        keep_ref[...] = second
        send_ref[...] = first


def pack_kernel(at_ref, all_ref, ids_ref, keep_ref, send_ref, dy_ref):
    ids = ids_ref[...].astype(BF16)
    zero = jnp.zeros((8, DH), BF16)
    heads = []
    for head in range(2):
        q, k, v = (all_ref[:, i * FEATS + head * DH : i * FEATS + (head + 1) * DH] for i in range(3))
        heads.append(jnp.concatenate([k, ids, v, zero, q, ids], axis=0))
    by_parity(at_ref[0], heads[0], heads[1], keep_ref, send_ref)
    dy_ref[...] = all_ref[:, 3 * FEATS : 3 * FEATS + WIDE]


def dattn_kernel(at_ref, *refs):
    dy_refs, (wo_ref, ids_ref, keep_ref, send_ref) = refs[0:4], refs[4:]
    acc = jnp.zeros((ROWS, FEATS), F32)
    for s, ref in enumerate(dy_refs):
        block = wo_ref[:, s * WIDE : (s + 1) * WIDE]
        acc = acc + lax.dot_general(ref[...], block, LAST, preferred_element_type=F32)
    ids = ids_ref[...].T
    real = jnp.concatenate([ids[:, 0:1], ids[0:8, 1:2]], axis=0) >= 0.0
    acc = jnp.where(real, acc, 0.0).astype(BF16)
    acc = jnp.concatenate([acc, jnp.zeros((PAD - ROWS, FEATS), BF16)], axis=0)
    by_parity(at_ref[0], acc[:, 0:DH], acc[:, DH:FEATS], keep_ref, send_ref)


def pairs_of(refs, slots, top):
    found = [None] * 4
    for i, slot in enumerate(slots):
        found[slot] = (refs[i // 2], top + i % 2 * PAIR)
    return found


def assemble(pairs, all_ref, base, cols):
    rest = base + QREST
    for j, (ref, at) in enumerate(pairs):
        for k in range(2):
            half = 2 * j + k
            top = at + k * PAD
            all_ref[base + half * FINE : base + (half + 1) * FINE, cols] = ref[top : top + FINE]
            all_ref[rest + half * REST : rest + (half + 1) * REST, cols] = ref[top + FINE : top + PAD]


def take_pair(value, j):
    pieces = []
    for half in (2 * j, 2 * j + 1):
        pieces.append(value[half * FINE : (half + 1) * FINE])
        pieces.append(value[QREST + half * REST : QREST + (half + 1) * REST])
    return jnp.concatenate(pieces, axis=0)


def masks(pairs, mask_ref, base, is_query):
    fine, last = [], []
    for ref, at in pairs:
        for k in range(2):
            rows = ref[at + k * PAD + FINE : at + (k + 1) * PAD].astype(F32)
            fine.append(rows[8:9])
            last.append(rows[9:10])
    fine = jnp.concatenate(fine, axis=0).T
    last = jnp.concatenate(last, axis=0).T
    rest = base + QREST

    def encode(column):
        lane = lax.broadcasted_iota(jnp.int32, (column.shape[0], DH), 1).astype(F32)
        if is_query:
            hidden = ((lane > column) & (lane < 13.0)) | (lane == 13.0)
            return jnp.where(hidden, BIG, 0.0).astype(BF16)
        return jnp.where(lane == jnp.where(column < 0.0, 13.0, column), 1.0, 0.0).astype(BF16)

    for half in range(2 * len(pairs)):
        mask_ref[base + half * FINE : base + (half + 1) * FINE] = encode(fine[:, half : half + 1])
        mask_ref[rest + half * REST : rest + (half + 1) * REST] = encode(last[0:REST, half : half + 1])


def in_three(row):
    high = row.astype(BF16).astype(F32)
    middle = (row - high).astype(BF16).astype(F32)
    return [high, middle, row - high - middle]


def forward_kernel(*refs):
    o_ref, stat_ref, q_ref, qm_ref, kv_ref, km_ref = refs[8:14]
    left, right = slice(0, DH), slice(DH, FEATS)
    queries = [(ref, 0) for ref in refs[0:4]]
    assemble(queries, q_ref, 0, left)
    masks(queries, qm_ref, 0, True)
    for base, parts in ((0, refs[4:6]), (NQ, refs[6:8])):
        keys = pairs_of(parts, (0, 1, 3, 2), 0)
        assemble(keys, kv_ref, base, left)
        assemble(pairs_of(parts, (0, 3, 1, 2), 2 * PAIR), kv_ref, base, right)
        masks(keys, km_ref, base, False)
    k_ext = jnp.concatenate([kv_ref[:, 0:DH], km_ref[...]], axis=1)
    lane = lax.broadcasted_iota(jnp.int32, (BLOCK, DH), 1)
    for block in range(NQ // BLOCK):
        rows = slice(block * BLOCK, (block + 1) * BLOCK)
        q_ext = jnp.concatenate([q_ref[rows], qm_ref[rows]], axis=1)
        s = lax.dot_general(q_ext, k_ext, LAST, preferred_element_type=F32)
        top = jnp.max(s, axis=1, keepdims=True)
        p = jnp.exp2((s - top) * UNIT)
        total = jnp.sum(p, axis=1, keepdims=True)
        o = jnp.dot(p.astype(BF16), kv_ref[:, DH:FEATS], preferred_element_type=F32) / total
        o_ref[rows] = o
        lse = top * UNIT + jnp.log2(total)
        stat_ref[:, rows] = jnp.where(lane == 0, lse, 0.0).T[0:8]


def share_kernel(*refs):
    o_ref, stat_ref, load_refs, da_ref, delta_ref = refs[4], refs[5], refs[6:10], refs[10], refs[11]
    assemble([(ref, 0) for ref in refs[0:4]], da_ref, 0, slice(0, DH))
    lane = lax.broadcasted_iota(jnp.int32, (BLOCK, DH), 1)
    for block in range(NQ // BLOCK):
        rows = slice(block * BLOCK, (block + 1) * BLOCK)
        share = jnp.sum(o_ref[rows] * da_ref[rows].astype(F32), axis=1, keepdims=True)
        delta_ref[:, rows] = jnp.where(lane == 0, share, 0.0).T[0:8]
    none = jnp.zeros((2, NQ), F32)
    sums = jnp.concatenate(in_three(stat_ref[0:1]) + in_three(delta_ref[0:1]) + [none], axis=0)
    tiles = [sums[:, i * DH : (i + 1) * DH] for i in range(NQ // DH)] + [jnp.zeros((8, DH), F32)]
    sums = jnp.concatenate(tiles, axis=0).astype(BF16)
    for j in range(4):
        load_refs[j][0:PAIR] = take_pair(o_ref, j).astype(BF16)
        load_refs[j][PAIR:LOAD] = sums


def row_sums(load_refs):
    lses, shares = [], []
    odd = lax.broadcasted_iota(jnp.int32, (8, DH), 1) % (4 * REST) >= 2 * REST
    for s, ref in enumerate(load_refs):
        sums = ref[PAIR:LOAD].astype(F32)
        tiles = [sums[8 * i : 8 * i + 8] for i in range(9)]
        last = tiles[8]
        if s % 2 == 1:
            last = jnp.where(odd, pltpu.roll(last, 2 * REST, 1), pltpu.roll(last, FINE - 2 * REST, 1))
        if s >= 2:
            last = pltpu.roll(last, FINE // 2, 1)
        rows = jnp.concatenate([tiles[2 * (j ^ s) + k] for j in range(4) for k in range(2)] + [last], axis=1)
        lses.append(rows[0:1] + rows[1:2] + rows[2:3])
        shares.append(rows[3:4] + rows[4:5] + rows[5:6])
    top = jnp.maximum(jnp.maximum(lses[0], lses[1]), jnp.maximum(lses[2], lses[3]))
    weights = [jnp.exp2(one - top) for one in lses]
    total = weights[0] + weights[1] + weights[2] + weights[3]
    delta = sum(weights[s] * shares[s] for s in range(4)) / total
    lse = top + jnp.log2(total)
    return jnp.where(lse < -1e28, 1e30, lse), delta


def backward_kernel(base, first, last, q_ref, qm_ref, da_ref, kv_ref, km_ref, *refs):
    load_refs, refs = refs[0:4], refs[4:]
    if first > 0 or base == 0:
        dq_in_ref, refs = refs[0], refs[1:]
    if first > 0:
        rows_in_ref, refs = refs[0], refs[1:]
    out_refs, dkv_ref, ds_ref = refs[:-2], refs[-2], refs[-1]
    lse, delta = row_sums(load_refs)
    q = q_ref[...]
    da = da_ref[...]
    q_ext = jnp.concatenate([q, qm_ref[...]], axis=1)
    if first > 0:
        dkv_ref[0 : first * BLOCK] = rows_in_ref[...]
    for block in range(first, last):
        rows = slice(block * BLOCK, (block + 1) * BLOCK)
        keys = slice(base + block * BLOCK, base + (block + 1) * BLOCK)
        k_ext = jnp.concatenate([kv_ref[keys, 0:DH], km_ref[keys]], axis=1)
        s = lax.dot_general(k_ext, q_ext, LAST, preferred_element_type=F32)
        p = jnp.exp2(s * UNIT - lse)
        dp = lax.dot_general(kv_ref[keys, DH:FEATS], da, LAST, preferred_element_type=F32)
        ds = (p * (dp - delta)).astype(BF16)
        dkv_ref[rows, DH:FEATS] = jnp.dot(p.astype(BF16), da, preferred_element_type=F32).astype(BF16)
        dkv_ref[rows, 0:DH] = (jnp.dot(ds, q, preferred_element_type=F32) * SCALE).astype(BF16)
        ds_ref[rows] = ds
    if last * BLOCK < NQ:
        out_refs[0][...] = dkv_ref[0 : last * BLOCK]
    else:
        for j in range(4):
            pair = take_pair(dkv_ref, j)
            out_refs[0][j] = pair[:, 0:DH]
            out_refs[0][4 + j] = pair[:, DH:FEATS]
    rows = slice(first * BLOCK, last * BLOCK)
    keys = slice(base + rows.start, base + rows.stop)
    dq = lax.dot_general(ds_ref[rows], kv_ref[keys, 0:DH], FIRST, preferred_element_type=F32)
    if first > 0 or base == 0:
        dq = dq + dq_in_ref[...]
    if base > 0:
        out_refs[1][...] = dq
    else:
        dq = dq * SCALE
        for at, (mine, theirs) in enumerate(((0, 1), (3, 2))):
            out_refs[1][at * PAIR : (at + 1) * PAIR] = take_pair(dq, mine)
            out_refs[2][at * PAIR : (at + 1) * PAIR] = take_pair(dq, theirs).astype(BF16)


def merge_kernel(l0_ref, l1_ref, l2_ref, l3_ref, keep_ref, send_ref):
    load_refs = (l0_ref, l1_ref, l2_ref, l3_ref)
    fine, last = [], []
    for s, ref in enumerate(load_refs):
        sums = ref[PAIR:LOAD].astype(F32)
        rows = sums[0:72]
        lse = [rows[8 * i : 8 * i + 1] + rows[8 * i + 1 : 8 * i + 2] + rows[8 * i + 2 : 8 * i + 3] for i in (2 * s, 2 * s + 1, 8)]
        fine += lse[0:2]
        last.append(lse[2] if s == 0 else pltpu.roll(lse[2], FINE - 2 * REST * s, 1))
    fine = jnp.concatenate(fine, axis=0).T
    last = jnp.concatenate(last + last, axis=0).T
    for k, out_ref in ((0, keep_ref), (1, send_ref)):
        for rows, columns in (
            (slice(0, FINE), [fine[:, 2 * s + k : 2 * s + k + 1] for s in range(4)]),
            (slice(FINE, PAD), [last[k * REST : (k + 1) * REST, s : s + 1] for s in range(4)]),
        ):
            source = slice(k * PAD + rows.start, k * PAD + rows.stop)
            top = jnp.maximum(jnp.maximum(columns[0], columns[1]), jnp.maximum(columns[2], columns[3]))
            weights = [jnp.exp2(one - top) for one in columns]
            total = weights[0] + weights[1] + weights[2] + weights[3]
            acc = sum(weights[s] * load_refs[s][source].astype(F32) for s in range(4))
            out_ref[rows] = (acc * jnp.where(top < -1e28, 0.0, 1.0 / total)).astype(BF16)


def project_kernel(at_ref, mine_ref, other_ref, wo_ref, dy0_ref, dy1_ref, dy2_ref, dy3_ref, *refs):
    out_refs, keep_ref, send_ref, dwo_ref = refs[0:4], *refs[4:7]
    e, h, zr, x, c = (at_ref[i] for i in range(5))
    mine, other = mine_ref[...], other_ref[...]
    even = e == 0
    attn = jnp.concatenate([jnp.where(even, mine, other), jnp.where(even, other, mine)], axis=1)
    for s in range(NH):
        at = -s % NH * WIDE
        part = jnp.dot(attn, wo_ref[:, at : at + WIDE], preferred_element_type=F32)
        out_refs[s][...] = part[0:ROWS].astype(BF16)
    for s, ref in enumerate((dy0_ref, dy1_ref, dy2_ref, dy3_ref)):
        dwo_ref[s] = lax.dot_general(ref[...], attn[0:ROWS], FIRST, preferred_element_type=F32).astype(BF16)
    for xt in range(4):
        for et in range(2):
            for t in range(4):
                s = lax.rem(h - jnp.bitwise_xor(zr, t) + NH, NH)
                row = lax.rem(e + et, 2) * 256 + jnp.bitwise_xor(x, xt) * 64
                to = slice((et * 4 + t) * COLS, (et * 4 + t + 1) * COLS)
                keep_ref[xt, to] = dwo_ref[s, pl.ds(pl.multiple_of(row + c * COLS, COLS), COLS)]
                send_ref[xt, to] = dwo_ref[s, pl.ds(pl.multiple_of(row + (1 - c) * COLS, COLS), COLS)]


def split_up(total, mine, theirs, keep_ref, send_ref):
    rows = total.shape[1]
    for at in range(len(mine)):
        keep_ref[at * rows : (at + 1) * rows] = total[mine[at]]
        send_ref[at * rows : (at + 1) * rows] = total[theirs[at]].astype(BF16)


def core_kernel(keep_ref, got_ref, *refs):
    total = keep_ref[...].astype(F32) + got_ref[...].astype(F32)
    split_up(total[0:4], (0, 3), (1, 2), refs[0], refs[1])
    split_up(total[4:8], (0, 1), (3, 2), refs[2], refs[3])


def dwo_kernel(keep_ref, got_ref, mine_ref, send_ref):
    total = keep_ref[...].astype(F32) + got_ref[...].astype(F32)
    split_up(total, (0, 1), (3, 2), mine_ref, send_ref)


def middle_kernel(*refs):
    count = len(refs) // 4
    for i in range(count):
        keep_ref, got_ref = refs[2 * i : 2 * i + 2]
        mine_ref, send_ref = refs[2 * (count + i) : 2 * (count + i) + 2]
        rows = mine_ref.shape[0]
        total = keep_ref[...] + got_ref[...].astype(F32)
        mine_ref[...] = total[0:rows]
        send_ref[...] = total[rows : 2 * rows].astype(BF16)


def ring_kernel(mine_ref, got_ref, keep_ref, send_ref):
    total = mine_ref[...] + got_ref[...].astype(F32)
    for et in range(2):
        at = et * 4 * COLS
        to = et * 2 * COLS
        keep_ref[to : to + 2 * COLS] = total[at : at + 2 * COLS]
        send_ref[to : to + COLS] = total[at + 3 * COLS : at + 4 * COLS].astype(BF16)
        send_ref[to + COLS : to + 2 * COLS] = total[at + 2 * COLS : at + 3 * COLS].astype(BF16)


def half_kernel(keep_ref, got_ref, out_ref, send_ref):
    total = keep_ref[...] + got_ref[...].astype(F32)
    for et in range(2):
        out_ref[et * COLS : (et + 1) * COLS] = total[et * 2 * COLS : (et * 2 + 1) * COLS]
        send_ref[et * COLS : (et + 1) * COLS] = total[(et * 2 + 1) * COLS : (et * 2 + 2) * COLS].astype(BF16)


def total_kernel(*refs):
    wkeep_ref, wgot_ref, keep_ref, wmine_ref, send_ref = refs[6:11]
    for i in range(3):
        total = (refs[2 * i][...] + refs[2 * i + 1][...].astype(F32)).astype(BF16)
        keep_ref[:, i * DH : (i + 1) * DH] = total[0:PAD]
        send_ref[i * PAD : (i + 1) * PAD] = total[PAD:PAIR]
    weights = wkeep_ref[...] + wgot_ref[...].astype(F32)
    wmine_ref[...] = weights[0:COLS]
    piece = weights[COLS : 2 * COLS].astype(BF16)
    send_ref[3 * PAD : 3 * PAD + COLS] = piece[:, 0:DH]
    send_ref[3 * PAD + COLS : 3 * PAD + 2 * COLS] = piece[:, DH:FEATS]


def place_kernel(at_ref, mine_ref, wmine_ref, got_ref, dq_ref, dk_ref, dv_ref, dwo_ref):
    even = at_ref[0] == 0
    for i, ref in enumerate((dq_ref, dk_ref, dv_ref)):
        mine = mine_ref[0:ROWS, i * DH : (i + 1) * DH]
        other = got_ref[i * PAD : i * PAD + ROWS]
        ref[:, 0:DH] = jnp.where(even, mine, other)
        ref[:, DH:FEATS] = jnp.where(even, other, mine)
    got = got_ref[3 * PAD : 3 * PAD + 2 * COLS].astype(F32)
    dwo_ref[...] = wmine_ref[...] + jnp.concatenate([got[0:COLS], got[COLS : 2 * COLS]], axis=1)


def shifted(value, axis, size, by):
    return lax.ppermute(value, axis, [(i, (i + by) % size) for i in range(size)])


def swapped(value, axis, size, mask):
    return lax.ppermute(value, axis, [(i, i ^ mask) for i in range(size)])


def around(value, axis):
    return [value] + [shifted(value, axis, 4, s) for s in (1, 2, 3)]


def local(queries, key_rows, value_rows, scale_of, wo, dy):
    axes = ("e", "head", "zr", "x", "c")
    at = jnp.stack([lax.axis_index(name) for name in axes]).astype(jnp.int32)
    ids = jnp.pad(scale_of, (0, 8 * DH - ROWS), constant_values=-1).reshape(8, DH).astype(F32)
    pair = (PAIR, DH)

    keep, send, dy = call(
        pack_kernel,
        "pack",
        [at, jnp.concatenate([queries, key_rows, value_rows, dy], axis=1), ids],
        [shape((3 * PAD, DH))] * 2 + [shape((ROWS, WIDE))],
        scalars=1,
    )
    got = swapped(send, "e", 2, 1)
    dy, send = lax.optimization_barrier((dy, send))
    k, v, q = (jnp.concatenate([keep[i : i + PAD], got[i : i + PAD]], axis=0) for i in (0, PAD, 2 * PAD))
    first = [swapped(k, "zr", 4, 1), swapped(v, "zr", 4, 3), swapped(q, "x", 4, 1), swapped(q, "x", 4, 3)]
    k_got, v_got, q_one, q_three = lax.optimization_barrier(first)
    k, v = jnp.concatenate([k, k_got], axis=0), jnp.concatenate([v, v_got], axis=0)
    dys = around(dy, "head")
    k, v, dys = lax.optimization_barrier((k, v, dys))
    ks, vs = [k, swapped(k, "zr", 4, 3)], [v, swapped(v, "zr", 4, 1)]
    qs = [q, q_one, swapped(q, "x", 4, 2), q_three]
    wo, _ = lax.optimization_barrier((wo, dy))
    at_head = lax.axis_index("head")
    wo = jnp.concatenate(
        [lax.dynamic_slice_in_dim(wo, lax.rem(at_head - s + NH, NH) * WIDE, WIDE, 1) for s in range(NH)], axis=1
    )
    keep, send = call(dattn_kernel, "dattn", [at, *dys, wo, ids], [shape((PAD, DH))] * 2, scalars=1)
    da = jnp.concatenate([keep, swapped(send, "e", 2, 1)], axis=0)
    das = [da] + [swapped(da, "x", 4, s) for s in (1, 2, 3)]
    ks[1], vs[1], das[1], das[3] = lax.optimization_barrier((ks[1], vs[1], das[1], das[3]))
    kvs = [jnp.concatenate([ks[i], vs[i]], axis=0) for i in range(2)]
    kvs = kvs + [swapped(one, "c", 2, 1) for one in kvs]

    rows = (NQ, DH)
    o, stat, q, qm, kv, km = call(
        forward_kernel,
        "forward",
        [*qs, *kvs],
        [shape(rows, F32), shape((8, NQ), F32), shape(rows), shape(rows), shape((NK, FEATS)), shape((NK, DH))],
        flops=6 * NQ * NK * DH,
    )
    *loads, da = call(
        share_kernel, "share", [*das, o, stat], [shape((LOAD, DH))] * 4 + [shape(rows)], [pltpu.VMEM((8, NQ), F32)]
    )
    loads = [loads[0]] + [swapped(loads[s], "x", 4, s) for s in (1, 2, 3)]

    keep, send = call(merge_kernel, "merge", loads, [shape((PAD, DH))] * 2)
    other = swapped(send, "e", 2, 1)
    q, send = lax.optimization_barrier((q, send))
    scratch = [pltpu.VMEM((NQ, FEATS), BF16), pltpu.VMEM((NQ, NQ), BF16)]
    sides = [q, qm, da, kv, km, *loads]
    dkv_part, dq_part = call(
        functools.partial(backward_kernel, NQ, 0, 2),
        "backward_one",
        sides,
        [shape((2 * BLOCK, FEATS)), shape(rows, F32)],
        scratch,
        flops=4 * NQ * NK * DH,
    )
    other, dq_part = lax.optimization_barrier((other, dq_part))
    *outs, wkeep, wsend = call(
        project_kernel,
        "project",
        [at, keep, other, wo, *dys],
        [shape((ROWS, WIDE))] * 4 + [shape((4, 256, FEATS))] * 2,
        [pltpu.VMEM((4, WIDE, FEATS), BF16)],
        scalars=1,
    )
    wsend, dq_part = lax.optimization_barrier((wsend, dq_part))
    dkv_send, dq_part = call(
        functools.partial(backward_kernel, NQ, 2, 3),
        "backward_two",
        [*sides, dq_part, dkv_part],
        [shape((8, *pair)), shape(rows, F32)],
        scratch,
        flops=2 * NQ * NK * DH,
    )
    wgot, dq_part = lax.optimization_barrier((swapped(wsend, "c", 2, 1), dq_part))
    wkeep, wsend = call(
        dwo_kernel, "dwo", [wkeep, wgot], [shape((512, FEATS), F32), shape((512, FEATS))]
    )
    wsend, dq_part = lax.optimization_barrier((wsend, dq_part))
    twice = (2 * PAIR, DH)
    dkv_keep, dq_keep, dq_send = call(
        functools.partial(backward_kernel, 0, 0, 3),
        "backward_three",
        [*sides, dq_part],
        [shape((8, *pair)), shape(twice, F32), shape(twice)],
        scratch,
        flops=6 * NQ * NK * DH,
    )
    dk_keep, dk_send, dv_keep, dv_send = call(
        core_kernel, "core", [dkv_keep, swapped(dkv_send, "c", 2, 1)], [shape(twice, F32), shape(twice)] * 2
    )
    wgot, dk_send = lax.optimization_barrier((swapped(wsend, "x", 4, 3), dk_send))
    wkeep, wsend = call(
        middle_kernel, "middle_dwo", [wkeep, wgot], [shape((256, FEATS), F32), shape((256, FEATS))]
    )
    wkeep, wsend = call(
        ring_kernel,
        "ring",
        [wkeep, swapped(wsend, "x", 4, 1)],
        [shape((128, FEATS), F32), shape((128, FEATS))],
    )
    wsend, outs[1], outs[3] = lax.optimization_barrier((wsend, outs[1], outs[3]))
    landed = [swapped(dk_send, "zr", 4, 1), swapped(dv_send, "zr", 4, 3), swapped(dq_send, "x", 4, 1), wsend]
    landed += [shifted(outs[1], "head", NH, 1), shifted(outs[3], "head", NH, 3)]
    dk_got, dv_got, dq_got, wsend, out_one, out_three = lax.optimization_barrier(landed)
    dk, dk_send, dv, dv_send, dq, dq_send = call(
        middle_kernel,
        "middle",
        [dk_keep, dk_got, dv_keep, dv_got, dq_keep, dq_got],
        [shape(pair, F32), shape(pair)] * 3,
    )
    wgot, dq_got = swapped(wsend, "zr", 4, 3), swapped(dq_send, "x", 4, 3)
    dk_got, dv_got = swapped(dk_send, "zr", 4, 3), swapped(dv_send, "zr", 4, 1)
    wkeep, wsend = call(half_kernel, "half", [wkeep, wgot], [shape((64, FEATS), F32), shape((64, FEATS))])
    out_two = shifted(outs[2], "head", NH, 2)
    block_out = sum(one.astype(F32) for one in (outs[0], out_one, out_two, out_three)).astype(BF16)
    keep, wkeep, send = call(
        total_kernel,
        "total",
        [dq, dq_got, dk, dk_got, dv, dv_got]
        + [wkeep, swapped(wsend, "zr", 4, 1)],
        [shape((PAD, 3 * DH)), shape((COLS, FEATS), F32), shape((3 * PAD + 2 * COLS, DH))],
    )
    dq, dk, dv, dwo = call(
        place_kernel,
        "place",
        [at, keep, wkeep, swapped(send, "e", 2, 1)],
        [shape((ROWS, FEATS))] * 3 + [shape((COLS, FEATS), F32)],
        scalars=1,
    )
    return (block_out, dq, dk, dv, dwo.T)


def solution(mesh):
    fine = Mesh(mesh.devices.reshape(4, 2, 4, 2, NH), ("zr", "e", "x", "c", "head"))
    seq = ("zr", "e", "x", "c")
    placed = (
        P(seq, "head"),
        P(seq, "head"),
        P(seq, "head"),
        P(seq),
        P("head", None),
        P(seq, "head"),
    )
    return jax.shard_map(
        local,
        mesh=fine,
        in_specs=placed,
        out_specs=(
            P(seq, "head"),
            P(seq, "head"),
            P(seq, "head"),
            P(seq, "head"),
            P("head", seq),
        ),
        check_vma=False,
    )
```

profile of v0, /device:TPU:8, one launch (start us, length us, event | category | flops | bytes accessed | tf_op | source)
XLA Modules:
  0.0 114.2 jit_solution(2980962409837810849)
XLA Ops:
  0.6 0.8 convert_bitcast_fusion.ids_ref.refs_5_
  1.4 1.0 pad_maximum_fusion.1.all_ref
  2.6 0.6 pack.1
  3.2 2.0 %collective-permute-start = (bf16[432,128]{1,0:T(8,128)(2,1)S(1)}, bf16[432,128]{1,0:T(8,128)(2,1)S(1)}, u32[]{:S(2)}, u32[]{:S(2)}) collective-permute-start(bf16[432,128]{1,0:T(8,128)(2,1)S(1)} %get-tuple-element.98), channel_id=1, source_target_pairs={{0,32},{32,0},{1,33},{33,1},{2,34},{34,2},{3,35},{35,3},{4,36},{36... | collective-permute-start | bytes 331784 | tf_op jit(solution)/shard_map/ppermute | solution.py:379
  5.2 0.4 collective-permute-start.7
  5.6 2.6 %collective-permute-start.6 = (bf16[136,512]{1,0:T(8,128)(2,1)S(1)}, bf16[136,512]{1,0:T(8,128)(2,1)S(1)}, u32[]{:S(2)}, u32[]{:S(2)}) collective-permute-start(bf16[136,512]{1,0:T(8,128)(2,1)S(1)} %get-tuple-element.103.refs_0_.dy0_ref), channel_id=1, source_target_pairs={{0,2},{1,3},{2,0},{3,1},{4,6},{5,7},{6,4},{7,5},{8,10},{9,11},{10,... | collective-permute-start | bytes 417800 | tf_op jit(solution)/shard_map/ppermute | solution.py:375
  8.2 1.9 %collective-permute-start.5 = (bf16[136,512]{1,0:T(8,128)(2,1)S(1)}, bf16[136,512]{1,0:T(8,128)(2,1)S(1)}, u32[]{:S(2)}, u32[]{:S(2)}) collective-permute-start(bf16[136,512]{1,0:T(8,128)(2,1)S(1)} %get-tuple-element.103.refs_0_.dy0_ref), channel_id=1, source_target_pairs={{0,1},{1,2},{2,3},{3,0},{4,5},{5,6},{6,7},{7,4},{8,9},{9,10},{10,1... | collective-permute-start | bytes 417800 | tf_op jit(solution)/shard_map/ppermute | solution.py:375
  10.3 3.4 %collective-permute-start.1 = (bf16[288,128]{1,0:T(8,128)(2,1)S(1)}, bf16[288,128]{1,0:T(8,128)(2,1)S(1)}, u32[]{:S(2)}, u32[]{:S(2)}) collective-permute-start(bf16[288,128]{1,0:T(8,128)(2,1)S(1)} %pad_maximum_fusion.4), channel_id=1, source_target_pairs={{0,64},{64,0},{128,192},{192,128},{1,65},{65,1},{129,193},{193,129... | collective-permute-start | bytes 221192 | tf_op jit(solution)/shard_map/ppermute | solution.py:379
  13.7 3.6 %collective-permute-start.2 = (bf16[288,128]{1,0:T(8,128)(2,1)S(1)}, bf16[288,128]{1,0:T(8,128)(2,1)S(1)}, u32[]{:S(2)}, u32[]{:S(2)}) collective-permute-start(bf16[288,128]{1,0:T(8,128)(2,1)S(1)} %pad_maximum_fusion.5), channel_id=1, source_target_pairs={{0,192},{64,128},{128,64},{192,0},{1,193},{65,129},{129,65},{193,1... | collective-permute-start | bytes 221192 | tf_op jit(solution)/shard_map/ppermute | solution.py:379
  17.3 2.8 %collective-permute-start.4 = (bf16[288,128]{1,0:T(8,128)(2,1)S(1)}, bf16[288,128]{1,0:T(8,128)(2,1)S(1)}, u32[]{:S(2)}, u32[]{:S(2)}) collective-permute-start(bf16[288,128]{1,0:T(8,128)(2,1)S(1)} %pad_maximum_fusion.6.refs_0_), channel_id=1, source_target_pairs={{0,24},{8,16},{16,8},{24,0},{1,25},{9,17},{17,9},{25,1},{2,26},{10... | collective-permute-start | bytes 221192 | tf_op jit(solution)/shard_map/ppermute | solution.py:379
  20.1 0.5 collective-permute-done.2
  20.6 1.5 %collective-permute-start.3 = (bf16[288,128]{1,0:T(8,128)(2,1)S(1)}, bf16[288,128]{1,0:T(8,128)(2,1)S(1)}, u32[]{:S(2)}, u32[]{:S(2)}) collective-permute-start(bf16[288,128]{1,0:T(8,128)(2,1)S(1)} %pad_maximum_fusion.6.refs_0_), channel_id=1, source_target_pairs={{0,8},{8,0},{16,24},{24,16},{1,9},{9,1},{17,25},{25,17},{2,10},{10... | collective-permute-start | bytes 221192 | tf_op jit(solution)/shard_map/ppermute | solution.py:379
  22.2 0.7 collective-permute-done.4.refs_3_
  22.9 2.0 %collective-permute-done.3.refs_1_ = bf16[288,128]{1,0:T(8,128)(2,1)S(1)} collective-permute-done((bf16[288,128]{1,0:T(8,128)(2,1)S(1)}, bf16[288,128]{1,0:T(8,128)(2,1)S(1)}, u32[]{:S(2)}, u32[]{:S(2)}) %collective-permute-start.3) | collective-permute-done | bytes 73760 | tf_op jit(solution)/shard_map/ppermute | solution.py:379
  25.0 4.0 %collective-permute-start.9 = (bf16[576,128]{1,0:T(8,128)(2,1)S(1)}, bf16[576,128]{1,0:T(8,128)(2,1)S(1)}, u32[]{:S(2)}, u32[]{:S(2)}) collective-permute-start(bf16[576,128]{1,0:T(8,128)(2,1)S(1)} %get-tuple-element.110), channel_id=1, source_target_pairs={{0,192},{64,128},{128,64},{192,0},{1,193},{65,129},{129,65},{193,1... | collective-permute-start | bytes 442376 | tf_op jit(solution)/shard_map/ppermute | solution.py:379
  29.0 1.5 %collective-permute-start.10 = (bf16[576,128]{1,0:T(8,128)(2,1)S(1)}, bf16[576,128]{1,0:T(8,128)(2,1)S(1)}, u32[]{:S(2)}, u32[]{:S(2)}) collective-permute-start(bf16[576,128]{1,0:T(8,128)(2,1)S(1)} %get-tuple-element.111), channel_id=1, source_target_pairs={{0,64},{64,0},{128,192},{192,128},{1,65},{65,1},{129,193},{193,129... | collective-permute-start | bytes 442376 | tf_op jit(solution)/shard_map/ppermute | solution.py:379
  30.6 1.0 dattn.1
  31.6 1.1 collective-permute-start.8
  32.7 3.1 %collective-permute-done.8 = bf16[144,128]{1,0:T(8,128)(2,1)S(1)} collective-permute-done((bf16[144,128]{1,0:T(8,128)(2,1)S(1)}, bf16[144,128]{1,0:T(8,128)(2,1)S(1)}, u32[]{:S(2)}, u32[]{:S(2)}) %collective-permute-start.8) | collective-permute-done | bytes 36896 | tf_op jit(solution)/shard_map/ppermute | solution.py:379
  35.8 2.0 %collective-permute-start.12 = (bf16[288,128]{1,0:T(8,128)(2,1)S(1)}, bf16[288,128]{1,0:T(8,128)(2,1)S(1)}, u32[]{:S(2)}, u32[]{:S(2)}) collective-permute-start(bf16[288,128]{1,0:T(8,128)(2,1)S(1)} %constant_dynamic-update-slice_fusion.refs_0_), channel_id=1, source_target_pairs={{0,24},{8,16},{16,8},{24,0},{1,25},{9,17},{17,9},{25,1},{2,26},{10... | collective-permute-start | bytes 221192 | tf_op jit(solution)/shard_map/ppermute | solution.py:379
  37.8 0.2 collective-permute-start.11
  38.2 3.3 %collective-permute-done.12.refs_3_ = bf16[288,128]{1,0:T(8,128)(2,1)S(1)} collective-permute-done((bf16[288,128]{1,0:T(8,128)(2,1)S(1)}, bf16[288,128]{1,0:T(8,128)(2,1)S(1)}, u32[]{:S(2)}, u32[]{:S(2)}) %collective-permute-start.12) | collective-permute-done | bytes 73760 | tf_op jit(solution)/shard_map/ppermute | solution.py:379
  41.5 0.7 collective-permute-done.11.refs_1_
  42.3 0.9 collective-permute-start.14
  43.2 2.7 %collective-permute-start.13 = (bf16[288,128]{1,0:T(8,128)(2,1)S(1)}, bf16[288,128]{1,0:T(8,128)(2,1)S(1)}, u32[]{:S(2)}, u32[]{:S(2)}) collective-permute-start(bf16[288,128]{1,0:T(8,128)(2,1)S(1)} %constant_dynamic-update-slice_fusion.refs_0_), channel_id=1, source_target_pairs={{0,16},{8,24},{16,0},{24,8},{1,17},{9,25},{17,1},{25,9},{2,18},{10... | collective-permute-start | bytes 221192 | tf_op jit(solution)/shard_map/ppermute | solution.py:379
  45.9 3.0 %collective-permute-done.14.refs_2_ = bf16[288,128]{1,0:T(8,128)(2,1)S(1)} collective-permute-done((bf16[288,128]{1,0:T(8,128)(2,1)S(1)}, bf16[288,128]{1,0:T(8,128)(2,1)S(1)}, u32[]{:S(2)}, u32[]{:S(2)}) %collective-permute-start.14) | collective-permute-done | bytes 73760 | tf_op jit(solution)/shard_map/ppermute | solution.py:379
  49.0 5.0 %forward.1 = (f32[1152,128]{1,0:T(8,128)S(1)}, f32[8,1152]{1,0:T(8,128)S(1)}, bf16[1152,128]{1,0:T(8,128)(2,1)S(1)}, bf16[1152,128]{1,0:T(8,128)(2,1)S(1)}, bf16...) custom-call(bf16[288,128]{1,0:T(8,128)(2,1)S(1)} %pad_maximum_fusion.6.refs_0_, ...), custom_call_target="tpu_custom_call" | custom-call | flops 2038431744 | bytes 1048576 | tf_op jit(solution)/shard_map/forward/pallas_call | solution.py:47
  54.0 0.4 share.1
  54.6 2.6 %collective-permute-start.18 = (bf16[368,128]{1,0:T(8,128)(2,1)S(1)}, bf16[368,128]{1,0:T(8,128)(2,1)S(1)}, u32[]{:S(2)}, u32[]{:S(2)}) collective-permute-start(bf16[368,128]{1,0:T(8,128)(2,1)S(1)} %get-tuple-element.122), channel_id=1, source_target_pairs={{0,16},{8,24},{16,0},{24,8},{1,17},{9,25},{17,1},{25,9},{2,18},{10... | collective-permute-start | bytes 282632 | tf_op jit(solution)/shard_map/ppermute | solution.py:379
  57.2 2.1 %collective-permute-start.19 = (bf16[368,128]{1,0:T(8,128)(2,1)S(1)}, bf16[368,128]{1,0:T(8,128)(2,1)S(1)}, u32[]{:S(2)}, u32[]{:S(2)}) collective-permute-start(bf16[368,128]{1,0:T(8,128)(2,1)S(1)} %get-tuple-element.123), channel_id=1, source_target_pairs={{0,24},{8,16},{16,8},{24,0},{1,25},{9,17},{17,9},{25,1},{2,26},{10... | collective-permute-start | bytes 282632 | tf_op jit(solution)/shard_map/ppermute | solution.py:379
  59.3 1.9 %collective-permute-done.18.l2_ref.refs_2_ = bf16[368,128]{1,0:T(8,128)(2,1)S(1)} collective-permute-done((bf16[368,128]{1,0:T(8,128)(2,1)S(1)}, bf16[368,128]{1,0:T(8,128)(2,1)S(1)}, u32[]{:S(2)}, u32[]{:S(2)}) %collective-permute-start.18) | collective-permute-done | bytes 94240 | tf_op jit(solution)/shard_map/ppermute | solution.py:379
  61.2 1.8 %collective-permute-done.19.l3_ref.refs_3_ = bf16[368,128]{1,0:T(8,128)(2,1)S(1)} collective-permute-done((bf16[368,128]{1,0:T(8,128)(2,1)S(1)}, bf16[368,128]{1,0:T(8,128)(2,1)S(1)}, u32[]{:S(2)}, u32[]{:S(2)}) %collective-permute-start.19) | collective-permute-done | bytes 94240 | tf_op jit(solution)/shard_map/ppermute | solution.py:379
  63.0 0.8 merge.1
  63.8 1.6 %collective-permute-start.20 = (bf16[144,128]{1,0:T(8,128)(2,1)S(1)}, bf16[144,128]{1,0:T(8,128)(2,1)S(1)}, u32[]{:S(2)}, u32[]{:S(2)}) collective-permute-start(bf16[144,128]{1,0:T(8,128)(2,1)S(1)} %get-tuple-element.125), channel_id=1, source_target_pairs={{0,32},{32,0},{1,33},{33,1},{2,34},{34,2},{3,35},{35,3},{4,36},{36... | collective-permute-start | bytes 110600 | tf_op jit(solution)/shard_map/ppermute | solution.py:379
  65.4 2.8 %backward_one.1 = (bf16[768,256]{1,0:T(8,128)(2,1)S(1)}, f32[1152,128]{1,0:T(8,128)S(1)}) custom-call(bf16[1152,128]{1,0:T(8,128)(2,1)S(1)} %get-tuple-element.127.q_ref, bf16[1152,128]{1,0:T(8,128)(2,1)S(1)} %get-tuple-element.128.qm_ref, bf16[1152,128]{1,0:T(8,128)(2,1)S(1)} %get-tuple-element.129.da_ref, bf16[2304,256]{1,0:T(8,128)(2,1)S(1)} %get-tuple-element.130.kv_ref, ...), custom_call_target="tpu_custom_call" | custom-call | flops 1358954496 | bytes 1048576 | tf_op jit(solution)/shard_map/backward_one/pallas_call | solution.py:47
  68.2 1.2 %project.1 = (bf16[136,512]{1,0:T(8,128)(2,1)S(1)}, bf16[136,512]{1,0:T(8,128)(2,1)S(1)}, bf16[136,512]{1,0:T(8,128)(2,1)S(1)}, bf16[136,512]{1,0:T(8,128)(2,1)S...) custom-call(s32[5]{0:T(128)S(1)} %stack.23.at_ref, ...), custom_call_target="tpu_custom_call" | custom-call | tf_op jit(solution)/shard_map/project/pallas_call | solution.py:47
  69.5 0.3 collective-permute-start.21
  69.8 1.6 %backward_two.1 = (bf16[8,288,128]{2,1,0:T(8,128)(2,1)S(1)}, f32[1152,128]{1,0:T(8,128)S(1)}) custom-call(bf16[1152,128]{1,0:T(8,128)(2,1)S(1)} %get-tuple-element.127.q_ref, bf16[1152,128]{1,0:T(8,128)(2,1)S(1)} %get-tuple-element.128.qm_ref, bf16[1152,128]{1,0:T(8,128)(2,1)S(1)} %get-tuple-element.129.da_ref, ...), custom_call_target="tpu_custom_call" | custom-call | flops 679477248 | bytes 1048576 | tf_op jit(solution)/shard_map/backward_two/pallas_call | solution.py:47
  71.4 0.6 collective-permute-start.23
  72.1 2.4 %collective-permute-start.22 = (bf16[512,256]{1,0:T(8,128)(2,1)S(1)}, bf16[512,256]{1,0:T(8,128)(2,1)S(1)}, u32[]{:S(2)}, u32[]{:S(2)}) collective-permute-start(bf16[512,256]{1,0:T(8,128)(2,1)S(1)} %get-tuple-element.145), channel_id=1, source_target_pairs={{0,24},{8,16},{16,8},{24,0},{1,25},{9,17},{17,9},{25,1},{2,26},{10... | collective-permute-start | bytes 786440 | tf_op jit(solution)/shard_map/ppermute | solution.py:379
  74.4 4.2 %backward_three.1 = (bf16[8,288,128]{2,1,0:T(8,128)(2,1)S(1)}, f32[576,128]{1,0:T(8,128)S(1)}, bf16[576,128]{1,0:T(8,128)(2,1)S(1)}) custom-call(bf16[1152,128]{1,0:T(8,128)(2,1)S(1)} %get-tuple-element.127.q_ref, bf16[1152,128]{1,0:T(8,128)(2,1)S(1)} %get-tuple-element.128.qm_ref, bf16[1152,128]{1,0:T(8,128)(2,1)S(1)} %get-tuple-element.129.da_ref, ...), custom_call_target="tpu_custom_call" | custom-call | flops 2038431744 | bytes 1048576 | tf_op jit(solution)/shard_map/backward_three/pallas_call | solution.py:47
  78.7 0.1 core.1
  78.8 2.8 %collective-permute-done.22.refs_1_ = bf16[512,256]{1,0:T(8,128)(2,1)S(1)} collective-permute-done((bf16[512,256]{1,0:T(8,128)(2,1)S(1)}, bf16[512,256]{1,0:T(8,128)(2,1)S(1)}, u32[]{:S(2)}, u32[]{:S(2)}) %collective-permute-start.22) | collective-permute-done | bytes 262176 | tf_op jit(solution)/shard_map/ppermute | solution.py:379
  81.8 2.0 %collective-permute-start.26 = (bf16[576,128]{1,0:T(8,128)(2,1)S(1)}, bf16[576,128]{1,0:T(8,128)(2,1)S(1)}, u32[]{:S(2)}, u32[]{:S(2)}) collective-permute-start(bf16[576,128]{1,0:T(8,128)(2,1)S(1)} %get-tuple-element.152), channel_id=1, source_target_pairs={{0,8},{8,0},{16,24},{24,16},{1,9},{9,1},{17,25},{25,17},{2,10},{10... | collective-permute-start | bytes 442376 | tf_op jit(solution)/shard_map/ppermute | solution.py:379
  83.8 2.5 %collective-permute-start.24 = (bf16[576,128]{1,0:T(8,128)(2,1)S(1)}, bf16[576,128]{1,0:T(8,128)(2,1)S(1)}, u32[]{:S(2)}, u32[]{:S(2)}) collective-permute-start(bf16[576,128]{1,0:T(8,128)(2,1)S(1)} %get-tuple-element.150), channel_id=1, source_target_pairs={{0,64},{64,0},{128,192},{192,128},{1,65},{65,1},{129,193},{193,129... | collective-permute-start | bytes 442376 | tf_op jit(solution)/shard_map/ppermute | solution.py:379
  86.3 1.6 %collective-permute-done.27.got_ref = bf16[256,256]{1,0:T(8,128)(2,1)S(1)} collective-permute-done((bf16[256,256]{1,0:T(8,128)(2,1)S(1)}, bf16[256,256]{1,0:T(8,128)(2,1)S(1)}, u32[]{:S(2)}, u32[]{:S(2)}) %collective-permute-start.27) | collective-permute-done | bytes 131104 | tf_op jit(solution)/shard_map/ppermute | solution.py:379
  87.9 0.3 collective-permute-start.28
  88.3 1.8 %collective-permute-start.29 = (bf16[136,512]{1,0:T(8,128)(2,1)S(1)}, bf16[136,512]{1,0:T(8,128)(2,1)S(1)}, u32[]{:S(2)}, u32[]{:S(2)}) collective-permute-start(bf16[136,512]{1,0:T(8,128)(2,1)S(1)} %get-tuple-element.162), channel_id=1, source_target_pairs={{0,3},{1,0},{2,1},{3,2},{4,7},{5,4},{6,5},{7,6},{8,11},{9,8},{10,9... | collective-permute-start | bytes 417800 | tf_op jit(solution)/shard_map/ppermute | solution.py:375
  90.0 1.2 %collective-permute-start.30 = (bf16[136,512]{1,0:T(8,128)(2,1)S(1)}, bf16[136,512]{1,0:T(8,128)(2,1)S(1)}, u32[]{:S(2)}, u32[]{:S(2)}) collective-permute-start(bf16[136,512]{1,0:T(8,128)(2,1)S(1)} %get-tuple-element.164), channel_id=1, source_target_pairs={{0,2},{1,3},{2,0},{3,1},{4,6},{5,7},{6,4},{7,5},{8,10},{9,11},{10,... | collective-permute-start | bytes 417800 | tf_op jit(solution)/shard_map/ppermute | solution.py:375
  91.3 1.0 collective-permute-done.25.refs_3_
  92.3 1.3 %collective-permute-done.28 = bf16[136,512]{1,0:T(8,128)(2,1)S(1)} collective-permute-done((bf16[136,512]{1,0:T(8,128)(2,1)S(1)}, bf16[136,512]{1,0:T(8,128)(2,1)S(1)}, u32[]{:S(2)}, u32[]{:S(2)}) %collective-permute-start.28) | collective-permute-done | bytes 139296 | tf_op jit(solution)/shard_map/ppermute | solution.py:375
  93.6 1.2 %collective-permute-done.29 = bf16[136,512]{1,0:T(8,128)(2,1)S(1)} collective-permute-done((bf16[136,512]{1,0:T(8,128)(2,1)S(1)}, bf16[136,512]{1,0:T(8,128)(2,1)S(1)}, u32[]{:S(2)}, u32[]{:S(2)}) %collective-permute-start.29) | collective-permute-done | bytes 139296 | tf_op jit(solution)/shard_map/ppermute | solution.py:375
  94.8 1.4 %collective-permute-start.34 = (bf16[128,256]{1,0:T(8,128)(2,1)S(1)}, bf16[128,256]{1,0:T(8,128)(2,1)S(1)}, u32[]{:S(2)}, u32[]{:S(2)}) collective-permute-start(bf16[128,256]{1,0:T(8,128)(2,1)S(1)} %get-tuple-element.179), channel_id=1, source_target_pairs={{0,192},{64,128},{128,64},{192,0},{1,193},{65,129},{129,65},{193,1... | collective-permute-start | bytes 196616 | tf_op jit(solution)/shard_map/ppermute | solution.py:379
  96.2 2.4 %collective-permute-start.31 = (bf16[288,128]{1,0:T(8,128)(2,1)S(1)}, bf16[288,128]{1,0:T(8,128)(2,1)S(1)}, u32[]{:S(2)}, u32[]{:S(2)}) collective-permute-start(bf16[288,128]{1,0:T(8,128)(2,1)S(1)} %get-tuple-element.173), channel_id=1, source_target_pairs={{0,24},{8,16},{16,8},{24,0},{1,25},{9,17},{17,9},{25,1},{2,26},{10... | collective-permute-start | bytes 221192 | tf_op jit(solution)/shard_map/ppermute | solution.py:379
  98.6 2.8 %collective-permute-start.32 = (bf16[288,128]{1,0:T(8,128)(2,1)S(1)}, bf16[288,128]{1,0:T(8,128)(2,1)S(1)}, u32[]{:S(2)}, u32[]{:S(2)}) collective-permute-start(bf16[288,128]{1,0:T(8,128)(2,1)S(1)} %get-tuple-element.175), channel_id=1, source_target_pairs={{0,192},{64,128},{128,64},{192,0},{1,193},{65,129},{129,65},{193,1... | collective-permute-start | bytes 221192 | tf_op jit(solution)/shard_map/ppermute | solution.py:379
  101.4 1.5 %collective-permute-start.33 = (bf16[288,128]{1,0:T(8,128)(2,1)S(1)}, bf16[288,128]{1,0:T(8,128)(2,1)S(1)}, u32[]{:S(2)}, u32[]{:S(2)}) collective-permute-start(bf16[288,128]{1,0:T(8,128)(2,1)S(1)} %get-tuple-element.177), channel_id=1, source_target_pairs={{0,64},{64,0},{128,192},{192,128},{1,65},{65,1},{129,193},{193,129... | collective-permute-start | bytes 221192 | tf_op jit(solution)/shard_map/ppermute | solution.py:379
  103.0 1.9 %collective-permute-start.35 = (bf16[64,256]{1,0:T(8,128)(2,1)S(1)}, bf16[64,256]{1,0:T(8,128)(2,1)S(1)}, u32[]{:S(2)}, u32[]{:S(2)}) collective-permute-start(bf16[64,256]{1,0:T(8,128)(2,1)S(1)} %get-tuple-element.181), channel_id=1, source_target_pairs={{0,64},{64,0},{128,192},{192,128},{1,65},{65,1},{129,193},{193,129... | collective-permute-start | bytes 98312 | tf_op jit(solution)/shard_map/ppermute | solution.py:379
  104.8 0.5 collective-permute-done.32.refs_3_
  105.3 2.2 %collective-permute-done.33.refs_5_ = bf16[288,128]{1,0:T(8,128)(2,1)S(1)} collective-permute-done((bf16[288,128]{1,0:T(8,128)(2,1)S(1)}, bf16[288,128]{1,0:T(8,128)(2,1)S(1)}, u32[]{:S(2)}, u32[]{:S(2)}) %collective-permute-start.33) | collective-permute-done | bytes 73760 | tf_op jit(solution)/shard_map/ppermute | solution.py:379
  107.5 0.4 collective-permute-done.35.refs_7_
  108.0 1.6 %collective-permute-start.36 = (bf16[496,128]{1,0:T(8,128)(2,1)S(1)}, bf16[496,128]{1,0:T(8,128)(2,1)S(1)}, u32[]{:S(2)}, u32[]{:S(2)}) collective-permute-start(bf16[496,128]{1,0:T(8,128)(2,1)S(1)} %get-tuple-element.184), channel_id=1, source_target_pairs={{0,32},{32,0},{1,33},{33,1},{2,34},{34,2},{3,35},{35,3},{4,36},{36... | collective-permute-start | bytes 380936 | tf_op jit(solution)/shard_map/ppermute | solution.py:379
  109.5 0.7 add_convert_fusion
  110.3 2.7 %collective-permute-done.36.got_ref = bf16[496,128]{1,0:T(8,128)(2,1)S(1)} collective-permute-done((bf16[496,128]{1,0:T(8,128)(2,1)S(1)}, bf16[496,128]{1,0:T(8,128)(2,1)S(1)}, u32[]{:S(2)}, u32[]{:S(2)}) %collective-permute-start.36) | collective-permute-done | bytes 127008 | tf_op jit(solution)/shard_map/ppermute | solution.py:379
  113.0 1.3 %place.1 = (bf16[136,256]{1,0:T(8,128)(2,1)}, bf16[136,256]{1,0:T(8,128)(2,1)}, bf16[136,256]{1,0:T(8,128)(2,1)}, f32[32,256]{1,0:T(8,128)}) custom-call(s32[5]{0:T(128)S(1)} %stack.23.at_ref, bf16[144,384]{1,0:T(8,128)(2,1)S(1)} %get-tuple-element.182.mine_ref, f32[32,256]{1,0:T(8,128)S(1)} %get-tuple-element.183.wmine_ref, ...), custom_call_target="tpu_custom_call" | custom-call | tf_op jit(solution)/shard_map/place/pallas_call | solution.py:47
  (47 shorter events, 1.3 us)
Async XLA Ops:
  0.6 9.5 %copy-start = (bf16[256,2048]{1,0:T(8,128)(2,1)S(1)}, bf16[256,2048]{1,0:T(8,128)(2,1)}, u32[]{:S(2)}) copy-start(bf16[256,2048]{1,0:T(8,128)(2,1)} %param.10) | copy-start | bytes 3145732
  3.2 7.1 %collective-permute-start = (bf16[432,128]{1,0:T(8,128)(2,1)S(1)}, bf16[432,128]{1,0:T(8,128)(2,1)S(1)}, u32[]{:S(2)}, u32[]{:S(2)}) collective-permute-start(bf16[432,128]{1,0:T(8,128)(2,1)S(1)} %get-tuple-element.98), channel_id=1, source_target_pairs={{0,32},{32,0},{1,33},{33,1},{2,34},{34,2},{3,35},{35,3},{4,36},{36... | collective-permute-start | bytes 331784 | tf_op jit(solution)/shard_map/ppermute | solution.py:379
  5.2 19.8 %collective-permute-start.7 = (bf16[136,512]{1,0:T(8,128)(2,1)S(1)}, bf16[136,512]{1,0:T(8,128)(2,1)S(1)}, u32[]{:S(2)}, u32[]{:S(2)}) collective-permute-start(bf16[136,512]{1,0:T(8,128)(2,1)S(1)} %get-tuple-element.103.refs_0_.dy0_ref), channel_id=1, source_target_pairs={{0,3},{1,0},{2,1},{3,2},{4,7},{5,4},{6,5},{7,6},{8,11},{9,8},{10,9... | collective-permute-start | bytes 417800 | tf_op jit(solution)/shard_map/ppermute | solution.py:375
  5.6 19.4 %collective-permute-start.6 = (bf16[136,512]{1,0:T(8,128)(2,1)S(1)}, bf16[136,512]{1,0:T(8,128)(2,1)S(1)}, u32[]{:S(2)}, u32[]{:S(2)}) collective-permute-start(bf16[136,512]{1,0:T(8,128)(2,1)S(1)} %get-tuple-element.103.refs_0_.dy0_ref), channel_id=1, source_target_pairs={{0,2},{1,3},{2,0},{3,1},{4,6},{5,7},{6,4},{7,5},{8,10},{9,11},{10,... | collective-permute-start | bytes 417800 | tf_op jit(solution)/shard_map/ppermute | solution.py:375
  8.2 16.8 %collective-permute-start.5 = (bf16[136,512]{1,0:T(8,128)(2,1)S(1)}, bf16[136,512]{1,0:T(8,128)(2,1)S(1)}, u32[]{:S(2)}, u32[]{:S(2)}) collective-permute-start(bf16[136,512]{1,0:T(8,128)(2,1)S(1)} %get-tuple-element.103.refs_0_.dy0_ref), channel_id=1, source_target_pairs={{0,1},{1,2},{2,3},{3,0},{4,5},{5,6},{6,7},{7,4},{8,9},{9,10},{10,1... | collective-permute-start | bytes 417800 | tf_op jit(solution)/shard_map/ppermute | solution.py:375
  10.3 7.0 %collective-permute-start.1 = (bf16[288,128]{1,0:T(8,128)(2,1)S(1)}, bf16[288,128]{1,0:T(8,128)(2,1)S(1)}, u32[]{:S(2)}, u32[]{:S(2)}) collective-permute-start(bf16[288,128]{1,0:T(8,128)(2,1)S(1)} %pad_maximum_fusion.4), channel_id=1, source_target_pairs={{0,64},{64,0},{128,192},{192,128},{1,65},{65,1},{129,193},{193,129... | collective-permute-start | bytes 221192 | tf_op jit(solution)/shard_map/ppermute | solution.py:379
  13.7 6.9 %collective-permute-start.2 = (bf16[288,128]{1,0:T(8,128)(2,1)S(1)}, bf16[288,128]{1,0:T(8,128)(2,1)S(1)}, u32[]{:S(2)}, u32[]{:S(2)}) collective-permute-start(bf16[288,128]{1,0:T(8,128)(2,1)S(1)} %pad_maximum_fusion.5), channel_id=1, source_target_pairs={{0,192},{64,128},{128,64},{192,0},{1,193},{65,129},{129,65},{193,1... | collective-permute-start | bytes 221192 | tf_op jit(solution)/shard_map/ppermute | solution.py:379
  17.3 5.7 %collective-permute-start.4 = (bf16[288,128]{1,0:T(8,128)(2,1)S(1)}, bf16[288,128]{1,0:T(8,128)(2,1)S(1)}, u32[]{:S(2)}, u32[]{:S(2)}) collective-permute-start(bf16[288,128]{1,0:T(8,128)(2,1)S(1)} %pad_maximum_fusion.6.refs_0_), channel_id=1, source_target_pairs={{0,24},{8,16},{16,8},{24,0},{1,25},{9,17},{17,9},{25,1},{2,26},{10... | collective-permute-start | bytes 221192 | tf_op jit(solution)/shard_map/ppermute | solution.py:379
  20.6 4.4 %collective-permute-start.3 = (bf16[288,128]{1,0:T(8,128)(2,1)S(1)}, bf16[288,128]{1,0:T(8,128)(2,1)S(1)}, u32[]{:S(2)}, u32[]{:S(2)}) collective-permute-start(bf16[288,128]{1,0:T(8,128)(2,1)S(1)} %pad_maximum_fusion.6.refs_0_), channel_id=1, source_target_pairs={{0,8},{8,0},{16,24},{24,16},{1,9},{9,1},{17,25},{25,17},{2,10},{10... | collective-permute-start | bytes 221192 | tf_op jit(solution)/shard_map/ppermute | solution.py:379
  25.0 17.2 %collective-permute-start.9 = (bf16[576,128]{1,0:T(8,128)(2,1)S(1)}, bf16[576,128]{1,0:T(8,128)(2,1)S(1)}, u32[]{:S(2)}, u32[]{:S(2)}) collective-permute-start(bf16[576,128]{1,0:T(8,128)(2,1)S(1)} %get-tuple-element.110), channel_id=1, source_target_pairs={{0,192},{64,128},{128,64},{192,0},{1,193},{65,129},{129,65},{193,1... | collective-permute-start | bytes 442376 | tf_op jit(solution)/shard_map/ppermute | solution.py:379
  29.0 13.2 %collective-permute-start.10 = (bf16[576,128]{1,0:T(8,128)(2,1)S(1)}, bf16[576,128]{1,0:T(8,128)(2,1)S(1)}, u32[]{:S(2)}, u32[]{:S(2)}) collective-permute-start(bf16[576,128]{1,0:T(8,128)(2,1)S(1)} %get-tuple-element.111), channel_id=1, source_target_pairs={{0,64},{64,0},{128,192},{192,128},{1,65},{65,1},{129,193},{193,129... | collective-permute-start | bytes 442376 | tf_op jit(solution)/shard_map/ppermute | solution.py:379
  31.6 4.2 %collective-permute-start.8 = (bf16[144,128]{1,0:T(8,128)(2,1)S(1)}, bf16[144,128]{1,0:T(8,128)(2,1)S(1)}, u32[]{:S(2)}, u32[]{:S(2)}) collective-permute-start(bf16[144,128]{1,0:T(8,128)(2,1)S(1)} %get-tuple-element.109), channel_id=1, source_target_pairs={{0,32},{32,0},{1,33},{33,1},{2,34},{34,2},{3,35},{35,3},{4,36},{36... | collective-permute-start | bytes 110600 | tf_op jit(solution)/shard_map/ppermute | solution.py:379
  35.8 5.6 %collective-permute-start.12 = (bf16[288,128]{1,0:T(8,128)(2,1)S(1)}, bf16[288,128]{1,0:T(8,128)(2,1)S(1)}, u32[]{:S(2)}, u32[]{:S(2)}) collective-permute-start(bf16[288,128]{1,0:T(8,128)(2,1)S(1)} %constant_dynamic-update-slice_fusion.refs_0_), channel_id=1, source_target_pairs={{0,24},{8,16},{16,8},{24,0},{1,25},{9,17},{17,9},{25,1},{2,26},{10... | collective-permute-start | bytes 221192 | tf_op jit(solution)/shard_map/ppermute | solution.py:379
  37.8 4.4 %collective-permute-start.11 = (bf16[288,128]{1,0:T(8,128)(2,1)S(1)}, bf16[288,128]{1,0:T(8,128)(2,1)S(1)}, u32[]{:S(2)}, u32[]{:S(2)}) collective-permute-start(bf16[288,128]{1,0:T(8,128)(2,1)S(1)} %constant_dynamic-update-slice_fusion.refs_0_), channel_id=1, source_target_pairs={{0,8},{8,0},{16,24},{24,16},{1,9},{9,1},{17,25},{25,17},{2,10},{10... | collective-permute-start | bytes 221192 | tf_op jit(solution)/shard_map/ppermute | solution.py:379
  38.1 10.9 %collective-permute-start.15 = (bf16[1152,128]{1,0:T(8,128)(2,1)S(1)}, bf16[1152,128]{1,0:T(8,128)(2,1)S(1)}, u32[]{:S(2)}, u32[]{:S(2)}) collective-permute-start(bf16[1152,128]{1,0:T(8,128)(2,1)S(1)} %constant_dynamic-update-slice_fusion.2.refs_4_), channel_id=1, source_target_pairs={{0,4},{4,0},{1,5},{5,1},{2,6},{6,2},{3,7},{7,3},{8,12},{12,8},{9,1... | collective-permute-start | bytes 884744 | tf_op jit(solution)/shard_map/ppermute | solution.py:379
  42.2 6.8 %collective-permute-start.16 = (bf16[1152,128]{1,0:T(8,128)(2,1)S(1)}, bf16[1152,128]{1,0:T(8,128)(2,1)S(1)}, u32[]{:S(2)}, u32[]{:S(2)}) collective-permute-start(bf16[1152,128]{1,0:T(8,128)(2,1)S(1)} %constant_dynamic-update-slice_fusion.4.refs_5_), channel_id=1, source_target_pairs={{0,4},{4,0},{1,5},{5,1},{2,6},{6,2},{3,7},{7,3},{8,12},{12,8},{9,1... | collective-permute-start | bytes 884744 | tf_op jit(solution)/shard_map/ppermute | solution.py:379
  42.3 6.7 %collective-permute-start.14 = (bf16[288,128]{1,0:T(8,128)(2,1)S(1)}, bf16[288,128]{1,0:T(8,128)(2,1)S(1)}, u32[]{:S(2)}, u32[]{:S(2)}) collective-permute-start(bf16[288,128]{1,0:T(8,128)(2,1)S(1)} %pad_maximum_fusion.6.refs_0_), channel_id=1, source_target_pairs={{0,16},{8,24},{16,0},{24,8},{1,17},{9,25},{17,1},{25,9},{2,18},{10... | collective-permute-start | bytes 221192 | tf_op jit(solution)/shard_map/ppermute | solution.py:379
  43.2 10.8 %collective-permute-start.13 = (bf16[288,128]{1,0:T(8,128)(2,1)S(1)}, bf16[288,128]{1,0:T(8,128)(2,1)S(1)}, u32[]{:S(2)}, u32[]{:S(2)}) collective-permute-start(bf16[288,128]{1,0:T(8,128)(2,1)S(1)} %constant_dynamic-update-slice_fusion.refs_0_), channel_id=1, source_target_pairs={{0,16},{8,24},{16,0},{24,8},{1,17},{9,25},{17,1},{25,9},{2,18},{10... | collective-permute-start | bytes 221192 | tf_op jit(solution)/shard_map/ppermute | solution.py:379
  54.5 4.9 %collective-permute-start.17 = (bf16[368,128]{1,0:T(8,128)(2,1)S(1)}, bf16[368,128]{1,0:T(8,128)(2,1)S(1)}, u32[]{:S(2)}, u32[]{:S(2)}) collective-permute-start(bf16[368,128]{1,0:T(8,128)(2,1)S(1)} %get-tuple-element.121), channel_id=1, source_target_pairs={{0,8},{8,0},{16,24},{24,16},{1,9},{9,1},{17,25},{25,17},{2,10},{10... | collective-permute-start | bytes 282632 | tf_op jit(solution)/shard_map/ppermute | solution.py:379
  54.6 6.6 %collective-permute-start.18 = (bf16[368,128]{1,0:T(8,128)(2,1)S(1)}, bf16[368,128]{1,0:T(8,128)(2,1)S(1)}, u32[]{:S(2)}, u32[]{:S(2)}) collective-permute-start(bf16[368,128]{1,0:T(8,128)(2,1)S(1)} %get-tuple-element.122), channel_id=1, source_target_pairs={{0,16},{8,24},{16,0},{24,8},{1,17},{9,25},{17,1},{25,9},{2,18},{10... | collective-permute-start | bytes 282632 | tf_op jit(solution)/shard_map/ppermute | solution.py:379
  57.2 5.8 %collective-permute-start.19 = (bf16[368,128]{1,0:T(8,128)(2,1)S(1)}, bf16[368,128]{1,0:T(8,128)(2,1)S(1)}, u32[]{:S(2)}, u32[]{:S(2)}) collective-permute-start(bf16[368,128]{1,0:T(8,128)(2,1)S(1)} %get-tuple-element.123), channel_id=1, source_target_pairs={{0,24},{8,16},{16,8},{24,0},{1,25},{9,17},{17,9},{25,1},{2,26},{10... | collective-permute-start | bytes 282632 | tf_op jit(solution)/shard_map/ppermute | solution.py:379
  63.8 4.4 %collective-permute-start.20 = (bf16[144,128]{1,0:T(8,128)(2,1)S(1)}, bf16[144,128]{1,0:T(8,128)(2,1)S(1)}, u32[]{:S(2)}, u32[]{:S(2)}) collective-permute-start(bf16[144,128]{1,0:T(8,128)(2,1)S(1)} %get-tuple-element.125), channel_id=1, source_target_pairs={{0,32},{32,0},{1,33},{33,1},{2,34},{34,2},{3,35},{35,3},{4,36},{36... | collective-permute-start | bytes 110600 | tf_op jit(solution)/shard_map/ppermute | solution.py:379
  69.5 2.5 %collective-permute-start.21 = (bf16[4,256,256]{2,1,0:T(8,128)(2,1)S(1)}, bf16[4,256,256]{2,1,0:T(8,128)(2,1)S(1)}, u32[]{:S(2)}, u32[]{:S(2)}) collective-permute-start(bf16[4,256,256]{2,1,0:T(8,128)(2,1)S(1)} %get-tuple-element.138), channel_id=1, source_target_pairs={{0,4},{4,0},{1,5},{5,1},{2,6},{6,2},{3,7},{7,3},{8,12},{12,8},{9,1... | collective-permute-start | bytes 1572872 | tf_op jit(solution)/shard_map/ppermute | solution.py:379
  71.4 7.3 %collective-permute-start.23 = (bf16[8,288,128]{2,1,0:T(8,128)(2,1)S(1)}, bf16[8,288,128]{2,1,0:T(8,128)(2,1)S(1)}, u32[]{:S(2)}, u32[]{:S(2)}) collective-permute-start(bf16[8,288,128]{2,1,0:T(8,128)(2,1)S(1)} %get-tuple-element.148), channel_id=1, source_target_pairs={{0,4},{4,0},{1,5},{5,1},{2,6},{6,2},{3,7},{7,3},{8,12},{12,8},{9,1... | collective-permute-start | bytes 1769480 | tf_op jit(solution)/shard_map/ppermute | solution.py:379
  72.1 9.5 %collective-permute-start.22 = (bf16[512,256]{1,0:T(8,128)(2,1)S(1)}, bf16[512,256]{1,0:T(8,128)(2,1)S(1)}, u32[]{:S(2)}, u32[]{:S(2)}) collective-permute-start(bf16[512,256]{1,0:T(8,128)(2,1)S(1)} %get-tuple-element.145), channel_id=1, source_target_pairs={{0,24},{8,16},{16,8},{24,0},{1,25},{9,17},{17,9},{25,1},{2,26},{10... | collective-permute-start | bytes 786440 | tf_op jit(solution)/shard_map/ppermute | solution.py:379
  81.7 6.2 %collective-permute-start.27 = (bf16[256,256]{1,0:T(8,128)(2,1)S(1)}, bf16[256,256]{1,0:T(8,128)(2,1)S(1)}, u32[]{:S(2)}, u32[]{:S(2)}) collective-permute-start(bf16[256,256]{1,0:T(8,128)(2,1)S(1)} %get-tuple-element.156), channel_id=1, source_target_pairs={{0,8},{8,0},{16,24},{24,16},{1,9},{9,1},{17,25},{25,17},{2,10},{10... | collective-permute-start | bytes 393224 | tf_op jit(solution)/shard_map/ppermute | solution.py:379
  81.8 8.3 %collective-permute-start.26 = (bf16[576,128]{1,0:T(8,128)(2,1)S(1)}, bf16[576,128]{1,0:T(8,128)(2,1)S(1)}, u32[]{:S(2)}, u32[]{:S(2)}) collective-permute-start(bf16[576,128]{1,0:T(8,128)(2,1)S(1)} %get-tuple-element.152), channel_id=1, source_target_pairs={{0,8},{8,0},{16,24},{24,16},{1,9},{9,1},{17,25},{25,17},{2,10},{10... | collective-permute-start | bytes 442376 | tf_op jit(solution)/shard_map/ppermute | solution.py:379
  83.8 8.6 %collective-permute-start.25 = (bf16[576,128]{1,0:T(8,128)(2,1)S(1)}, bf16[576,128]{1,0:T(8,128)(2,1)S(1)}, u32[]{:S(2)}, u32[]{:S(2)}) collective-permute-start(bf16[576,128]{1,0:T(8,128)(2,1)S(1)} %get-tuple-element.151), channel_id=1, source_target_pairs={{0,192},{64,128},{128,64},{192,0},{1,193},{65,129},{129,65},{193,1... | collective-permute-start | bytes 442376 | tf_op jit(solution)/shard_map/ppermute | solution.py:379
  83.8 8.6 %collective-permute-start.24 = (bf16[576,128]{1,0:T(8,128)(2,1)S(1)}, bf16[576,128]{1,0:T(8,128)(2,1)S(1)}, u32[]{:S(2)}, u32[]{:S(2)}) collective-permute-start(bf16[576,128]{1,0:T(8,128)(2,1)S(1)} %get-tuple-element.150), channel_id=1, source_target_pairs={{0,64},{64,0},{128,192},{192,128},{1,65},{65,1},{129,193},{193,129... | collective-permute-start | bytes 442376 | tf_op jit(solution)/shard_map/ppermute | solution.py:379
  87.9 5.7 %collective-permute-start.28 = (bf16[136,512]{1,0:T(8,128)(2,1)S(1)}, bf16[136,512]{1,0:T(8,128)(2,1)S(1)}, u32[]{:S(2)}, u32[]{:S(2)}) collective-permute-start(bf16[136,512]{1,0:T(8,128)(2,1)S(1)} %get-tuple-element.161), channel_id=1, source_target_pairs={{0,1},{1,2},{2,3},{3,0},{4,5},{5,6},{6,7},{7,4},{8,9},{9,10},{10,1... | collective-permute-start | bytes 417800 | tf_op jit(solution)/shard_map/ppermute | solution.py:375
  88.3 6.5 %collective-permute-start.29 = (bf16[136,512]{1,0:T(8,128)(2,1)S(1)}, bf16[136,512]{1,0:T(8,128)(2,1)S(1)}, u32[]{:S(2)}, u32[]{:S(2)}) collective-permute-start(bf16[136,512]{1,0:T(8,128)(2,1)S(1)} %get-tuple-element.162), channel_id=1, source_target_pairs={{0,3},{1,0},{2,1},{3,2},{4,7},{5,4},{6,5},{7,6},{8,11},{9,8},{10,9... | collective-permute-start | bytes 417800 | tf_op jit(solution)/shard_map/ppermute | solution.py:375
  90.0 19.5 %collective-permute-start.30 = (bf16[136,512]{1,0:T(8,128)(2,1)S(1)}, bf16[136,512]{1,0:T(8,128)(2,1)S(1)}, u32[]{:S(2)}, u32[]{:S(2)}) collective-permute-start(bf16[136,512]{1,0:T(8,128)(2,1)S(1)} %get-tuple-element.164), channel_id=1, source_target_pairs={{0,2},{1,3},{2,0},{3,1},{4,6},{5,7},{6,4},{7,5},{8,10},{9,11},{10,... | collective-permute-start | bytes 417800 | tf_op jit(solution)/shard_map/ppermute | solution.py:375
  94.8 8.1 %collective-permute-start.34 = (bf16[128,256]{1,0:T(8,128)(2,1)S(1)}, bf16[128,256]{1,0:T(8,128)(2,1)S(1)}, u32[]{:S(2)}, u32[]{:S(2)}) collective-permute-start(bf16[128,256]{1,0:T(8,128)(2,1)S(1)} %get-tuple-element.179), channel_id=1, source_target_pairs={{0,192},{64,128},{128,64},{192,0},{1,193},{65,129},{129,65},{193,1... | collective-permute-start | bytes 196616 | tf_op jit(solution)/shard_map/ppermute | solution.py:379
  96.2 8.6 %collective-permute-start.31 = (bf16[288,128]{1,0:T(8,128)(2,1)S(1)}, bf16[288,128]{1,0:T(8,128)(2,1)S(1)}, u32[]{:S(2)}, u32[]{:S(2)}) collective-permute-start(bf16[288,128]{1,0:T(8,128)(2,1)S(1)} %get-tuple-element.173), channel_id=1, source_target_pairs={{0,24},{8,16},{16,8},{24,0},{1,25},{9,17},{17,9},{25,1},{2,26},{10... | collective-permute-start | bytes 221192 | tf_op jit(solution)/shard_map/ppermute | solution.py:379
  98.6 6.7 %collective-permute-start.32 = (bf16[288,128]{1,0:T(8,128)(2,1)S(1)}, bf16[288,128]{1,0:T(8,128)(2,1)S(1)}, u32[]{:S(2)}, u32[]{:S(2)}) collective-permute-start(bf16[288,128]{1,0:T(8,128)(2,1)S(1)} %get-tuple-element.175), channel_id=1, source_target_pairs={{0,192},{64,128},{128,64},{192,0},{1,193},{65,129},{129,65},{193,1... | collective-permute-start | bytes 221192 | tf_op jit(solution)/shard_map/ppermute | solution.py:379
  101.4 6.1 %collective-permute-start.33 = (bf16[288,128]{1,0:T(8,128)(2,1)S(1)}, bf16[288,128]{1,0:T(8,128)(2,1)S(1)}, u32[]{:S(2)}, u32[]{:S(2)}) collective-permute-start(bf16[288,128]{1,0:T(8,128)(2,1)S(1)} %get-tuple-element.177), channel_id=1, source_target_pairs={{0,64},{64,0},{128,192},{192,128},{1,65},{65,1},{129,193},{193,129... | collective-permute-start | bytes 221192 | tf_op jit(solution)/shard_map/ppermute | solution.py:379
  103.0 5.0 %collective-permute-start.35 = (bf16[64,256]{1,0:T(8,128)(2,1)S(1)}, bf16[64,256]{1,0:T(8,128)(2,1)S(1)}, u32[]{:S(2)}, u32[]{:S(2)}) collective-permute-start(bf16[64,256]{1,0:T(8,128)(2,1)S(1)} %get-tuple-element.181), channel_id=1, source_target_pairs={{0,64},{64,0},{128,192},{192,128},{1,65},{65,1},{129,193},{193,129... | collective-permute-start | bytes 98312 | tf_op jit(solution)/shard_map/ppermute | solution.py:379
  108.0 5.0 %collective-permute-start.36 = (bf16[496,128]{1,0:T(8,128)(2,1)S(1)}, bf16[496,128]{1,0:T(8,128)(2,1)S(1)}, u32[]{:S(2)}, u32[]{:S(2)}) collective-permute-start(bf16[496,128]{1,0:T(8,128)(2,1)S(1)} %get-tuple-element.184), channel_id=1, source_target_pairs={{0,32},{32,0},{1,33},{33,1},{2,34},{34,2},{3,35},{35,3},{4,36},{36... | collective-permute-start | bytes 380936 | tf_op jit(solution)/shard_map/ppermute | solution.py:379
where the time goes:
time: 114 us
  starting transfers between devices  60 us (53%)
  waiting for transfers between devices  30.9 us (27%)
  Pallas kernels  19.5 us (17%)
  other arithmetic  2.7 us (2%)
    ppermute x31, starting transfers between devices, swapped(): return lax.ppermute(value, axis, [(i, i ^ mask) for i in range(size)])  51.7 us
    ppermute x31, waiting for transfers between devices, swapped(): return lax.ppermute(value, axis, [(i, i ^ mask) for i in range(size)])  28.4 us
    pallas_call x17, Pallas kernels, call(): pl.pallas_call(kernel, in_specs=[SMEM] * scalars + [VMEM] * (len(ins) - s...  19.5 us
    ppermute x6, starting transfers between devices, shifted(): lax.ppermute(value, axis, [(i, (i + by) % size) for i in range(size)])  8.27 us
    ppermute x6, waiting for transfers between devices, shifted(): lax.ppermute(value, axis, [(i, (i + by) % size) for i in range(size)])  2.49 us
  transfers between devices with their start and end apart: 37, of which 19 were waited for; matrix products, arithmetic and copies ran while one was open for 1% of the time, Pallas kernels for 13%

commit v1 on v0

--- a/solution.py
+++ b/solution.py
@@ -211,13 +211,13 @@
 
 
 def backward_kernel(base, first, last, q_ref, qm_ref, da_ref, kv_ref, km_ref, *refs):
-    load_refs, refs = refs[0:4], refs[4:]
+    rows_ref, refs = refs[0], refs[1:]
     if first > 0 or base == 0:
         dq_in_ref, refs = refs[0], refs[1:]
     if first > 0:
         rows_in_ref, refs = refs[0], refs[1:]
     out_refs, dkv_ref, ds_ref = refs[:-2], refs[-2], refs[-1]
-    lse, delta = row_sums(load_refs)
+    lse, delta = rows_ref[0:1], rows_ref[1:2]
     q = q_ref[...]
     da = da_ref[...]
     q_ext = jnp.concatenate([q, qm_ref[...]], axis=1)
@@ -255,8 +255,11 @@
             out_refs[2][at * PAIR : (at + 1) * PAIR] = take_pair(dq, theirs).astype(BF16)
 
 
-def merge_kernel(l0_ref, l1_ref, l2_ref, l3_ref, keep_ref, send_ref):
+def merge_kernel(l0_ref, l1_ref, l2_ref, l3_ref, keep_ref, send_ref, rows_ref):
     load_refs = (l0_ref, l1_ref, l2_ref, l3_ref)
+    lse, delta = row_sums(load_refs)
+    rows_ref[0:1] = lse
+    rows_ref[1:2] = delta
     fine, last = [], []
     for s, ref in enumerate(load_refs):
         sums = ref[PAIR:LOAD].astype(F32)
@@ -291,14 +294,14 @@
         out_refs[s][...] = part[0:ROWS].astype(BF16)
     for s, ref in enumerate((dy0_ref, dy1_ref, dy2_ref, dy3_ref)):
         dwo_ref[s] = lax.dot_general(ref[...], attn[0:ROWS], FIRST, preferred_element_type=F32).astype(BF16)
-    for xt in range(4):
-        for et in range(2):
-            for t in range(4):
-                s = lax.rem(h - jnp.bitwise_xor(zr, t) + NH, NH)
-                row = lax.rem(e + et, 2) * 256 + jnp.bitwise_xor(x, xt) * 64
-                to = slice((et * 4 + t) * COLS, (et * 4 + t + 1) * COLS)
-                keep_ref[xt, to] = dwo_ref[s, pl.ds(pl.multiple_of(row + c * COLS, COLS), COLS)]
-                send_ref[xt, to] = dwo_ref[s, pl.ds(pl.multiple_of(row + (1 - c) * COLS, COLS), COLS)]
+    for ref, core in ((keep_ref, c), (send_ref, 1 - c)):
+        for i, xt in enumerate((0, 1 + 2 * core, 3 - 2 * core, 2)):
+            for et in range(2):
+                for t in range(4):
+                    s = lax.rem(h - jnp.bitwise_xor(zr, t) + NH, NH)
+                    row = lax.rem(e + et, 2) * 256 + jnp.bitwise_xor(x, xt) * 64 + core * COLS
+                    to = slice((et * 4 + t) * COLS, (et * 4 + t + 1) * COLS)
+                    ref[i, to] = dwo_ref[s, pl.ds(pl.multiple_of(row, COLS), COLS)]
 
 
 def split_up(total, mine, theirs, keep_ref, send_ref):
@@ -316,7 +319,7 @@
 
 def dwo_kernel(keep_ref, got_ref, mine_ref, send_ref):
     total = keep_ref[...].astype(F32) + got_ref[...].astype(F32)
-    split_up(total, (0, 1), (3, 2), mine_ref, send_ref)
+    split_up(total, (0, 1), (2, 3), mine_ref, send_ref)
 
 
 def middle_kernel(*refs):
@@ -379,6 +382,11 @@
     return lax.ppermute(value, axis, [(i, i ^ mask) for i in range(size)])
 
 
+def by_core(value, axis, flip):
+    masks = (3, 1) if flip else (1, 3)
+    return lax.ppermute(value, (axis, "c"), [(i, (i // 2 ^ masks[i % 2]) * 2 + i % 2) for i in range(8)])
+
+
 def around(value, axis):
     return [value] + [shifted(value, axis, 4, s) for s in (1, 2, 3)]
 
@@ -399,22 +407,26 @@
     got = swapped(send, "e", 2, 1)
     dy, send = lax.optimization_barrier((dy, send))
     k, v, q = (jnp.concatenate([keep[i : i + PAD], got[i : i + PAD]], axis=0) for i in (0, PAD, 2 * PAD))
-    first = [swapped(k, "zr", 4, 1), swapped(v, "zr", 4, 3), swapped(q, "x", 4, 1), swapped(q, "x", 4, 3)]
-    k_got, v_got, q_one, q_three = lax.optimization_barrier(first)
-    k, v = jnp.concatenate([k, k_got], axis=0), jnp.concatenate([v, v_got], axis=0)
+    k = jnp.concatenate([k, swapped(k, "zr", 4, 1)], axis=0)
+    v = jnp.concatenate([v, swapped(v, "zr", 4, 3)], axis=0)
     dys = around(dy, "head")
+    q_one, q_three = swapped(q, "x", 4, 1), swapped(q, "x", 4, 3)
     k, v, dys = lax.optimization_barrier((k, v, dys))
     ks, vs = [k, swapped(k, "zr", 4, 3)], [v, swapped(v, "zr", 4, 1)]
-    qs = [q, q_one, swapped(q, "x", 4, 2), q_three]
+    dys, q_one, q_three = lax.optimization_barrier((dys, q_one, q_three))
     wo, _ = lax.optimization_barrier((wo, dy))
     at_head = lax.axis_index("head")
     wo = jnp.concatenate(
         [lax.dynamic_slice_in_dim(wo, lax.rem(at_head - s + NH, NH) * WIDE, WIDE, 1) for s in range(NH)], axis=1
     )
     keep, send = call(dattn_kernel, "dattn", [at, *dys, wo, ids], [shape((PAD, DH))] * 2, scalars=1)
+    q_late, send = lax.optimization_barrier((q, send))
+    q_two = swapped(q_late, "x", 4, 2)
     da = jnp.concatenate([keep, swapped(send, "e", 2, 1)], axis=0)
     das = [da] + [swapped(da, "x", 4, s) for s in (1, 2, 3)]
-    ks[1], vs[1], das[1], das[3] = lax.optimization_barrier((ks[1], vs[1], das[1], das[3]))
+    late = [ks[1], vs[1], das[1], das[3], q_two]
+    ks[1], vs[1], das[1], das[3], q_two = lax.optimization_barrier(late)
+    qs = [q, q_one, q_two, q_three]
     kvs = [jnp.concatenate([ks[i], vs[i]], axis=0) for i in range(2)]
     kvs = kvs + [swapped(one, "c", 2, 1) for one in kvs]
 
@@ -431,11 +443,11 @@
     )
     loads = [loads[0]] + [swapped(loads[s], "x", 4, s) for s in (1, 2, 3)]
 
-    keep, send = call(merge_kernel, "merge", loads, [shape((PAD, DH))] * 2)
+    keep, send, sums = call(merge_kernel, "merge", loads, [shape((PAD, DH))] * 2 + [shape((8, NQ), F32)])
     other = swapped(send, "e", 2, 1)
     q, send = lax.optimization_barrier((q, send))
     scratch = [pltpu.VMEM((NQ, FEATS), BF16), pltpu.VMEM((NQ, NQ), BF16)]
-    sides = [q, qm, da, kv, km, *loads]
+    sides = [q, qm, da, kv, km, sums]
     dkv_part, dq_part = call(
         functools.partial(backward_kernel, NQ, 0, 2),
         "backward_one",
@@ -479,14 +491,14 @@
     dk_keep, dk_send, dv_keep, dv_send = call(
         core_kernel, "core", [dkv_keep, swapped(dkv_send, "c", 2, 1)], [shape(twice, F32), shape(twice)] * 2
     )
-    wgot, dk_send = lax.optimization_barrier((swapped(wsend, "x", 4, 3), dk_send))
+    wgot, dk_send = lax.optimization_barrier((by_core(wsend, "x", 1), dk_send))
     wkeep, wsend = call(
         middle_kernel, "middle_dwo", [wkeep, wgot], [shape((256, FEATS), F32), shape((256, FEATS))]
     )
     wkeep, wsend = call(
         ring_kernel,
         "ring",
-        [wkeep, swapped(wsend, "x", 4, 1)],
+        [wkeep, by_core(wsend, "x", 0)],
         [shape((128, FEATS), F32), shape((128, FEATS))],
     )
     wsend, outs[1], outs[3] = lax.optimization_barrier((wsend, outs[1], outs[3]))

time: 114 us -> 106 us (0.930); the launches traced: 114 us -> 104 us
  waiting for transfers between devices: 30.9 us -> 20 us
    ppermute x31 -> x29, waiting for transfers between devices: 28.4 us -> 18.2 us  [swapped(): return lax.ppermute(value, axis, [(i, i ^ mask) for i in range(size)])]
    ppermute x6, waiting for transfers between devices: 2.49 us -> 0.02 us  [shifted(): lax.ppermute(value, axis, [(i, (i + by) % size) for i in range(size)])]
    ppermute x0 -> x2, waiting for transfers between devices: none -> 1.75 us  [by_core(): lax.ppermute(value, (axis, 'c'), [(i, (i // 2 ^ masks[i % 2]) * 2 + i % 2...]
    ppermute x0 -> x2, starting transfers between devices: none -> 1.73 us  [by_core(): lax.ppermute(value, (axis, 'c'), [(i, (i // 2 ^ masks[i % 2]) * 2 + i % 2...]
    ppermute x31 -> x29, starting transfers between devices: 51.7 us -> 51.1 us  [swapped(): return lax.ppermute(value, axis, [(i, i ^ mask) for i in range(size)])]
  transfers between devices with their start and end apart: 37 -> 37, of which waited for: 19 -> 15; matrix products, arithmetic and copies ran while one was open for 1% -> 1% of each run, Pallas kernels for 13% -> 14%
where the time goes in v1:
time: 106 us; the launch traced here: 104 us
  starting transfers between devices  61.1 us (58%)
  waiting for transfers between devices  20 us (19%)
  Pallas kernels  19.4 us (18%)
  other arithmetic  2.72 us (3%)
    ppermute x29, starting transfers between devices, swapped(): return lax.ppermute(value, axis, [(i, i ^ mask) for i in range(size)])  51.1 us
    pallas_call x17, Pallas kernels, call(): pl.pallas_call(kernel, in_specs=[SMEM] * scalars + [VMEM] * (len(ins) - s...  19.4 us
    ppermute x29, waiting for transfers between devices, swapped(): return lax.ppermute(value, axis, [(i, i ^ mask) for i in range(size)])  18.2 us
    ppermute x6, starting transfers between devices, shifted(): lax.ppermute(value, axis, [(i, (i + by) % size) for i in range(size)])  8.26 us
  transfers between devices with their start and end apart: 37, of which 15 were waited for; matrix products, arithmetic and copies ran while one was open for 1% of the time, Pallas kernels for 14%

profile of v1, /device:TPU:8, one launch (start us, length us, event | category | flops | bytes accessed | tf_op | source)
XLA Modules:
  0.0 104.5 jit_solution(14090478930416177686)
XLA Ops:
  0.6 0.8 convert_bitcast_fusion.ids_ref.refs_5_
  1.4 1.0 pad_maximum_fusion.1.all_ref
  2.6 0.6 pack.1
  3.2 2.0 %collective-permute-start = (bf16[432,128]{1,0:T(8,128)(2,1)S(1)}, bf16[432,128]{1,0:T(8,128)(2,1)S(1)}, u32[]{:S(2)}, u32[]{:S(2)}) collective-permute-start(bf16[432,128]{1,0:T(8,128)(2,1)S(1)} %get-tuple-element.104), channel_id=1, source_target_pairs={{0,32},{32,0},{1,33},{33,1},{2,34},{34,2},{3,35},{35,3},{4,36},{36... | collective-permute-start | bytes 331784 | tf_op jit(solution)/shard_map/ppermute | solution.py:382
  5.2 0.4 collective-permute-start.5
  5.6 2.6 %collective-permute-start.4 = (bf16[136,512]{1,0:T(8,128)(2,1)S(1)}, bf16[136,512]{1,0:T(8,128)(2,1)S(1)}, u32[]{:S(2)}, u32[]{:S(2)}) collective-permute-start(bf16[136,512]{1,0:T(8,128)(2,1)S(1)} %get-tuple-element.111.refs_0_.dy0_ref), channel_id=1, source_target_pairs={{0,2},{1,3},{2,0},{3,1},{4,6},{5,7},{6,4},{7,5},{8,10},{9,11},{10,... | collective-permute-start | bytes 417800 | tf_op jit(solution)/shard_map/ppermute | solution.py:378
  8.2 1.9 %collective-permute-start.3 = (bf16[136,512]{1,0:T(8,128)(2,1)S(1)}, bf16[136,512]{1,0:T(8,128)(2,1)S(1)}, u32[]{:S(2)}, u32[]{:S(2)}) collective-permute-start(bf16[136,512]{1,0:T(8,128)(2,1)S(1)} %get-tuple-element.111.refs_0_.dy0_ref), channel_id=1, source_target_pairs={{0,1},{1,2},{2,3},{3,0},{4,5},{5,6},{6,7},{7,4},{8,9},{9,10},{10,1... | collective-permute-start | bytes 417800 | tf_op jit(solution)/shard_map/ppermute | solution.py:378
  10.2 0.1 pad_maximum_fusion.refs_4_.wo_ref
  10.4 3.4 %collective-permute-start.1 = (bf16[288,128]{1,0:T(8,128)(2,1)S(1)}, bf16[288,128]{1,0:T(8,128)(2,1)S(1)}, u32[]{:S(2)}, u32[]{:S(2)}) collective-permute-start(bf16[288,128]{1,0:T(8,128)(2,1)S(1)} %pad_maximum_fusion.4), channel_id=1, source_target_pairs={{0,64},{64,0},{128,192},{192,128},{1,65},{65,1},{129,193},{193,129... | collective-permute-start | bytes 221192 | tf_op jit(solution)/shard_map/ppermute | solution.py:382
  13.8 3.6 %collective-permute-start.2 = (bf16[288,128]{1,0:T(8,128)(2,1)S(1)}, bf16[288,128]{1,0:T(8,128)(2,1)S(1)}, u32[]{:S(2)}, u32[]{:S(2)}) collective-permute-start(bf16[288,128]{1,0:T(8,128)(2,1)S(1)} %pad_maximum_fusion.5), channel_id=1, source_target_pairs={{0,192},{64,128},{128,64},{192,0},{1,193},{65,129},{129,65},{193,1... | collective-permute-start | bytes 221192 | tf_op jit(solution)/shard_map/ppermute | solution.py:382
  17.4 2.8 %collective-permute-start.7 = (bf16[288,128]{1,0:T(8,128)(2,1)S(1)}, bf16[288,128]{1,0:T(8,128)(2,1)S(1)}, u32[]{:S(2)}, u32[]{:S(2)}) collective-permute-start(bf16[288,128]{1,0:T(8,128)(2,1)S(1)} %pad_maximum_fusion.6.refs_0_), channel_id=1, source_target_pairs={{0,24},{8,16},{16,8},{24,0},{1,25},{9,17},{17,9},{25,1},{2,26},{10... | collective-permute-start | bytes 221192 | tf_op jit(solution)/shard_map/ppermute | solution.py:382
  20.2 0.5 collective-permute-done.2
  20.7 1.5 %collective-permute-start.6 = (bf16[288,128]{1,0:T(8,128)(2,1)S(1)}, bf16[288,128]{1,0:T(8,128)(2,1)S(1)}, u32[]{:S(2)}, u32[]{:S(2)}) collective-permute-start(bf16[288,128]{1,0:T(8,128)(2,1)S(1)} %pad_maximum_fusion.6.refs_0_), channel_id=1, source_target_pairs={{0,8},{8,0},{16,24},{24,16},{1,9},{9,1},{17,25},{25,17},{2,10},{10... | collective-permute-start | bytes 221192 | tf_op jit(solution)/shard_map/ppermute | solution.py:382
  22.2 4.0 %collective-permute-start.9 = (bf16[576,128]{1,0:T(8,128)(2,1)S(1)}, bf16[576,128]{1,0:T(8,128)(2,1)S(1)}, u32[]{:S(2)}, u32[]{:S(2)}) collective-permute-start(bf16[576,128]{1,0:T(8,128)(2,1)S(1)} %pad_maximum_fusion.2), channel_id=1, source_target_pairs={{0,192},{64,128},{128,64},{192,0},{1,193},{65,129},{129,65},{193,1... | collective-permute-start | bytes 442376 | tf_op jit(solution)/shard_map/ppermute | solution.py:382
  26.3 0.9 collective-permute-start.10
  27.1 1.0 dattn.1
  28.2 1.8 %collective-permute-start.8 = (bf16[144,128]{1,0:T(8,128)(2,1)S(1)}, bf16[144,128]{1,0:T(8,128)(2,1)S(1)}, u32[]{:S(2)}, u32[]{:S(2)}) collective-permute-start(bf16[144,128]{1,0:T(8,128)(2,1)S(1)} %get-tuple-element.118), channel_id=1, source_target_pairs={{0,32},{32,0},{1,33},{33,1},{2,34},{34,2},{3,35},{35,3},{4,36},{36... | collective-permute-start | bytes 110600 | tf_op jit(solution)/shard_map/ppermute | solution.py:382
  30.0 2.7 %collective-permute-start.13 = (bf16[288,128]{1,0:T(8,128)(2,1)S(1)}, bf16[288,128]{1,0:T(8,128)(2,1)S(1)}, u32[]{:S(2)}, u32[]{:S(2)}) collective-permute-start(bf16[288,128]{1,0:T(8,128)(2,1)S(1)} %pad_maximum_fusion.6.refs_0_), channel_id=1, source_target_pairs={{0,16},{8,24},{16,0},{24,8},{1,17},{9,25},{17,1},{25,9},{2,18},{10... | collective-permute-start | bytes 221192 | tf_op jit(solution)/shard_map/ppermute | solution.py:382
  32.7 1.7 %collective-permute-start.12 = (bf16[288,128]{1,0:T(8,128)(2,1)S(1)}, bf16[288,128]{1,0:T(8,128)(2,1)S(1)}, u32[]{:S(2)}, u32[]{:S(2)}) collective-permute-start(bf16[288,128]{1,0:T(8,128)(2,1)S(1)} %constant_dynamic-update-slice_fusion.refs_0_), channel_id=1, source_target_pairs={{0,24},{8,16},{16,8},{24,0},{1,25},{9,17},{17,9},{25,1},{2,26},{10... | collective-permute-start | bytes 221192 | tf_op jit(solution)/shard_map/ppermute | solution.py:382
  34.4 0.6 collective-permute-start.11
  35.0 1.3 %collective-permute-done.13.refs_2_ = bf16[288,128]{1,0:T(8,128)(2,1)S(1)} collective-permute-done((bf16[288,128]{1,0:T(8,128)(2,1)S(1)}, bf16[288,128]{1,0:T(8,128)(2,1)S(1)}, u32[]{:S(2)}, u32[]{:S(2)}) %collective-permute-start.13) | collective-permute-done | bytes 73760 | tf_op jit(solution)/shard_map/ppermute | solution.py:382
  36.3 2.1 %collective-permute-done.12.refs_3_ = bf16[288,128]{1,0:T(8,128)(2,1)S(1)} collective-permute-done((bf16[288,128]{1,0:T(8,128)(2,1)S(1)}, bf16[288,128]{1,0:T(8,128)(2,1)S(1)}, u32[]{:S(2)}, u32[]{:S(2)}) %collective-permute-start.12) | collective-permute-done | bytes 73760 | tf_op jit(solution)/shard_map/ppermute | solution.py:382
  38.4 0.4 collective-permute-done.11.refs_1_
  38.9 1.6 %collective-permute-start.14 = (bf16[288,128]{1,0:T(8,128)(2,1)S(1)}, bf16[288,128]{1,0:T(8,128)(2,1)S(1)}, u32[]{:S(2)}, u32[]{:S(2)}) collective-permute-start(bf16[288,128]{1,0:T(8,128)(2,1)S(1)} %constant_dynamic-update-slice_fusion.refs_0_), channel_id=1, source_target_pairs={{0,16},{8,24},{16,0},{24,8},{1,17},{9,25},{17,1},{25,9},{2,18},{10... | collective-permute-start | bytes 221192 | tf_op jit(solution)/shard_map/ppermute | solution.py:382
  40.5 5.0 %forward.1 = (f32[1152,128]{1,0:T(8,128)S(1)}, f32[8,1152]{1,0:T(8,128)S(1)}, bf16[1152,128]{1,0:T(8,128)(2,1)S(1)}, bf16[1152,128]{1,0:T(8,128)(2,1)S(1)}, bf16...) custom-call(bf16[288,128]{1,0:T(8,128)(2,1)S(1)} %pad_maximum_fusion.6.refs_0_, ...), custom_call_target="tpu_custom_call" | custom-call | flops 2038431744 | bytes 1048576 | tf_op jit(solution)/shard_map/forward/pallas_call | solution.py:47
  45.6 0.4 share.1
  46.0 1.2 %collective-permute-start.17 = (bf16[368,128]{1,0:T(8,128)(2,1)S(1)}, bf16[368,128]{1,0:T(8,128)(2,1)S(1)}, u32[]{:S(2)}, u32[]{:S(2)}) collective-permute-start(bf16[368,128]{1,0:T(8,128)(2,1)S(1)} %get-tuple-element.132), channel_id=1, source_target_pairs={{0,8},{8,0},{16,24},{24,16},{1,9},{9,1},{17,25},{25,17},{2,10},{10... | collective-permute-start | bytes 282632 | tf_op jit(solution)/shard_map/ppermute | solution.py:382
  47.2 2.2 %collective-permute-start.18 = (bf16[368,128]{1,0:T(8,128)(2,1)S(1)}, bf16[368,128]{1,0:T(8,128)(2,1)S(1)}, u32[]{:S(2)}, u32[]{:S(2)}) collective-permute-start(bf16[368,128]{1,0:T(8,128)(2,1)S(1)} %get-tuple-element.133), channel_id=1, source_target_pairs={{0,16},{8,24},{16,0},{24,8},{1,17},{9,25},{17,1},{25,9},{2,18},{10... | collective-permute-start | bytes 282632 | tf_op jit(solution)/shard_map/ppermute | solution.py:382
  49.4 1.3 %collective-permute-start.19 = (bf16[368,128]{1,0:T(8,128)(2,1)S(1)}, bf16[368,128]{1,0:T(8,128)(2,1)S(1)}, u32[]{:S(2)}, u32[]{:S(2)}) collective-permute-start(bf16[368,128]{1,0:T(8,128)(2,1)S(1)} %get-tuple-element.134), channel_id=1, source_target_pairs={{0,24},{8,16},{16,8},{24,0},{1,25},{9,17},{17,9},{25,1},{2,26},{10... | collective-permute-start | bytes 282632 | tf_op jit(solution)/shard_map/ppermute | solution.py:382
  50.8 0.8 collective-permute-done.17.l1_ref
  51.6 2.5 %collective-permute-done.18.l2_ref = bf16[368,128]{1,0:T(8,128)(2,1)S(1)} collective-permute-done((bf16[368,128]{1,0:T(8,128)(2,1)S(1)}, bf16[368,128]{1,0:T(8,128)(2,1)S(1)}, u32[]{:S(2)}, u32[]{:S(2)}) %collective-permute-start.18) | collective-permute-done | bytes 94240 | tf_op jit(solution)/shard_map/ppermute | solution.py:382
  54.1 1.7 %collective-permute-done.19.l3_ref = bf16[368,128]{1,0:T(8,128)(2,1)S(1)} collective-permute-done((bf16[368,128]{1,0:T(8,128)(2,1)S(1)}, bf16[368,128]{1,0:T(8,128)(2,1)S(1)}, u32[]{:S(2)}, u32[]{:S(2)}) %collective-permute-start.19) | collective-permute-done | bytes 94240 | tf_op jit(solution)/shard_map/ppermute | solution.py:382
  55.8 0.9 merge.1
  56.7 1.8 %collective-permute-start.20 = (bf16[144,128]{1,0:T(8,128)(2,1)S(1)}, bf16[144,128]{1,0:T(8,128)(2,1)S(1)}, u32[]{:S(2)}, u32[]{:S(2)}) collective-permute-start(bf16[144,128]{1,0:T(8,128)(2,1)S(1)} %get-tuple-element.136), channel_id=1, source_target_pairs={{0,32},{32,0},{1,33},{33,1},{2,34},{34,2},{3,35},{35,3},{4,36},{36... | collective-permute-start | bytes 110600 | tf_op jit(solution)/shard_map/ppermute | solution.py:382
  58.5 2.8 %backward_one.1 = (bf16[768,256]{1,0:T(8,128)(2,1)S(1)}, f32[1152,128]{1,0:T(8,128)S(1)}) custom-call(bf16[1152,128]{1,0:T(8,128)(2,1)S(1)} %get-tuple-element.138.q_ref, bf16[1152,128]{1,0:T(8,128)(2,1)S(1)} %get-tuple-element.139.qm_ref, bf16[1152,128]{1,0:T(8,128)(2,1)S(1)} %get-tuple-element.140.da_ref, bf16[2304,256]{1,0:T(8,128)(2,1)S(1)} %get-tuple-element.141.kv_ref, ...), custom_call_target="tpu_custom_call" | custom-call | flops 1358954496 | bytes 1048576 | tf_op jit(solution)/shard_map/backward_one/pallas_call | solution.py:47
  61.3 1.2 %project.1 = (bf16[136,512]{1,0:T(8,128)(2,1)S(1)}, bf16[136,512]{1,0:T(8,128)(2,1)S(1)}, bf16[136,512]{1,0:T(8,128)(2,1)S(1)}, bf16[136,512]{1,0:T(8,128)(2,1)S...) custom-call(s32[5]{0:T(128)S(1)} %stack.23.at_ref, ...), custom_call_target="tpu_custom_call" | custom-call | tf_op jit(solution)/shard_map/project/pallas_call | solution.py:47
  62.6 0.3 collective-permute-start.21
  62.9 1.6 %backward_two.1 = (bf16[8,288,128]{2,1,0:T(8,128)(2,1)S(1)}, f32[1152,128]{1,0:T(8,128)S(1)}) custom-call(bf16[1152,128]{1,0:T(8,128)(2,1)S(1)} %get-tuple-element.138.q_ref, bf16[1152,128]{1,0:T(8,128)(2,1)S(1)} %get-tuple-element.139.qm_ref, bf16[1152,128]{1,0:T(8,128)(2,1)S(1)} %get-tuple-element.140.da_ref, ...), custom_call_target="tpu_custom_call" | custom-call | flops 679477248 | bytes 1048576 | tf_op jit(solution)/shard_map/backward_two/pallas_call | solution.py:47
  64.5 0.6 collective-permute-start.23
  65.2 1.6 %collective-permute-start.22 = (bf16[512,256]{1,0:T(8,128)(2,1)S(1)}, bf16[512,256]{1,0:T(8,128)(2,1)S(1)}, u32[]{:S(2)}, u32[]{:S(2)}) collective-permute-start(bf16[512,256]{1,0:T(8,128)(2,1)S(1)} %get-tuple-element.157), channel_id=1, source_target_pairs={{0,24},{4,12},{8,16},{12,4},{16,8},{20,28},{24,0},{28,20},{1,25},{... | collective-permute-start | bytes 786440 | tf_op jit(solution)/shard_map/ppermute | solution.py:387
  66.8 4.1 %backward_three.1 = (bf16[8,288,128]{2,1,0:T(8,128)(2,1)S(1)}, f32[576,128]{1,0:T(8,128)S(1)}, bf16[576,128]{1,0:T(8,128)(2,1)S(1)}) custom-call(bf16[1152,128]{1,0:T(8,128)(2,1)S(1)} %get-tuple-element.138.q_ref, bf16[1152,128]{1,0:T(8,128)(2,1)S(1)} %get-tuple-element.139.qm_ref, bf16[1152,128]{1,0:T(8,128)(2,1)S(1)} %get-tuple-element.140.da_ref, ...), custom_call_target="tpu_custom_call" | custom-call | flops 2038431744 | bytes 1048576 | tf_op jit(solution)/shard_map/backward_three/pallas_call | solution.py:47
  70.9 0.2 core.1
  71.1 1.7 %collective-permute-done.22.refs_1_ = bf16[512,256]{1,0:T(8,128)(2,1)S(1)} collective-permute-done((bf16[512,256]{1,0:T(8,128)(2,1)S(1)}, bf16[512,256]{1,0:T(8,128)(2,1)S(1)}, u32[]{:S(2)}, u32[]{:S(2)}) %collective-permute-start.22) | collective-permute-done | bytes 262176 | tf_op jit(solution)/shard_map/ppermute | solution.py:387
  73.0 2.0 %collective-permute-start.26 = (bf16[576,128]{1,0:T(8,128)(2,1)S(1)}, bf16[576,128]{1,0:T(8,128)(2,1)S(1)}, u32[]{:S(2)}, u32[]{:S(2)}) collective-permute-start(bf16[576,128]{1,0:T(8,128)(2,1)S(1)} %get-tuple-element.164), channel_id=1, source_target_pairs={{0,8},{8,0},{16,24},{24,16},{1,9},{9,1},{17,25},{25,17},{2,10},{10... | collective-permute-start | bytes 442376 | tf_op jit(solution)/shard_map/ppermute | solution.py:382
  75.0 3.2 %collective-permute-start.25 = (bf16[576,128]{1,0:T(8,128)(2,1)S(1)}, bf16[576,128]{1,0:T(8,128)(2,1)S(1)}, u32[]{:S(2)}, u32[]{:S(2)}) collective-permute-start(bf16[576,128]{1,0:T(8,128)(2,1)S(1)} %get-tuple-element.163), channel_id=1, source_target_pairs={{0,192},{64,128},{128,64},{192,0},{1,193},{65,129},{129,65},{193,1... | collective-permute-start | bytes 442376 | tf_op jit(solution)/shard_map/ppermute | solution.py:382
  78.2 1.6 %collective-permute-start.24 = (bf16[576,128]{1,0:T(8,128)(2,1)S(1)}, bf16[576,128]{1,0:T(8,128)(2,1)S(1)}, u32[]{:S(2)}, u32[]{:S(2)}) collective-permute-start(bf16[576,128]{1,0:T(8,128)(2,1)S(1)} %get-tuple-element.162), channel_id=1, source_target_pairs={{0,64},{64,0},{128,192},{192,128},{1,65},{65,1},{129,193},{193,129... | collective-permute-start | bytes 442376 | tf_op jit(solution)/shard_map/ppermute | solution.py:382
  79.9 0.2 collective-permute-start.28
  80.1 1.9 %collective-permute-start.29 = (bf16[136,512]{1,0:T(8,128)(2,1)S(1)}, bf16[136,512]{1,0:T(8,128)(2,1)S(1)}, u32[]{:S(2)}, u32[]{:S(2)}) collective-permute-start(bf16[136,512]{1,0:T(8,128)(2,1)S(1)} %get-tuple-element.174), channel_id=1, source_target_pairs={{0,3},{1,0},{2,1},{3,2},{4,7},{5,4},{6,5},{7,6},{8,11},{9,8},{10,9... | collective-permute-start | bytes 417800 | tf_op jit(solution)/shard_map/ppermute | solution.py:378
  82.0 1.2 %collective-permute-start.30 = (bf16[136,512]{1,0:T(8,128)(2,1)S(1)}, bf16[136,512]{1,0:T(8,128)(2,1)S(1)}, u32[]{:S(2)}, u32[]{:S(2)}) collective-permute-start(bf16[136,512]{1,0:T(8,128)(2,1)S(1)} %get-tuple-element.176), channel_id=1, source_target_pairs={{0,2},{1,3},{2,0},{3,1},{4,6},{5,7},{6,4},{7,5},{8,10},{9,11},{10,... | collective-permute-start | bytes 417800 | tf_op jit(solution)/shard_map/ppermute | solution.py:378
  83.2 0.5 collective-permute-done.25.refs_3_
  83.7 2.6 %collective-permute-done.24.refs_1_ = bf16[576,128]{1,0:T(8,128)(2,1)S(1)} collective-permute-done((bf16[576,128]{1,0:T(8,128)(2,1)S(1)}, bf16[576,128]{1,0:T(8,128)(2,1)S(1)}, u32[]{:S(2)}, u32[]{:S(2)}) %collective-permute-start.24) | collective-permute-done | bytes 147488 | tf_op jit(solution)/shard_map/ppermute | solution.py:382
  86.3 1.5 %collective-permute-start.34 = (bf16[128,256]{1,0:T(8,128)(2,1)S(1)}, bf16[128,256]{1,0:T(8,128)(2,1)S(1)}, u32[]{:S(2)}, u32[]{:S(2)}) collective-permute-start(bf16[128,256]{1,0:T(8,128)(2,1)S(1)} %get-tuple-element.191), channel_id=1, source_target_pairs={{0,192},{64,128},{128,64},{192,0},{1,193},{65,129},{129,65},{193,1... | collective-permute-start | bytes 196616 | tf_op jit(solution)/shard_map/ppermute | solution.py:382
  88.0 1.8 %collective-permute-start.31 = (bf16[288,128]{1,0:T(8,128)(2,1)S(1)}, bf16[288,128]{1,0:T(8,128)(2,1)S(1)}, u32[]{:S(2)}, u32[]{:S(2)}) collective-permute-start(bf16[288,128]{1,0:T(8,128)(2,1)S(1)} %get-tuple-element.185), channel_id=1, source_target_pairs={{0,24},{8,16},{16,8},{24,0},{1,25},{9,17},{17,9},{25,1},{2,26},{10... | collective-permute-start | bytes 221192 | tf_op jit(solution)/shard_map/ppermute | solution.py:382
  89.8 2.2 %collective-permute-start.32 = (bf16[288,128]{1,0:T(8,128)(2,1)S(1)}, bf16[288,128]{1,0:T(8,128)(2,1)S(1)}, u32[]{:S(2)}, u32[]{:S(2)}) collective-permute-start(bf16[288,128]{1,0:T(8,128)(2,1)S(1)} %get-tuple-element.187), channel_id=1, source_target_pairs={{0,192},{64,128},{128,64},{192,0},{1,193},{65,129},{129,65},{193,1... | collective-permute-start | bytes 221192 | tf_op jit(solution)/shard_map/ppermute | solution.py:382
  92.0 0.5 collective-permute-start.33
  92.6 0.3 collective-permute-done.34.got_ref
  92.8 2.2 %collective-permute-start.35 = (bf16[64,256]{1,0:T(8,128)(2,1)S(1)}, bf16[64,256]{1,0:T(8,128)(2,1)S(1)}, u32[]{:S(2)}, u32[]{:S(2)}) collective-permute-start(bf16[64,256]{1,0:T(8,128)(2,1)S(1)} %get-tuple-element.193), channel_id=1, source_target_pairs={{0,64},{64,0},{128,192},{192,128},{1,65},{65,1},{129,193},{193,129... | collective-permute-start | bytes 98312 | tf_op jit(solution)/shard_map/ppermute | solution.py:382
  95.1 1.3 %collective-permute-done.32.refs_3_ = bf16[288,128]{1,0:T(8,128)(2,1)S(1)} collective-permute-done((bf16[288,128]{1,0:T(8,128)(2,1)S(1)}, bf16[288,128]{1,0:T(8,128)(2,1)S(1)}, u32[]{:S(2)}, u32[]{:S(2)}) %collective-permute-start.32) | collective-permute-done | bytes 73760 | tf_op jit(solution)/shard_map/ppermute | solution.py:382
  96.4 1.4 %collective-permute-done.33.refs_5_ = bf16[288,128]{1,0:T(8,128)(2,1)S(1)} collective-permute-done((bf16[288,128]{1,0:T(8,128)(2,1)S(1)}, bf16[288,128]{1,0:T(8,128)(2,1)S(1)}, u32[]{:S(2)}, u32[]{:S(2)}) %collective-permute-start.33) | collective-permute-done | bytes 73760 | tf_op jit(solution)/shard_map/ppermute | solution.py:382
  97.8 0.4 collective-permute-done.35.refs_7_
  98.2 1.8 %collective-permute-start.36 = (bf16[496,128]{1,0:T(8,128)(2,1)S(1)}, bf16[496,128]{1,0:T(8,128)(2,1)S(1)}, u32[]{:S(2)}, u32[]{:S(2)}) collective-permute-start(bf16[496,128]{1,0:T(8,128)(2,1)S(1)} %get-tuple-element.196), channel_id=1, source_target_pairs={{0,32},{32,0},{1,33},{33,1},{2,34},{34,2},{3,35},{35,3},{4,36},{36... | collective-permute-start | bytes 380936 | tf_op jit(solution)/shard_map/ppermute | solution.py:382
  100.0 0.7 add_convert_fusion
  100.7 2.5 %collective-permute-done.36.got_ref = bf16[496,128]{1,0:T(8,128)(2,1)S(1)} collective-permute-done((bf16[496,128]{1,0:T(8,128)(2,1)S(1)}, bf16[496,128]{1,0:T(8,128)(2,1)S(1)}, u32[]{:S(2)}, u32[]{:S(2)}) %collective-permute-start.36) | collective-permute-done | bytes 127008 | tf_op jit(solution)/shard_map/ppermute | solution.py:382
  103.2 1.3 %place.1 = (bf16[136,256]{1,0:T(8,128)(2,1)}, bf16[136,256]{1,0:T(8,128)(2,1)}, bf16[136,256]{1,0:T(8,128)(2,1)}, f32[32,256]{1,0:T(8,128)}) custom-call(s32[5]{0:T(128)S(1)} %stack.23.at_ref, bf16[144,384]{1,0:T(8,128)(2,1)S(1)} %get-tuple-element.194.mine_ref, f32[32,256]{1,0:T(8,128)S(1)} %get-tuple-element.195.wmine_ref, ...), custom_call_target="tpu_custom_call" | custom-call | tf_op jit(solution)/shard_map/place/pallas_call | solution.py:47
  (48 shorter events, 0.9 us)
Async XLA Ops:
  0.6 9.5 %copy-start = (bf16[256,2048]{1,0:T(8,128)(2,1)S(1)}, bf16[256,2048]{1,0:T(8,128)(2,1)}, u32[]{:S(2)}) copy-start(bf16[256,2048]{1,0:T(8,128)(2,1)} %param.10) | copy-start | bytes 3145732
  3.2 7.2 %collective-permute-start = (bf16[432,128]{1,0:T(8,128)(2,1)S(1)}, bf16[432,128]{1,0:T(8,128)(2,1)S(1)}, u32[]{:S(2)}, u32[]{:S(2)}) collective-permute-start(bf16[432,128]{1,0:T(8,128)(2,1)S(1)} %get-tuple-element.104), channel_id=1, source_target_pairs={{0,32},{32,0},{1,33},{33,1},{2,34},{34,2},{3,35},{35,3},{4,36},{36... | collective-permute-start | bytes 331784 | tf_op jit(solution)/shard_map/ppermute | solution.py:382
  5.2 17.0 %collective-permute-start.5 = (bf16[136,512]{1,0:T(8,128)(2,1)S(1)}, bf16[136,512]{1,0:T(8,128)(2,1)S(1)}, u32[]{:S(2)}, u32[]{:S(2)}) collective-permute-start(bf16[136,512]{1,0:T(8,128)(2,1)S(1)} %get-tuple-element.111.refs_0_.dy0_ref), channel_id=1, source_target_pairs={{0,3},{1,0},{2,1},{3,2},{4,7},{5,4},{6,5},{7,6},{8,11},{9,8},{10,9... | collective-permute-start | bytes 417800 | tf_op jit(solution)/shard_map/ppermute | solution.py:378
  5.6 16.6 %collective-permute-start.4 = (bf16[136,512]{1,0:T(8,128)(2,1)S(1)}, bf16[136,512]{1,0:T(8,128)(2,1)S(1)}, u32[]{:S(2)}, u32[]{:S(2)}) collective-permute-start(bf16[136,512]{1,0:T(8,128)(2,1)S(1)} %get-tuple-element.111.refs_0_.dy0_ref), channel_id=1, source_target_pairs={{0,2},{1,3},{2,0},{3,1},{4,6},{5,7},{6,4},{7,5},{8,10},{9,11},{10,... | collective-permute-start | bytes 417800 | tf_op jit(solution)/shard_map/ppermute | solution.py:378
  8.2 14.0 %collective-permute-start.3 = (bf16[136,512]{1,0:T(8,128)(2,1)S(1)}, bf16[136,512]{1,0:T(8,128)(2,1)S(1)}, u32[]{:S(2)}, u32[]{:S(2)}) collective-permute-start(bf16[136,512]{1,0:T(8,128)(2,1)S(1)} %get-tuple-element.111.refs_0_.dy0_ref), channel_id=1, source_target_pairs={{0,1},{1,2},{2,3},{3,0},{4,5},{5,6},{6,7},{7,4},{8,9},{9,10},{10,1... | collective-permute-start | bytes 417800 | tf_op jit(solution)/shard_map/ppermute | solution.py:378
  10.4 7.0 %collective-permute-start.1 = (bf16[288,128]{1,0:T(8,128)(2,1)S(1)}, bf16[288,128]{1,0:T(8,128)(2,1)S(1)}, u32[]{:S(2)}, u32[]{:S(2)}) collective-permute-start(bf16[288,128]{1,0:T(8,128)(2,1)S(1)} %pad_maximum_fusion.4), channel_id=1, source_target_pairs={{0,64},{64,0},{128,192},{192,128},{1,65},{65,1},{129,193},{193,129... | collective-permute-start | bytes 221192 | tf_op jit(solution)/shard_map/ppermute | solution.py:382
  13.8 6.9 %collective-permute-start.2 = (bf16[288,128]{1,0:T(8,128)(2,1)S(1)}, bf16[288,128]{1,0:T(8,128)(2,1)S(1)}, u32[]{:S(2)}, u32[]{:S(2)}) collective-permute-start(bf16[288,128]{1,0:T(8,128)(2,1)S(1)} %pad_maximum_fusion.5), channel_id=1, source_target_pairs={{0,192},{64,128},{128,64},{192,0},{1,193},{65,129},{129,65},{193,1... | collective-permute-start | bytes 221192 | tf_op jit(solution)/shard_map/ppermute | solution.py:382
  17.4 8.9 %collective-permute-start.7 = (bf16[288,128]{1,0:T(8,128)(2,1)S(1)}, bf16[288,128]{1,0:T(8,128)(2,1)S(1)}, u32[]{:S(2)}, u32[]{:S(2)}) collective-permute-start(bf16[288,128]{1,0:T(8,128)(2,1)S(1)} %pad_maximum_fusion.6.refs_0_), channel_id=1, source_target_pairs={{0,24},{8,16},{16,8},{24,0},{1,25},{9,17},{17,9},{25,1},{2,26},{10... | collective-permute-start | bytes 221192 | tf_op jit(solution)/shard_map/ppermute | solution.py:382
  20.7 5.6 %collective-permute-start.6 = (bf16[288,128]{1,0:T(8,128)(2,1)S(1)}, bf16[288,128]{1,0:T(8,128)(2,1)S(1)}, u32[]{:S(2)}, u32[]{:S(2)}) collective-permute-start(bf16[288,128]{1,0:T(8,128)(2,1)S(1)} %pad_maximum_fusion.6.refs_0_), channel_id=1, source_target_pairs={{0,8},{8,0},{16,24},{24,16},{1,9},{9,1},{17,25},{25,17},{2,10},{10... | collective-permute-start | bytes 221192 | tf_op jit(solution)/shard_map/ppermute | solution.py:382
  22.2 16.5 %collective-permute-start.9 = (bf16[576,128]{1,0:T(8,128)(2,1)S(1)}, bf16[576,128]{1,0:T(8,128)(2,1)S(1)}, u32[]{:S(2)}, u32[]{:S(2)}) collective-permute-start(bf16[576,128]{1,0:T(8,128)(2,1)S(1)} %pad_maximum_fusion.2), channel_id=1, source_target_pairs={{0,192},{64,128},{128,64},{192,0},{1,193},{65,129},{129,65},{193,1... | collective-permute-start | bytes 442376 | tf_op jit(solution)/shard_map/ppermute | solution.py:382
  26.3 12.5 %collective-permute-start.10 = (bf16[576,128]{1,0:T(8,128)(2,1)S(1)}, bf16[576,128]{1,0:T(8,128)(2,1)S(1)}, u32[]{:S(2)}, u32[]{:S(2)}) collective-permute-start(bf16[576,128]{1,0:T(8,128)(2,1)S(1)} %pad_maximum_fusion.3), channel_id=1, source_target_pairs={{0,64},{64,0},{128,192},{192,128},{1,65},{65,1},{129,193},{193,129... | collective-permute-start | bytes 442376 | tf_op jit(solution)/shard_map/ppermute | solution.py:382
  28.2 4.5 %collective-permute-start.8 = (bf16[144,128]{1,0:T(8,128)(2,1)S(1)}, bf16[144,128]{1,0:T(8,128)(2,1)S(1)}, u32[]{:S(2)}, u32[]{:S(2)}) collective-permute-start(bf16[144,128]{1,0:T(8,128)(2,1)S(1)} %get-tuple-element.118), channel_id=1, source_target_pairs={{0,32},{32,0},{1,33},{33,1},{2,34},{34,2},{3,35},{35,3},{4,36},{36... | collective-permute-start | bytes 110600 | tf_op jit(solution)/shard_map/ppermute | solution.py:382
  30.0 6.3 %collective-permute-start.13 = (bf16[288,128]{1,0:T(8,128)(2,1)S(1)}, bf16[288,128]{1,0:T(8,128)(2,1)S(1)}, u32[]{:S(2)}, u32[]{:S(2)}) collective-permute-start(bf16[288,128]{1,0:T(8,128)(2,1)S(1)} %pad_maximum_fusion.6.refs_0_), channel_id=1, source_target_pairs={{0,16},{8,24},{16,0},{24,8},{1,17},{9,25},{17,1},{25,9},{2,18},{10... | collective-permute-start | bytes 221192 | tf_op jit(solution)/shard_map/ppermute | solution.py:382
  32.7 5.7 %collective-permute-start.12 = (bf16[288,128]{1,0:T(8,128)(2,1)S(1)}, bf16[288,128]{1,0:T(8,128)(2,1)S(1)}, u32[]{:S(2)}, u32[]{:S(2)}) collective-permute-start(bf16[288,128]{1,0:T(8,128)(2,1)S(1)} %constant_dynamic-update-slice_fusion.refs_0_), channel_id=1, source_target_pairs={{0,24},{8,16},{16,8},{24,0},{1,25},{9,17},{17,9},{25,1},{2,26},{10... | collective-permute-start | bytes 221192 | tf_op jit(solution)/shard_map/ppermute | solution.py:382
  34.4 4.4 %collective-permute-start.11 = (bf16[288,128]{1,0:T(8,128)(2,1)S(1)}, bf16[288,128]{1,0:T(8,128)(2,1)S(1)}, u32[]{:S(2)}, u32[]{:S(2)}) collective-permute-start(bf16[288,128]{1,0:T(8,128)(2,1)S(1)} %constant_dynamic-update-slice_fusion.refs_0_), channel_id=1, source_target_pairs={{0,8},{8,0},{16,24},{24,16},{1,9},{9,1},{17,25},{25,17},{2,10},{10... | collective-permute-start | bytes 221192 | tf_op jit(solution)/shard_map/ppermute | solution.py:382
  36.3 4.3 %collective-permute-start.15 = (bf16[1152,128]{1,0:T(8,128)(2,1)S(1)}, bf16[1152,128]{1,0:T(8,128)(2,1)S(1)}, u32[]{:S(2)}, u32[]{:S(2)}) collective-permute-start(bf16[1152,128]{1,0:T(8,128)(2,1)S(1)} %constant_dynamic-update-slice_fusion.2.refs_4_), channel_id=1, source_target_pairs={{0,4},{4,0},{1,5},{5,1},{2,6},{6,2},{3,7},{7,3},{8,12},{12,8},{9,1... | collective-permute-start | bytes 884744 | tf_op jit(solution)/shard_map/ppermute | solution.py:382
  38.8 1.7 %collective-permute-start.16 = (bf16[1152,128]{1,0:T(8,128)(2,1)S(1)}, bf16[1152,128]{1,0:T(8,128)(2,1)S(1)}, u32[]{:S(2)}, u32[]{:S(2)}) collective-permute-start(bf16[1152,128]{1,0:T(8,128)(2,1)S(1)} %constant_dynamic-update-slice_fusion.4.refs_5_), channel_id=1, source_target_pairs={{0,4},{4,0},{1,5},{5,1},{2,6},{6,2},{3,7},{7,3},{8,12},{12,8},{9,1... | collective-permute-start | bytes 884744 | tf_op jit(solution)/shard_map/ppermute | solution.py:382
  38.9 6.6 %collective-permute-start.14 = (bf16[288,128]{1,0:T(8,128)(2,1)S(1)}, bf16[288,128]{1,0:T(8,128)(2,1)S(1)}, u32[]{:S(2)}, u32[]{:S(2)}) collective-permute-start(bf16[288,128]{1,0:T(8,128)(2,1)S(1)} %constant_dynamic-update-slice_fusion.refs_0_), channel_id=1, source_target_pairs={{0,16},{8,24},{16,0},{24,8},{1,17},{9,25},{17,1},{25,9},{2,18},{10... | collective-permute-start | bytes 221192 | tf_op jit(solution)/shard_map/ppermute | solution.py:382
  46.0 5.6 %collective-permute-start.17 = (bf16[368,128]{1,0:T(8,128)(2,1)S(1)}, bf16[368,128]{1,0:T(8,128)(2,1)S(1)}, u32[]{:S(2)}, u32[]{:S(2)}) collective-permute-start(bf16[368,128]{1,0:T(8,128)(2,1)S(1)} %get-tuple-element.132), channel_id=1, source_target_pairs={{0,8},{8,0},{16,24},{24,16},{1,9},{9,1},{17,25},{25,17},{2,10},{10... | collective-permute-start | bytes 282632 | tf_op jit(solution)/shard_map/ppermute | solution.py:382
  47.2 6.9 %collective-permute-start.18 = (bf16[368,128]{1,0:T(8,128)(2,1)S(1)}, bf16[368,128]{1,0:T(8,128)(2,1)S(1)}, u32[]{:S(2)}, u32[]{:S(2)}) collective-permute-start(bf16[368,128]{1,0:T(8,128)(2,1)S(1)} %get-tuple-element.133), channel_id=1, source_target_pairs={{0,16},{8,24},{16,0},{24,8},{1,17},{9,25},{17,1},{25,9},{2,18},{10... | collective-permute-start | bytes 282632 | tf_op jit(solution)/shard_map/ppermute | solution.py:382
  49.4 6.4 %collective-permute-start.19 = (bf16[368,128]{1,0:T(8,128)(2,1)S(1)}, bf16[368,128]{1,0:T(8,128)(2,1)S(1)}, u32[]{:S(2)}, u32[]{:S(2)}) collective-permute-start(bf16[368,128]{1,0:T(8,128)(2,1)S(1)} %get-tuple-element.134), channel_id=1, source_target_pairs={{0,24},{8,16},{16,8},{24,0},{1,25},{9,17},{17,9},{25,1},{2,26},{10... | collective-permute-start | bytes 282632 | tf_op jit(solution)/shard_map/ppermute | solution.py:382
  56.7 4.6 %collective-permute-start.20 = (bf16[144,128]{1,0:T(8,128)(2,1)S(1)}, bf16[144,128]{1,0:T(8,128)(2,1)S(1)}, u32[]{:S(2)}, u32[]{:S(2)}) collective-permute-start(bf16[144,128]{1,0:T(8,128)(2,1)S(1)} %get-tuple-element.136), channel_id=1, source_target_pairs={{0,32},{32,0},{1,33},{33,1},{2,34},{34,2},{3,35},{35,3},{4,36},{36... | collective-permute-start | bytes 110600 | tf_op jit(solution)/shard_map/ppermute | solution.py:382
  62.6 2.5 %collective-permute-start.21 = (bf16[4,256,256]{2,1,0:T(8,128)(2,1)S(1)}, bf16[4,256,256]{2,1,0:T(8,128)(2,1)S(1)}, u32[]{:S(2)}, u32[]{:S(2)}) collective-permute-start(bf16[4,256,256]{2,1,0:T(8,128)(2,1)S(1)} %get-tuple-element.150), channel_id=1, source_target_pairs={{0,4},{4,0},{1,5},{5,1},{2,6},{6,2},{3,7},{7,3},{8,12},{12,8},{9,1... | collective-permute-start | bytes 1572872 | tf_op jit(solution)/shard_map/ppermute | solution.py:382
  64.5 6.5 %collective-permute-start.23 = (bf16[8,288,128]{2,1,0:T(8,128)(2,1)S(1)}, bf16[8,288,128]{2,1,0:T(8,128)(2,1)S(1)}, u32[]{:S(2)}, u32[]{:S(2)}) collective-permute-start(bf16[8,288,128]{2,1,0:T(8,128)(2,1)S(1)} %get-tuple-element.160), channel_id=1, source_target_pairs={{0,4},{4,0},{1,5},{5,1},{2,6},{6,2},{3,7},{7,3},{8,12},{12,8},{9,1... | collective-permute-start | bytes 1769480 | tf_op jit(solution)/shard_map/ppermute | solution.py:382
  65.2 7.7 %collective-permute-start.22 = (bf16[512,256]{1,0:T(8,128)(2,1)S(1)}, bf16[512,256]{1,0:T(8,128)(2,1)S(1)}, u32[]{:S(2)}, u32[]{:S(2)}) collective-permute-start(bf16[512,256]{1,0:T(8,128)(2,1)S(1)} %get-tuple-element.157), channel_id=1, source_target_pairs={{0,24},{4,12},{8,16},{12,4},{16,8},{20,28},{24,0},{28,20},{1,25},{... | collective-permute-start | bytes 786440 | tf_op jit(solution)/shard_map/ppermute | solution.py:387
  72.9 7.0 %collective-permute-start.27 = (bf16[256,256]{1,0:T(8,128)(2,1)S(1)}, bf16[256,256]{1,0:T(8,128)(2,1)S(1)}, u32[]{:S(2)}, u32[]{:S(2)}) collective-permute-start(bf16[256,256]{1,0:T(8,128)(2,1)S(1)} %get-tuple-element.168), channel_id=1, source_target_pairs={{0,8},{4,28},{8,0},{12,20},{16,24},{20,12},{24,16},{28,4},{1,9},{5... | collective-permute-start | bytes 393224 | tf_op jit(solution)/shard_map/ppermute | solution.py:387
  73.0 9.0 %collective-permute-start.26 = (bf16[576,128]{1,0:T(8,128)(2,1)S(1)}, bf16[576,128]{1,0:T(8,128)(2,1)S(1)}, u32[]{:S(2)}, u32[]{:S(2)}) collective-permute-start(bf16[576,128]{1,0:T(8,128)(2,1)S(1)} %get-tuple-element.164), channel_id=1, source_target_pairs={{0,8},{8,0},{16,24},{24,16},{1,9},{9,1},{17,25},{25,17},{2,10},{10... | collective-permute-start | bytes 442376 | tf_op jit(solution)/shard_map/ppermute | solution.py:382
  75.0 8.7 %collective-permute-start.25 = (bf16[576,128]{1,0:T(8,128)(2,1)S(1)}, bf16[576,128]{1,0:T(8,128)(2,1)S(1)}, u32[]{:S(2)}, u32[]{:S(2)}) collective-permute-start(bf16[576,128]{1,0:T(8,128)(2,1)S(1)} %get-tuple-element.163), channel_id=1, source_target_pairs={{0,192},{64,128},{128,64},{192,0},{1,193},{65,129},{129,65},{193,1... | collective-permute-start | bytes 442376 | tf_op jit(solution)/shard_map/ppermute | solution.py:382
  78.2 8.1 %collective-permute-start.24 = (bf16[576,128]{1,0:T(8,128)(2,1)S(1)}, bf16[576,128]{1,0:T(8,128)(2,1)S(1)}, u32[]{:S(2)}, u32[]{:S(2)}) collective-permute-start(bf16[576,128]{1,0:T(8,128)(2,1)S(1)} %get-tuple-element.162), channel_id=1, source_target_pairs={{0,64},{64,0},{128,192},{192,128},{1,65},{65,1},{129,193},{193,129... | collective-permute-start | bytes 442376 | tf_op jit(solution)/shard_map/ppermute | solution.py:382
  79.9 6.4 %collective-permute-start.28 = (bf16[136,512]{1,0:T(8,128)(2,1)S(1)}, bf16[136,512]{1,0:T(8,128)(2,1)S(1)}, u32[]{:S(2)}, u32[]{:S(2)}) collective-permute-start(bf16[136,512]{1,0:T(8,128)(2,1)S(1)} %get-tuple-element.173), channel_id=1, source_target_pairs={{0,1},{1,2},{2,3},{3,0},{4,5},{5,6},{6,7},{7,4},{8,9},{9,10},{10,1... | collective-permute-start | bytes 417800 | tf_op jit(solution)/shard_map/ppermute | solution.py:378
  80.1 6.2 %collective-permute-start.29 = (bf16[136,512]{1,0:T(8,128)(2,1)S(1)}, bf16[136,512]{1,0:T(8,128)(2,1)S(1)}, u32[]{:S(2)}, u32[]{:S(2)}) collective-permute-start(bf16[136,512]{1,0:T(8,128)(2,1)S(1)} %get-tuple-element.174), channel_id=1, source_target_pairs={{0,3},{1,0},{2,1},{3,2},{4,7},{5,4},{6,5},{7,6},{8,11},{9,8},{10,9... | collective-permute-start | bytes 417800 | tf_op jit(solution)/shard_map/ppermute | solution.py:378
  82.0 18.0 %collective-permute-start.30 = (bf16[136,512]{1,0:T(8,128)(2,1)S(1)}, bf16[136,512]{1,0:T(8,128)(2,1)S(1)}, u32[]{:S(2)}, u32[]{:S(2)}) collective-permute-start(bf16[136,512]{1,0:T(8,128)(2,1)S(1)} %get-tuple-element.176), channel_id=1, source_target_pairs={{0,2},{1,3},{2,0},{3,1},{4,6},{5,7},{6,4},{7,5},{8,10},{9,11},{10,... | collective-permute-start | bytes 417800 | tf_op jit(solution)/shard_map/ppermute | solution.py:378
  86.3 6.5 %collective-permute-start.34 = (bf16[128,256]{1,0:T(8,128)(2,1)S(1)}, bf16[128,256]{1,0:T(8,128)(2,1)S(1)}, u32[]{:S(2)}, u32[]{:S(2)}) collective-permute-start(bf16[128,256]{1,0:T(8,128)(2,1)S(1)} %get-tuple-element.191), channel_id=1, source_target_pairs={{0,192},{64,128},{128,64},{192,0},{1,193},{65,129},{129,65},{193,1... | collective-permute-start | bytes 196616 | tf_op jit(solution)/shard_map/ppermute | solution.py:382
  88.0 7.1 %collective-permute-start.31 = (bf16[288,128]{1,0:T(8,128)(2,1)S(1)}, bf16[288,128]{1,0:T(8,128)(2,1)S(1)}, u32[]{:S(2)}, u32[]{:S(2)}) collective-permute-start(bf16[288,128]{1,0:T(8,128)(2,1)S(1)} %get-tuple-element.185), channel_id=1, source_target_pairs={{0,24},{8,16},{16,8},{24,0},{1,25},{9,17},{17,9},{25,1},{2,26},{10... | collective-permute-start | bytes 221192 | tf_op jit(solution)/shard_map/ppermute | solution.py:382
  89.8 6.6 %collective-permute-start.32 = (bf16[288,128]{1,0:T(8,128)(2,1)S(1)}, bf16[288,128]{1,0:T(8,128)(2,1)S(1)}, u32[]{:S(2)}, u32[]{:S(2)}) collective-permute-start(bf16[288,128]{1,0:T(8,128)(2,1)S(1)} %get-tuple-element.187), channel_id=1, source_target_pairs={{0,192},{64,128},{128,64},{192,0},{1,193},{65,129},{129,65},{193,1... | collective-permute-start | bytes 221192 | tf_op jit(solution)/shard_map/ppermute | solution.py:382
  92.0 5.8 %collective-permute-start.33 = (bf16[288,128]{1,0:T(8,128)(2,1)S(1)}, bf16[288,128]{1,0:T(8,128)(2,1)S(1)}, u32[]{:S(2)}, u32[]{:S(2)}) collective-permute-start(bf16[288,128]{1,0:T(8,128)(2,1)S(1)} %get-tuple-element.189), channel_id=1, source_target_pairs={{0,64},{64,0},{128,192},{192,128},{1,65},{65,1},{129,193},{193,129... | collective-permute-start | bytes 221192 | tf_op jit(solution)/shard_map/ppermute | solution.py:382
  92.8 5.3 %collective-permute-start.35 = (bf16[64,256]{1,0:T(8,128)(2,1)S(1)}, bf16[64,256]{1,0:T(8,128)(2,1)S(1)}, u32[]{:S(2)}, u32[]{:S(2)}) collective-permute-start(bf16[64,256]{1,0:T(8,128)(2,1)S(1)} %get-tuple-element.193), channel_id=1, source_target_pairs={{0,64},{64,0},{128,192},{192,128},{1,65},{65,1},{129,193},{193,129... | collective-permute-start | bytes 98312 | tf_op jit(solution)/shard_map/ppermute | solution.py:382
  98.2 5.0 %collective-permute-start.36 = (bf16[496,128]{1,0:T(8,128)(2,1)S(1)}, bf16[496,128]{1,0:T(8,128)(2,1)S(1)}, u32[]{:S(2)}, u32[]{:S(2)}) collective-permute-start(bf16[496,128]{1,0:T(8,128)(2,1)S(1)} %get-tuple-element.196), channel_id=1, source_target_pairs={{0,32},{32,0},{1,33},{33,1},{2,34},{34,2},{3,35},{35,3},{4,36},{36... | collective-permute-start | bytes 380936 | tf_op jit(solution)/shard_map/ppermute | solution.py:382

commit v2 on v1

--- a/solution.py
+++ b/solution.py
@@ -409,7 +409,9 @@
     k, v, q = (jnp.concatenate([keep[i : i + PAD], got[i : i + PAD]], axis=0) for i in (0, PAD, 2 * PAD))
     k = jnp.concatenate([k, swapped(k, "zr", 4, 1)], axis=0)
     v = jnp.concatenate([v, swapped(v, "zr", 4, 3)], axis=0)
-    dys = around(dy, "head")
+    dys = [dy, shifted(dy, "head", NH, 1), None, shifted(dy, "head", NH, 3)]
+    dy_late, _ = lax.optimization_barrier((dy, got))
+    dys[2] = shifted(dy_late, "head", NH, 2)
     q_one, q_three = swapped(q, "x", 4, 1), swapped(q, "x", 4, 3)
     k, v, dys = lax.optimization_barrier((k, v, dys))
     ks, vs = [k, swapped(k, "zr", 4, 3)], [v, swapped(v, "zr", 4, 1)]
@@ -422,11 +424,11 @@
     keep, send = call(dattn_kernel, "dattn", [at, *dys, wo, ids], [shape((PAD, DH))] * 2, scalars=1)
     q_late, send = lax.optimization_barrier((q, send))
     q_two = swapped(q_late, "x", 4, 2)
-    da = jnp.concatenate([keep, swapped(send, "e", 2, 1)], axis=0)
+    da_got = swapped(send, "e", 2, 1)
+    ks[1], vs[1], da_got, q_two = lax.optimization_barrier((ks[1], vs[1], da_got, q_two))
+    qs = [q, q_one, q_two, q_three]
+    da = jnp.concatenate([keep, da_got], axis=0)
     das = [da] + [swapped(da, "x", 4, s) for s in (1, 2, 3)]
-    late = [ks[1], vs[1], das[1], das[3], q_two]
-    ks[1], vs[1], das[1], das[3], q_two = lax.optimization_barrier(late)
-    qs = [q, q_one, q_two, q_three]
     kvs = [jnp.concatenate([ks[i], vs[i]], axis=0) for i in range(2)]
     kvs = kvs + [swapped(one, "c", 2, 1) for one in kvs]
 
@@ -495,16 +497,16 @@
     wkeep, wsend = call(
         middle_kernel, "middle_dwo", [wkeep, wgot], [shape((256, FEATS), F32), shape((256, FEATS))]
     )
+    wsend, outs[1], outs[3] = lax.optimization_barrier((wsend, outs[1], outs[3]))
+    landed = [swapped(dk_send, "zr", 4, 1), swapped(dv_send, "zr", 4, 3), swapped(dq_send, "x", 4, 1)]
+    landed += [by_core(wsend, "x", 0), shifted(outs[1], "head", NH, 1), shifted(outs[3], "head", NH, 3)]
+    dk_got, dv_got, dq_got, wgot, out_one, out_three = lax.optimization_barrier(landed)
     wkeep, wsend = call(
         ring_kernel,
         "ring",
-        [wkeep, by_core(wsend, "x", 0)],
+        [wkeep, wgot],
         [shape((128, FEATS), F32), shape((128, FEATS))],
     )
-    wsend, outs[1], outs[3] = lax.optimization_barrier((wsend, outs[1], outs[3]))
-    landed = [swapped(dk_send, "zr", 4, 1), swapped(dv_send, "zr", 4, 3), swapped(dq_send, "x", 4, 1), wsend]
-    landed += [shifted(outs[1], "head", NH, 1), shifted(outs[3], "head", NH, 3)]
-    dk_got, dv_got, dq_got, wsend, out_one, out_three = lax.optimization_barrier(landed)
     dk, dk_send, dv, dv_send, dq, dq_send = call(
         middle_kernel,
         "middle",

time: 106 us -> 104 us (0.981)
  starting transfers between devices: 61.1 us -> 58.4 us
  waiting for transfers between devices: 20 us -> 21.3 us
    ppermute x29, starting transfers between devices: 51.1 us -> 46.8 us  [swapped(): return lax.ppermute(value, axis, [(i, i ^ mask) for i in range(size)])]
    ppermute x6, waiting for transfers between devices: 0.02 us -> 3.91 us  [shifted(): lax.ppermute(value, axis, [(i, (i + by) % size) for i in range(size)])]
    ppermute x2, waiting for transfers between devices: 1.75 us -> 0.17 us  [by_core(): lax.ppermute(value, (axis, 'c'), [(i, (i // 2 ^ masks[i % 2]) * 2 + i % 2...]
    ppermute x2, starting transfers between devices: 1.73 us -> 2.94 us  [by_core(): lax.ppermute(value, (axis, 'c'), [(i, (i // 2 ^ masks[i % 2]) * 2 + i % 2...]
  transfers between devices with their start and end apart: 37 -> 37, of which waited for: 15 -> 14; matrix products, arithmetic and copies ran while one was open for 1% -> 1% of each run, Pallas kernels for 14% -> 15%
where the time goes in v2:
time: 104 us; the launch traced here: 103 us
  starting transfers between devices  58.4 us (56%)
  waiting for transfers between devices  21.3 us (20%)
  Pallas kernels  19.4 us (19%)
  other arithmetic  2.72 us (3%)
    ppermute x29, starting transfers between devices, swapped(): return lax.ppermute(value, axis, [(i, i ^ mask) for i in range(size)])  46.8 us
    pallas_call x17, Pallas kernels, call(): pl.pallas_call(kernel, in_specs=[SMEM] * scalars + [VMEM] * (len(ins) - s...  19.4 us
    ppermute x29, waiting for transfers between devices, swapped(): return lax.ppermute(value, axis, [(i, i ^ mask) for i in range(size)])  17.2 us
    ppermute x6, starting transfers between devices, shifted(): lax.ppermute(value, axis, [(i, (i + by) % size) for i in range(size)])  8.69 us
    ppermute x6, waiting for transfers between devices, shifted(): lax.ppermute(value, axis, [(i, (i + by) % size) for i in range(size)])  3.91 us
    ppermute x2, starting transfers between devices, by_core(): lax.ppermute(value, (axis, 'c'), [(i, (i // 2 ^ masks[i % 2]) * 2 + i % 2...  2.94 us
  transfers between devices with their start and end apart: 37, of which 14 were waited for; matrix products, arithmetic and copies ran while one was open for 1% of the time, Pallas kernels for 15%

profile of v2, /device:TPU:8, one launch (start us, length us, event | category | flops | bytes accessed | tf_op | source)
XLA Modules:
  0.0 103.1 jit_solution(8887557684124332348)
XLA Ops:
  0.6 0.8 convert_bitcast_fusion.ids_ref.refs_5_
  1.4 1.0 %pad_maximum_fusion.1.all_ref = bf16[136,1280]{1,0:T(8,128)(2,1)S(1)} fusion(bf16[136,512]{1,0:T(8,128)(2,1)} %param.11, bf16[136,256]{1,0:T(8,128)(2,1)} %param.8, bf16[136,256]{1,0:T(8,128)(2,1)} %param.7, bf16[136,256]{1,0:T(8,128)(2,1)} %param.6), kind=kLoop, calls=%fused_computation.1 | loop fusion | flops 1392640 | bytes 696320 | tf_op jit(solution)/shard_map/concatenate | solution.py:403
  2.6 0.6 pack.1
  3.2 2.0 %collective-permute-start = (bf16[432,128]{1,0:T(8,128)(2,1)S(1)}, bf16[432,128]{1,0:T(8,128)(2,1)S(1)}, u32[]{:S(2)}, u32[]{:S(2)}) collective-permute-start(bf16[432,128]{1,0:T(8,128)(2,1)S(1)} %get-tuple-element.104), channel_id=1, source_target_pairs={{0,32},{32,0},{1,33},{33,1},{2,34},{34,2},{3,35},{35,3},{4,36},{36... | collective-permute-start | bytes 331784 | tf_op jit(solution)/shard_map/ppermute | solution.py:382
  5.2 0.4 collective-permute-start.5
  5.6 1.6 %collective-permute-start.3 = (bf16[136,512]{1,0:T(8,128)(2,1)S(1)}, bf16[136,512]{1,0:T(8,128)(2,1)S(1)}, u32[]{:S(2)}, u32[]{:S(2)}) collective-permute-start(bf16[136,512]{1,0:T(8,128)(2,1)S(1)} %get-tuple-element.112.refs_0_.dy0_ref), channel_id=1, source_target_pairs={{0,1},{1,2},{2,3},{3,0},{4,5},{5,6},{6,7},{7,4},{8,9},{9,10},{10,1... | collective-permute-start | bytes 417800 | tf_op jit(solution)/shard_map/ppermute | solution.py:378
  7.3 0.1 pad_maximum_fusion.refs_4_.wo_ref
  7.5 0.8 collective-permute-done
  8.3 3.4 %collective-permute-start.1 = (bf16[288,128]{1,0:T(8,128)(2,1)S(1)}, bf16[288,128]{1,0:T(8,128)(2,1)S(1)}, u32[]{:S(2)}, u32[]{:S(2)}) collective-permute-start(bf16[288,128]{1,0:T(8,128)(2,1)S(1)} %pad_maximum_fusion.4), channel_id=1, source_target_pairs={{0,64},{64,0},{128,192},{192,128},{1,65},{65,1},{129,193},{193,129... | collective-permute-start | bytes 221192 | tf_op jit(solution)/shard_map/ppermute | solution.py:382
  11.6 4.3 %collective-permute-start.2 = (bf16[288,128]{1,0:T(8,128)(2,1)S(1)}, bf16[288,128]{1,0:T(8,128)(2,1)S(1)}, u32[]{:S(2)}, u32[]{:S(2)}) collective-permute-start(bf16[288,128]{1,0:T(8,128)(2,1)S(1)} %pad_maximum_fusion.5), channel_id=1, source_target_pairs={{0,192},{64,128},{128,64},{192,0},{1,193},{65,129},{129,65},{193,1... | collective-permute-start | bytes 221192 | tf_op jit(solution)/shard_map/ppermute | solution.py:382
  15.9 2.8 %collective-permute-start.7 = (bf16[288,128]{1,0:T(8,128)(2,1)S(1)}, bf16[288,128]{1,0:T(8,128)(2,1)S(1)}, u32[]{:S(2)}, u32[]{:S(2)}) collective-permute-start(bf16[288,128]{1,0:T(8,128)(2,1)S(1)} %pad_maximum_fusion.6.refs_0_), channel_id=1, source_target_pairs={{0,24},{8,16},{16,8},{24,0},{1,25},{9,17},{17,9},{25,1},{2,26},{10... | collective-permute-start | bytes 221192 | tf_op jit(solution)/shard_map/ppermute | solution.py:382
  18.7 2.3 %collective-permute-start.4 = (bf16[136,512]{1,0:T(8,128)(2,1)S(1)}, bf16[136,512]{1,0:T(8,128)(2,1)S(1)}, u32[]{:S(2)}, u32[]{:S(2)}) collective-permute-start(bf16[136,512]{1,0:T(8,128)(2,1)S(1)} %get-tuple-element.112.refs_0_.dy0_ref), channel_id=1, source_target_pairs={{0,2},{1,3},{2,0},{3,1},{4,6},{5,7},{6,4},{7,5},{8,10},{9,11},{10,... | collective-permute-start | bytes 417800 | tf_op jit(solution)/shard_map/ppermute | solution.py:378
  21.0 0.3 collective-permute-start.6
  21.4 3.9 %collective-permute-done.4.refs_2_.dy2_ref = bf16[136,512]{1,0:T(8,128)(2,1)S(1)} collective-permute-done((bf16[136,512]{1,0:T(8,128)(2,1)S(1)}, bf16[136,512]{1,0:T(8,128)(2,1)S(1)}, u32[]{:S(2)}, u32[]{:S(2)}) %collective-permute-start.4) | collective-permute-done | bytes 139296 | tf_op jit(solution)/shard_map/ppermute | solution.py:378
  25.3 1.1 %collective-permute-start.8 = (bf16[576,128]{1,0:T(8,128)(2,1)S(1)}, bf16[576,128]{1,0:T(8,128)(2,1)S(1)}, u32[]{:S(2)}, u32[]{:S(2)}) collective-permute-start(bf16[576,128]{1,0:T(8,128)(2,1)S(1)} %pad_maximum_fusion.2), channel_id=1, source_target_pairs={{0,192},{64,128},{128,64},{192,0},{1,193},{65,129},{129,65},{193,1... | collective-permute-start | bytes 442376 | tf_op jit(solution)/shard_map/ppermute | solution.py:382
  26.4 2.1 %collective-permute-start.9 = (bf16[576,128]{1,0:T(8,128)(2,1)S(1)}, bf16[576,128]{1,0:T(8,128)(2,1)S(1)}, u32[]{:S(2)}, u32[]{:S(2)}) collective-permute-start(bf16[576,128]{1,0:T(8,128)(2,1)S(1)} %pad_maximum_fusion.3), channel_id=1, source_target_pairs={{0,64},{64,0},{128,192},{192,128},{1,65},{65,1},{129,193},{193,129... | collective-permute-start | bytes 442376 | tf_op jit(solution)/shard_map/ppermute | solution.py:382
  28.6 1.0 dattn.1
  29.6 0.4 collective-permute-start.10
  30.0 3.0 %collective-permute-start.11 = (bf16[288,128]{1,0:T(8,128)(2,1)S(1)}, bf16[288,128]{1,0:T(8,128)(2,1)S(1)}, u32[]{:S(2)}, u32[]{:S(2)}) collective-permute-start(bf16[288,128]{1,0:T(8,128)(2,1)S(1)} %pad_maximum_fusion.6.refs_0_), channel_id=1, source_target_pairs={{0,16},{8,24},{16,0},{24,8},{1,17},{9,25},{17,1},{25,9},{2,18},{10... | collective-permute-start | bytes 221192 | tf_op jit(solution)/shard_map/ppermute | solution.py:382
  33.2 0.5 collective-permute-done.10
  33.6 2.2 %collective-permute-done.11.refs_2_ = bf16[288,128]{1,0:T(8,128)(2,1)S(1)} collective-permute-done((bf16[288,128]{1,0:T(8,128)(2,1)S(1)}, bf16[288,128]{1,0:T(8,128)(2,1)S(1)}, u32[]{:S(2)}, u32[]{:S(2)}) %collective-permute-start.11) | collective-permute-done | bytes 73760 | tf_op jit(solution)/shard_map/ppermute | solution.py:382
  36.1 2.8 %collective-permute-start.14 = (bf16[288,128]{1,0:T(8,128)(2,1)S(1)}, bf16[288,128]{1,0:T(8,128)(2,1)S(1)}, u32[]{:S(2)}, u32[]{:S(2)}) collective-permute-start(bf16[288,128]{1,0:T(8,128)(2,1)S(1)} %constant_dynamic-update-slice_fusion.refs_0_), channel_id=1, source_target_pairs={{0,24},{8,16},{16,8},{24,0},{1,25},{9,17},{17,9},{25,1},{2,26},{10... | collective-permute-start | bytes 221192 | tf_op jit(solution)/shard_map/ppermute | solution.py:382
  38.9 0.8 collective-permute-start.13
  39.7 0.5 collective-permute-start.12
  40.2 5.0 %forward.1 = (f32[1152,128]{1,0:T(8,128)S(1)}, f32[8,1152]{1,0:T(8,128)S(1)}, bf16[1152,128]{1,0:T(8,128)(2,1)S(1)}, bf16[1152,128]{1,0:T(8,128)(2,1)S(1)}, bf16...) custom-call(bf16[288,128]{1,0:T(8,128)(2,1)S(1)} %pad_maximum_fusion.6.refs_0_, ...), custom_call_target="tpu_custom_call" | custom-call | flops 2038431744 | bytes 1048576 | tf_op jit(solution)/shard_map/forward/pallas_call | solution.py:47
  45.3 0.3 collective-permute-done.13.refs_2_
  45.5 0.4 share.1
  45.9 1.3 %collective-permute-start.17 = (bf16[368,128]{1,0:T(8,128)(2,1)S(1)}, bf16[368,128]{1,0:T(8,128)(2,1)S(1)}, u32[]{:S(2)}, u32[]{:S(2)}) collective-permute-start(bf16[368,128]{1,0:T(8,128)(2,1)S(1)} %get-tuple-element.132), channel_id=1, source_target_pairs={{0,8},{8,0},{16,24},{24,16},{1,9},{9,1},{17,25},{25,17},{2,10},{10... | collective-permute-start | bytes 282632 | tf_op jit(solution)/shard_map/ppermute | solution.py:382
  47.3 2.7 %collective-permute-start.18 = (bf16[368,128]{1,0:T(8,128)(2,1)S(1)}, bf16[368,128]{1,0:T(8,128)(2,1)S(1)}, u32[]{:S(2)}, u32[]{:S(2)}) collective-permute-start(bf16[368,128]{1,0:T(8,128)(2,1)S(1)} %get-tuple-element.133), channel_id=1, source_target_pairs={{0,16},{8,24},{16,0},{24,8},{1,17},{9,25},{17,1},{25,9},{2,18},{10... | collective-permute-start | bytes 282632 | tf_op jit(solution)/shard_map/ppermute | solution.py:382
  50.0 0.7 collective-permute-start.19
  50.7 0.4 collective-permute-done.17.l1_ref
  51.1 3.3 %collective-permute-done.18.l2_ref = bf16[368,128]{1,0:T(8,128)(2,1)S(1)} collective-permute-done((bf16[368,128]{1,0:T(8,128)(2,1)S(1)}, bf16[368,128]{1,0:T(8,128)(2,1)S(1)}, u32[]{:S(2)}, u32[]{:S(2)}) %collective-permute-start.18) | collective-permute-done | bytes 94240 | tf_op jit(solution)/shard_map/ppermute | solution.py:382
  54.4 1.6 %collective-permute-done.19.l3_ref = bf16[368,128]{1,0:T(8,128)(2,1)S(1)} collective-permute-done((bf16[368,128]{1,0:T(8,128)(2,1)S(1)}, bf16[368,128]{1,0:T(8,128)(2,1)S(1)}, u32[]{:S(2)}, u32[]{:S(2)}) %collective-permute-start.19) | collective-permute-done | bytes 94240 | tf_op jit(solution)/shard_map/ppermute | solution.py:382
  55.9 0.9 merge.1
  56.8 1.8 %collective-permute-start.20 = (bf16[144,128]{1,0:T(8,128)(2,1)S(1)}, bf16[144,128]{1,0:T(8,128)(2,1)S(1)}, u32[]{:S(2)}, u32[]{:S(2)}) collective-permute-start(bf16[144,128]{1,0:T(8,128)(2,1)S(1)} %get-tuple-element.136), channel_id=1, source_target_pairs={{0,32},{32,0},{1,33},{33,1},{2,34},{34,2},{3,35},{35,3},{4,36},{36... | collective-permute-start | bytes 110600 | tf_op jit(solution)/shard_map/ppermute | solution.py:382
  58.6 2.8 %backward_one.1 = (bf16[768,256]{1,0:T(8,128)(2,1)S(1)}, f32[1152,128]{1,0:T(8,128)S(1)}) custom-call(bf16[1152,128]{1,0:T(8,128)(2,1)S(1)} %get-tuple-element.138.q_ref, bf16[1152,128]{1,0:T(8,128)(2,1)S(1)} %get-tuple-element.139.qm_ref, bf16[1152,128]{1,0:T(8,128)(2,1)S(1)} %get-tuple-element.140.da_ref, bf16[2304,256]{1,0:T(8,128)(2,1)S(1)} %get-tuple-element.141.kv_ref, ...), custom_call_target="tpu_custom_call" | custom-call | flops 1358954496 | bytes 1048576 | tf_op jit(solution)/shard_map/backward_one/pallas_call | solution.py:47
  61.4 1.2 %project.1 = (bf16[136,512]{1,0:T(8,128)(2,1)S(1)}, bf16[136,512]{1,0:T(8,128)(2,1)S(1)}, bf16[136,512]{1,0:T(8,128)(2,1)S(1)}, bf16[136,512]{1,0:T(8,128)(2,1)S...) custom-call(s32[5]{0:T(128)S(1)} %stack.23.at_ref, ...), custom_call_target="tpu_custom_call" | custom-call | tf_op jit(solution)/shard_map/project/pallas_call | solution.py:47
  62.7 0.3 collective-permute-start.21
  63.0 1.6 %backward_two.1 = (bf16[8,288,128]{2,1,0:T(8,128)(2,1)S(1)}, f32[1152,128]{1,0:T(8,128)S(1)}) custom-call(bf16[1152,128]{1,0:T(8,128)(2,1)S(1)} %get-tuple-element.138.q_ref, bf16[1152,128]{1,0:T(8,128)(2,1)S(1)} %get-tuple-element.139.qm_ref, bf16[1152,128]{1,0:T(8,128)(2,1)S(1)} %get-tuple-element.140.da_ref, ...), custom_call_target="tpu_custom_call" | custom-call | flops 679477248 | bytes 1048576 | tf_op jit(solution)/shard_map/backward_two/pallas_call | solution.py:47
  64.6 0.6 collective-permute-start.23
  65.1 0.1 dwo.1
  65.3 1.3 %collective-permute-start.22 = (bf16[512,256]{1,0:T(8,128)(2,1)S(1)}, bf16[512,256]{1,0:T(8,128)(2,1)S(1)}, u32[]{:S(2)}, u32[]{:S(2)}) collective-permute-start(bf16[512,256]{1,0:T(8,128)(2,1)S(1)} %get-tuple-element.157), channel_id=1, source_target_pairs={{0,24},{4,12},{8,16},{12,4},{16,8},{20,28},{24,0},{28,20},{1,25},{... | collective-permute-start | bytes 786440 | tf_op jit(solution)/shard_map/ppermute | solution.py:387
  66.5 4.1 %backward_three.1 = (bf16[8,288,128]{2,1,0:T(8,128)(2,1)S(1)}, f32[576,128]{1,0:T(8,128)S(1)}, bf16[576,128]{1,0:T(8,128)(2,1)S(1)}) custom-call(bf16[1152,128]{1,0:T(8,128)(2,1)S(1)} %get-tuple-element.138.q_ref, bf16[1152,128]{1,0:T(8,128)(2,1)S(1)} %get-tuple-element.139.qm_ref, bf16[1152,128]{1,0:T(8,128)(2,1)S(1)} %get-tuple-element.140.da_ref, ...), custom_call_target="tpu_custom_call" | custom-call | flops 2038431744 | bytes 1048576 | tf_op jit(solution)/shard_map/backward_three/pallas_call | solution.py:47
  70.7 0.2 core.1
  70.9 1.9 %collective-permute-start.25 = (bf16[576,128]{1,0:T(8,128)(2,1)S(1)}, bf16[576,128]{1,0:T(8,128)(2,1)S(1)}, u32[]{:S(2)}, u32[]{:S(2)}) collective-permute-start(bf16[576,128]{1,0:T(8,128)(2,1)S(1)} %get-tuple-element.163), channel_id=1, source_target_pairs={{0,192},{64,128},{128,64},{192,0},{1,193},{65,129},{129,65},{193,1... | collective-permute-start | bytes 442376 | tf_op jit(solution)/shard_map/ppermute | solution.py:382
  72.8 0.2 collective-permute-done.22.refs_1_
  72.9 1.6 %collective-permute-start.24 = (bf16[576,128]{1,0:T(8,128)(2,1)S(1)}, bf16[576,128]{1,0:T(8,128)(2,1)S(1)}, u32[]{:S(2)}, u32[]{:S(2)}) collective-permute-start(bf16[576,128]{1,0:T(8,128)(2,1)S(1)} %get-tuple-element.162), channel_id=1, source_target_pairs={{0,64},{64,0},{128,192},{192,128},{1,65},{65,1},{129,193},{193,129... | collective-permute-start | bytes 442376 | tf_op jit(solution)/shard_map/ppermute | solution.py:382
  74.6 1.6 %collective-permute-start.28 = (bf16[136,512]{1,0:T(8,128)(2,1)S(1)}, bf16[136,512]{1,0:T(8,128)(2,1)S(1)}, u32[]{:S(2)}, u32[]{:S(2)}) collective-permute-start(bf16[136,512]{1,0:T(8,128)(2,1)S(1)} %get-tuple-element.171), channel_id=1, source_target_pairs={{0,1},{1,2},{2,3},{3,0},{4,5},{5,6},{6,7},{7,4},{8,9},{9,10},{10,1... | collective-permute-start | bytes 417800 | tf_op jit(solution)/shard_map/ppermute | solution.py:378
  76.2 0.5 collective-permute-start.29
  76.7 1.7 %collective-permute-start.27 = (bf16[256,256]{1,0:T(8,128)(2,1)S(1)}, bf16[256,256]{1,0:T(8,128)(2,1)S(1)}, u32[]{:S(2)}, u32[]{:S(2)}) collective-permute-start(bf16[256,256]{1,0:T(8,128)(2,1)S(1)} %get-tuple-element.170), channel_id=1, source_target_pairs={{0,8},{4,28},{8,0},{12,20},{16,24},{20,12},{24,16},{28,4},{1,9},{5... | collective-permute-start | bytes 393224 | tf_op jit(solution)/shard_map/ppermute | solution.py:387
  78.4 1.7 %collective-permute-done.25.refs_3_ = bf16[576,128]{1,0:T(8,128)(2,1)S(1)} collective-permute-done((bf16[576,128]{1,0:T(8,128)(2,1)S(1)}, bf16[576,128]{1,0:T(8,128)(2,1)S(1)}, u32[]{:S(2)}, u32[]{:S(2)}) %collective-permute-start.25) | collective-permute-done | bytes 147488 | tf_op jit(solution)/shard_map/ppermute | solution.py:382
  80.1 2.3 %collective-permute-start.30 = (bf16[136,512]{1,0:T(8,128)(2,1)S(1)}, bf16[136,512]{1,0:T(8,128)(2,1)S(1)}, u32[]{:S(2)}, u32[]{:S(2)}) collective-permute-start(bf16[136,512]{1,0:T(8,128)(2,1)S(1)} %get-tuple-element.174), channel_id=1, source_target_pairs={{0,2},{1,3},{2,0},{3,1},{4,6},{5,7},{6,4},{7,5},{8,10},{9,11},{10,... | collective-permute-start | bytes 417800 | tf_op jit(solution)/shard_map/ppermute | solution.py:378
  82.4 3.3 %collective-permute-start.34 = (bf16[128,256]{1,0:T(8,128)(2,1)S(1)}, bf16[128,256]{1,0:T(8,128)(2,1)S(1)}, u32[]{:S(2)}, u32[]{:S(2)}) collective-permute-start(bf16[128,256]{1,0:T(8,128)(2,1)S(1)} %get-tuple-element.191), channel_id=1, source_target_pairs={{0,192},{64,128},{128,64},{192,0},{1,193},{65,129},{129,65},{193,1... | collective-permute-start | bytes 196616 | tf_op jit(solution)/shard_map/ppermute | solution.py:382
  85.7 2.2 %collective-permute-start.31 = (bf16[288,128]{1,0:T(8,128)(2,1)S(1)}, bf16[288,128]{1,0:T(8,128)(2,1)S(1)}, u32[]{:S(2)}, u32[]{:S(2)}) collective-permute-start(bf16[288,128]{1,0:T(8,128)(2,1)S(1)} %get-tuple-element.183), channel_id=1, source_target_pairs={{0,24},{8,16},{16,8},{24,0},{1,25},{9,17},{17,9},{25,1},{2,26},{10... | collective-permute-start | bytes 221192 | tf_op jit(solution)/shard_map/ppermute | solution.py:382
  88.0 0.2 collective-permute-start.32
  88.2 3.7 %collective-permute-start.33 = (bf16[288,128]{1,0:T(8,128)(2,1)S(1)}, bf16[288,128]{1,0:T(8,128)(2,1)S(1)}, u32[]{:S(2)}, u32[]{:S(2)}) collective-permute-start(bf16[288,128]{1,0:T(8,128)(2,1)S(1)} %get-tuple-element.187), channel_id=1, source_target_pairs={{0,64},{64,0},{128,192},{192,128},{1,65},{65,1},{129,193},{193,129... | collective-permute-start | bytes 221192 | tf_op jit(solution)/shard_map/ppermute | solution.py:382
  91.9 1.5 %collective-permute-start.35 = (bf16[64,256]{1,0:T(8,128)(2,1)S(1)}, bf16[64,256]{1,0:T(8,128)(2,1)S(1)}, u32[]{:S(2)}, u32[]{:S(2)}) collective-permute-start(bf16[64,256]{1,0:T(8,128)(2,1)S(1)} %get-tuple-element.193), channel_id=1, source_target_pairs={{0,64},{64,0},{128,192},{192,128},{1,65},{65,1},{129,193},{193,129... | collective-permute-start | bytes 98312 | tf_op jit(solution)/shard_map/ppermute | solution.py:382
  93.4 1.4 %collective-permute-done.32.refs_3_ = bf16[288,128]{1,0:T(8,128)(2,1)S(1)} collective-permute-done((bf16[288,128]{1,0:T(8,128)(2,1)S(1)}, bf16[288,128]{1,0:T(8,128)(2,1)S(1)}, u32[]{:S(2)}, u32[]{:S(2)}) %collective-permute-start.32) | collective-permute-done | bytes 73760 | tf_op jit(solution)/shard_map/ppermute | solution.py:382
  94.8 0.3 collective-permute-done.33.refs_5_
  95.1 1.7 %collective-permute-done.35.refs_7_ = bf16[64,256]{1,0:T(8,128)(2,1)S(1)} collective-permute-done((bf16[64,256]{1,0:T(8,128)(2,1)S(1)}, bf16[64,256]{1,0:T(8,128)(2,1)S(1)}, u32[]{:S(2)}, u32[]{:S(2)}) %collective-permute-start.35) | collective-permute-done | bytes 32800 | tf_op jit(solution)/shard_map/ppermute | solution.py:382
  96.8 1.1 %collective-permute-start.36 = (bf16[496,128]{1,0:T(8,128)(2,1)S(1)}, bf16[496,128]{1,0:T(8,128)(2,1)S(1)}, u32[]{:S(2)}, u32[]{:S(2)}) collective-permute-start(bf16[496,128]{1,0:T(8,128)(2,1)S(1)} %get-tuple-element.196), channel_id=1, source_target_pairs={{0,32},{32,0},{1,33},{33,1},{2,34},{34,2},{3,35},{35,3},{4,36},{36... | collective-permute-start | bytes 380936 | tf_op jit(solution)/shard_map/ppermute | solution.py:382
  97.9 0.7 add_convert_fusion
  98.6 3.2 %collective-permute-done.36.got_ref = bf16[496,128]{1,0:T(8,128)(2,1)S(1)} collective-permute-done((bf16[496,128]{1,0:T(8,128)(2,1)S(1)}, bf16[496,128]{1,0:T(8,128)(2,1)S(1)}, u32[]{:S(2)}, u32[]{:S(2)}) %collective-permute-start.36) | collective-permute-done | bytes 127008 | tf_op jit(solution)/shard_map/ppermute | solution.py:382
  101.8 1.3 %place.1 = (bf16[136,256]{1,0:T(8,128)(2,1)}, bf16[136,256]{1,0:T(8,128)(2,1)}, bf16[136,256]{1,0:T(8,128)(2,1)}, f32[32,256]{1,0:T(8,128)}) custom-call(s32[5]{0:T(128)S(1)} %stack.23.at_ref, bf16[144,384]{1,0:T(8,128)(2,1)S(1)} %get-tuple-element.194.mine_ref, f32[32,256]{1,0:T(8,128)S(1)} %get-tuple-element.195.wmine_ref, ...), custom_call_target="tpu_custom_call" | custom-call | tf_op jit(solution)/shard_map/place/pallas_call | solution.py:47
  (48 shorter events, 0.9 us)
Async XLA Ops:
  0.6 6.6 %copy-start = (bf16[256,2048]{1,0:T(8,128)(2,1)S(1)}, bf16[256,2048]{1,0:T(8,128)(2,1)}, u32[]{:S(2)}) copy-start(bf16[256,2048]{1,0:T(8,128)(2,1)} %param.10) | copy-start | bytes 3145732
  3.2 5.1 %collective-permute-start = (bf16[432,128]{1,0:T(8,128)(2,1)S(1)}, bf16[432,128]{1,0:T(8,128)(2,1)S(1)}, u32[]{:S(2)}, u32[]{:S(2)}) collective-permute-start(bf16[432,128]{1,0:T(8,128)(2,1)S(1)} %get-tuple-element.104), channel_id=1, source_target_pairs={{0,32},{32,0},{1,33},{33,1},{2,34},{34,2},{3,35},{35,3},{4,36},{36... | collective-permute-start | bytes 331784 | tf_op jit(solution)/shard_map/ppermute | solution.py:382
  5.2 16.2 %collective-permute-start.5 = (bf16[136,512]{1,0:T(8,128)(2,1)S(1)}, bf16[136,512]{1,0:T(8,128)(2,1)S(1)}, u32[]{:S(2)}, u32[]{:S(2)}) collective-permute-start(bf16[136,512]{1,0:T(8,128)(2,1)S(1)} %get-tuple-element.112.refs_0_.dy0_ref), channel_id=1, source_target_pairs={{0,3},{1,0},{2,1},{3,2},{4,7},{5,4},{6,5},{7,6},{8,11},{9,8},{10,9... | collective-permute-start | bytes 417800 | tf_op jit(solution)/shard_map/ppermute | solution.py:378
  5.6 15.7 %collective-permute-start.3 = (bf16[136,512]{1,0:T(8,128)(2,1)S(1)}, bf16[136,512]{1,0:T(8,128)(2,1)S(1)}, u32[]{:S(2)}, u32[]{:S(2)}) collective-permute-start(bf16[136,512]{1,0:T(8,128)(2,1)S(1)} %get-tuple-element.112.refs_0_.dy0_ref), channel_id=1, source_target_pairs={{0,1},{1,2},{2,3},{3,0},{4,5},{5,6},{6,7},{7,4},{8,9},{9,10},{10,1... | collective-permute-start | bytes 417800 | tf_op jit(solution)/shard_map/ppermute | solution.py:378
  8.3 10.4 %collective-permute-start.1 = (bf16[288,128]{1,0:T(8,128)(2,1)S(1)}, bf16[288,128]{1,0:T(8,128)(2,1)S(1)}, u32[]{:S(2)}, u32[]{:S(2)}) collective-permute-start(bf16[288,128]{1,0:T(8,128)(2,1)S(1)} %pad_maximum_fusion.4), channel_id=1, source_target_pairs={{0,64},{64,0},{128,192},{192,128},{1,65},{65,1},{129,193},{193,129... | collective-permute-start | bytes 221192 | tf_op jit(solution)/shard_map/ppermute | solution.py:382
  11.6 9.4 %collective-permute-start.2 = (bf16[288,128]{1,0:T(8,128)(2,1)S(1)}, bf16[288,128]{1,0:T(8,128)(2,1)S(1)}, u32[]{:S(2)}, u32[]{:S(2)}) collective-permute-start(bf16[288,128]{1,0:T(8,128)(2,1)S(1)} %pad_maximum_fusion.5), channel_id=1, source_target_pairs={{0,192},{64,128},{128,64},{192,0},{1,193},{65,129},{129,65},{193,1... | collective-permute-start | bytes 221192 | tf_op jit(solution)/shard_map/ppermute | solution.py:382
  15.9 12.6 %collective-permute-start.7 = (bf16[288,128]{1,0:T(8,128)(2,1)S(1)}, bf16[288,128]{1,0:T(8,128)(2,1)S(1)}, u32[]{:S(2)}, u32[]{:S(2)}) collective-permute-start(bf16[288,128]{1,0:T(8,128)(2,1)S(1)} %pad_maximum_fusion.6.refs_0_), channel_id=1, source_target_pairs={{0,24},{8,16},{16,8},{24,0},{1,25},{9,17},{17,9},{25,1},{2,26},{10... | collective-permute-start | bytes 221192 | tf_op jit(solution)/shard_map/ppermute | solution.py:382
  18.7 6.6 %collective-permute-start.4 = (bf16[136,512]{1,0:T(8,128)(2,1)S(1)}, bf16[136,512]{1,0:T(8,128)(2,1)S(1)}, u32[]{:S(2)}, u32[]{:S(2)}) collective-permute-start(bf16[136,512]{1,0:T(8,128)(2,1)S(1)} %get-tuple-element.112.refs_0_.dy0_ref), channel_id=1, source_target_pairs={{0,2},{1,3},{2,0},{3,1},{4,6},{5,7},{6,4},{7,5},{8,10},{9,11},{10,... | collective-permute-start | bytes 417800 | tf_op jit(solution)/shard_map/ppermute | solution.py:378
  21.0 7.5 %collective-permute-start.6 = (bf16[288,128]{1,0:T(8,128)(2,1)S(1)}, bf16[288,128]{1,0:T(8,128)(2,1)S(1)}, u32[]{:S(2)}, u32[]{:S(2)}) collective-permute-start(bf16[288,128]{1,0:T(8,128)(2,1)S(1)} %pad_maximum_fusion.6.refs_0_), channel_id=1, source_target_pairs={{0,8},{8,0},{16,24},{24,16},{1,9},{9,1},{17,25},{25,17},{2,10},{10... | collective-permute-start | bytes 221192 | tf_op jit(solution)/shard_map/ppermute | solution.py:382
  25.3 10.6 %collective-permute-start.8 = (bf16[576,128]{1,0:T(8,128)(2,1)S(1)}, bf16[576,128]{1,0:T(8,128)(2,1)S(1)}, u32[]{:S(2)}, u32[]{:S(2)}) collective-permute-start(bf16[576,128]{1,0:T(8,128)(2,1)S(1)} %pad_maximum_fusion.2), channel_id=1, source_target_pairs={{0,192},{64,128},{128,64},{192,0},{1,193},{65,129},{129,65},{193,1... | collective-permute-start | bytes 442376 | tf_op jit(solution)/shard_map/ppermute | solution.py:382
  26.4 9.5 %collective-permute-start.9 = (bf16[576,128]{1,0:T(8,128)(2,1)S(1)}, bf16[576,128]{1,0:T(8,128)(2,1)S(1)}, u32[]{:S(2)}, u32[]{:S(2)}) collective-permute-start(bf16[576,128]{1,0:T(8,128)(2,1)S(1)} %pad_maximum_fusion.3), channel_id=1, source_target_pairs={{0,64},{64,0},{128,192},{192,128},{1,65},{65,1},{129,193},{193,129... | collective-permute-start | bytes 442376 | tf_op jit(solution)/shard_map/ppermute | solution.py:382
  29.6 4.0 %collective-permute-start.10 = (bf16[144,128]{1,0:T(8,128)(2,1)S(1)}, bf16[144,128]{1,0:T(8,128)(2,1)S(1)}, u32[]{:S(2)}, u32[]{:S(2)}) collective-permute-start(bf16[144,128]{1,0:T(8,128)(2,1)S(1)} %get-tuple-element.121), channel_id=1, source_target_pairs={{0,32},{32,0},{1,33},{33,1},{2,34},{34,2},{3,35},{35,3},{4,36},{36... | collective-permute-start | bytes 110600 | tf_op jit(solution)/shard_map/ppermute | solution.py:382
  30.0 5.9 %collective-permute-start.11 = (bf16[288,128]{1,0:T(8,128)(2,1)S(1)}, bf16[288,128]{1,0:T(8,128)(2,1)S(1)}, u32[]{:S(2)}, u32[]{:S(2)}) collective-permute-start(bf16[288,128]{1,0:T(8,128)(2,1)S(1)} %pad_maximum_fusion.6.refs_0_), channel_id=1, source_target_pairs={{0,16},{8,24},{16,0},{24,8},{1,17},{9,25},{17,1},{25,9},{2,18},{10... | collective-permute-start | bytes 221192 | tf_op jit(solution)/shard_map/ppermute | solution.py:382
  33.1 7.2 %collective-permute-start.15 = (bf16[1152,128]{1,0:T(8,128)(2,1)S(1)}, bf16[1152,128]{1,0:T(8,128)(2,1)S(1)}, u32[]{:S(2)}, u32[]{:S(2)}) collective-permute-start(bf16[1152,128]{1,0:T(8,128)(2,1)S(1)} %constant_dynamic-update-slice_fusion.2.refs_4_), channel_id=1, source_target_pairs={{0,4},{4,0},{1,5},{5,1},{2,6},{6,2},{3,7},{7,3},{8,12},{12,8},{9,1... | collective-permute-start | bytes 884744 | tf_op jit(solution)/shard_map/ppermute | solution.py:382
  35.9 4.3 %collective-permute-start.16 = (bf16[1152,128]{1,0:T(8,128)(2,1)S(1)}, bf16[1152,128]{1,0:T(8,128)(2,1)S(1)}, u32[]{:S(2)}, u32[]{:S(2)}) collective-permute-start(bf16[1152,128]{1,0:T(8,128)(2,1)S(1)} %constant_dynamic-update-slice_fusion.4.refs_5_), channel_id=1, source_target_pairs={{0,4},{4,0},{1,5},{5,1},{2,6},{6,2},{3,7},{7,3},{8,12},{12,8},{9,1... | collective-permute-start | bytes 884744 | tf_op jit(solution)/shard_map/ppermute | solution.py:382
  36.1 9.2 %collective-permute-start.14 = (bf16[288,128]{1,0:T(8,128)(2,1)S(1)}, bf16[288,128]{1,0:T(8,128)(2,1)S(1)}, u32[]{:S(2)}, u32[]{:S(2)}) collective-permute-start(bf16[288,128]{1,0:T(8,128)(2,1)S(1)} %constant_dynamic-update-slice_fusion.refs_0_), channel_id=1, source_target_pairs={{0,24},{8,16},{16,8},{24,0},{1,25},{9,17},{17,9},{25,1},{2,26},{10... | collective-permute-start | bytes 221192 | tf_op jit(solution)/shard_map/ppermute | solution.py:382
  38.9 6.6 %collective-permute-start.13 = (bf16[288,128]{1,0:T(8,128)(2,1)S(1)}, bf16[288,128]{1,0:T(8,128)(2,1)S(1)}, u32[]{:S(2)}, u32[]{:S(2)}) collective-permute-start(bf16[288,128]{1,0:T(8,128)(2,1)S(1)} %constant_dynamic-update-slice_fusion.refs_0_), channel_id=1, source_target_pairs={{0,16},{8,24},{16,0},{24,8},{1,17},{9,25},{17,1},{25,9},{2,18},{10... | collective-permute-start | bytes 221192 | tf_op jit(solution)/shard_map/ppermute | solution.py:382
  39.7 5.8 %collective-permute-start.12 = (bf16[288,128]{1,0:T(8,128)(2,1)S(1)}, bf16[288,128]{1,0:T(8,128)(2,1)S(1)}, u32[]{:S(2)}, u32[]{:S(2)}) collective-permute-start(bf16[288,128]{1,0:T(8,128)(2,1)S(1)} %constant_dynamic-update-slice_fusion.refs_0_), channel_id=1, source_target_pairs={{0,8},{8,0},{16,24},{24,16},{1,9},{9,1},{17,25},{25,17},{2,10},{10... | collective-permute-start | bytes 221192 | tf_op jit(solution)/shard_map/ppermute | solution.py:382
  45.9 5.2 %collective-permute-start.17 = (bf16[368,128]{1,0:T(8,128)(2,1)S(1)}, bf16[368,128]{1,0:T(8,128)(2,1)S(1)}, u32[]{:S(2)}, u32[]{:S(2)}) collective-permute-start(bf16[368,128]{1,0:T(8,128)(2,1)S(1)} %get-tuple-element.132), channel_id=1, source_target_pairs={{0,8},{8,0},{16,24},{24,16},{1,9},{9,1},{17,25},{25,17},{2,10},{10... | collective-permute-start | bytes 282632 | tf_op jit(solution)/shard_map/ppermute | solution.py:382
  47.3 7.1 %collective-permute-start.18 = (bf16[368,128]{1,0:T(8,128)(2,1)S(1)}, bf16[368,128]{1,0:T(8,128)(2,1)S(1)}, u32[]{:S(2)}, u32[]{:S(2)}) collective-permute-start(bf16[368,128]{1,0:T(8,128)(2,1)S(1)} %get-tuple-element.133), channel_id=1, source_target_pairs={{0,16},{8,24},{16,0},{24,8},{1,17},{9,25},{17,1},{25,9},{2,18},{10... | collective-permute-start | bytes 282632 | tf_op jit(solution)/shard_map/ppermute | solution.py:382
  50.0 5.9 %collective-permute-start.19 = (bf16[368,128]{1,0:T(8,128)(2,1)S(1)}, bf16[368,128]{1,0:T(8,128)(2,1)S(1)}, u32[]{:S(2)}, u32[]{:S(2)}) collective-permute-start(bf16[368,128]{1,0:T(8,128)(2,1)S(1)} %get-tuple-element.134), channel_id=1, source_target_pairs={{0,24},{8,16},{16,8},{24,0},{1,25},{9,17},{17,9},{25,1},{2,26},{10... | collective-permute-start | bytes 282632 | tf_op jit(solution)/shard_map/ppermute | solution.py:382
  56.8 4.6 %collective-permute-start.20 = (bf16[144,128]{1,0:T(8,128)(2,1)S(1)}, bf16[144,128]{1,0:T(8,128)(2,1)S(1)}, u32[]{:S(2)}, u32[]{:S(2)}) collective-permute-start(bf16[144,128]{1,0:T(8,128)(2,1)S(1)} %get-tuple-element.136), channel_id=1, source_target_pairs={{0,32},{32,0},{1,33},{33,1},{2,34},{34,2},{3,35},{35,3},{4,36},{36... | collective-permute-start | bytes 110600 | tf_op jit(solution)/shard_map/ppermute | solution.py:382
  62.7 2.5 %collective-permute-start.21 = (bf16[4,256,256]{2,1,0:T(8,128)(2,1)S(1)}, bf16[4,256,256]{2,1,0:T(8,128)(2,1)S(1)}, u32[]{:S(2)}, u32[]{:S(2)}) collective-permute-start(bf16[4,256,256]{2,1,0:T(8,128)(2,1)S(1)} %get-tuple-element.150), channel_id=1, source_target_pairs={{0,4},{4,0},{1,5},{5,1},{2,6},{6,2},{3,7},{7,3},{8,12},{12,8},{9,1... | collective-permute-start | bytes 1572872 | tf_op jit(solution)/shard_map/ppermute | solution.py:382
  64.6 6.2 %collective-permute-start.23 = (bf16[8,288,128]{2,1,0:T(8,128)(2,1)S(1)}, bf16[8,288,128]{2,1,0:T(8,128)(2,1)S(1)}, u32[]{:S(2)}, u32[]{:S(2)}) collective-permute-start(bf16[8,288,128]{2,1,0:T(8,128)(2,1)S(1)} %get-tuple-element.160), channel_id=1, source_target_pairs={{0,4},{4,0},{1,5},{5,1},{2,6},{6,2},{3,7},{7,3},{8,12},{12,8},{9,1... | collective-permute-start | bytes 1769480 | tf_op jit(solution)/shard_map/ppermute | solution.py:382
  65.3 7.7 %collective-permute-start.22 = (bf16[512,256]{1,0:T(8,128)(2,1)S(1)}, bf16[512,256]{1,0:T(8,128)(2,1)S(1)}, u32[]{:S(2)}, u32[]{:S(2)}) collective-permute-start(bf16[512,256]{1,0:T(8,128)(2,1)S(1)} %get-tuple-element.157), channel_id=1, source_target_pairs={{0,24},{4,12},{8,16},{12,4},{16,8},{20,28},{24,0},{28,20},{1,25},{... | collective-permute-start | bytes 786440 | tf_op jit(solution)/shard_map/ppermute | solution.py:387
  70.6 6.1 %collective-permute-start.26 = (bf16[576,128]{1,0:T(8,128)(2,1)S(1)}, bf16[576,128]{1,0:T(8,128)(2,1)S(1)}, u32[]{:S(2)}, u32[]{:S(2)}) collective-permute-start(bf16[576,128]{1,0:T(8,128)(2,1)S(1)} %get-tuple-element.164), channel_id=1, source_target_pairs={{0,8},{8,0},{16,24},{24,16},{1,9},{9,1},{17,25},{25,17},{2,10},{10... | collective-permute-start | bytes 442376 | tf_op jit(solution)/shard_map/ppermute | solution.py:382
  70.9 9.2 %collective-permute-start.25 = (bf16[576,128]{1,0:T(8,128)(2,1)S(1)}, bf16[576,128]{1,0:T(8,128)(2,1)S(1)}, u32[]{:S(2)}, u32[]{:S(2)}) collective-permute-start(bf16[576,128]{1,0:T(8,128)(2,1)S(1)} %get-tuple-element.163), channel_id=1, source_target_pairs={{0,192},{64,128},{128,64},{192,0},{1,193},{65,129},{129,65},{193,1... | collective-permute-start | bytes 442376 | tf_op jit(solution)/shard_map/ppermute | solution.py:382
  72.9 9.4 %collective-permute-start.24 = (bf16[576,128]{1,0:T(8,128)(2,1)S(1)}, bf16[576,128]{1,0:T(8,128)(2,1)S(1)}, u32[]{:S(2)}, u32[]{:S(2)}) collective-permute-start(bf16[576,128]{1,0:T(8,128)(2,1)S(1)} %get-tuple-element.162), channel_id=1, source_target_pairs={{0,64},{64,0},{128,192},{192,128},{1,65},{65,1},{129,193},{193,129... | collective-permute-start | bytes 442376 | tf_op jit(solution)/shard_map/ppermute | solution.py:382
  74.6 7.7 %collective-permute-start.28 = (bf16[136,512]{1,0:T(8,128)(2,1)S(1)}, bf16[136,512]{1,0:T(8,128)(2,1)S(1)}, u32[]{:S(2)}, u32[]{:S(2)}) collective-permute-start(bf16[136,512]{1,0:T(8,128)(2,1)S(1)} %get-tuple-element.171), channel_id=1, source_target_pairs={{0,1},{1,2},{2,3},{3,0},{4,5},{5,6},{6,7},{7,4},{8,9},{9,10},{10,1... | collective-permute-start | bytes 417800 | tf_op jit(solution)/shard_map/ppermute | solution.py:378
  76.2 6.1 %collective-permute-start.29 = (bf16[136,512]{1,0:T(8,128)(2,1)S(1)}, bf16[136,512]{1,0:T(8,128)(2,1)S(1)}, u32[]{:S(2)}, u32[]{:S(2)}) collective-permute-start(bf16[136,512]{1,0:T(8,128)(2,1)S(1)} %get-tuple-element.172), channel_id=1, source_target_pairs={{0,3},{1,0},{2,1},{3,2},{4,7},{5,4},{6,5},{7,6},{8,11},{9,8},{10,9... | collective-permute-start | bytes 417800 | tf_op jit(solution)/shard_map/ppermute | solution.py:378
  76.7 5.6 %collective-permute-start.27 = (bf16[256,256]{1,0:T(8,128)(2,1)S(1)}, bf16[256,256]{1,0:T(8,128)(2,1)S(1)}, u32[]{:S(2)}, u32[]{:S(2)}) collective-permute-start(bf16[256,256]{1,0:T(8,128)(2,1)S(1)} %get-tuple-element.170), channel_id=1, source_target_pairs={{0,8},{4,28},{8,0},{12,20},{16,24},{20,12},{24,16},{28,4},{1,9},{5... | collective-permute-start | bytes 393224 | tf_op jit(solution)/shard_map/ppermute | solution.py:387
  80.1 17.8 %collective-permute-start.30 = (bf16[136,512]{1,0:T(8,128)(2,1)S(1)}, bf16[136,512]{1,0:T(8,128)(2,1)S(1)}, u32[]{:S(2)}, u32[]{:S(2)}) collective-permute-start(bf16[136,512]{1,0:T(8,128)(2,1)S(1)} %get-tuple-element.174), channel_id=1, source_target_pairs={{0,2},{1,3},{2,0},{3,1},{4,6},{5,7},{6,4},{7,5},{8,10},{9,11},{10,... | collective-permute-start | bytes 417800 | tf_op jit(solution)/shard_map/ppermute | solution.py:378
  82.4 9.5 %collective-permute-start.34 = (bf16[128,256]{1,0:T(8,128)(2,1)S(1)}, bf16[128,256]{1,0:T(8,128)(2,1)S(1)}, u32[]{:S(2)}, u32[]{:S(2)}) collective-permute-start(bf16[128,256]{1,0:T(8,128)(2,1)S(1)} %get-tuple-element.191), channel_id=1, source_target_pairs={{0,192},{64,128},{128,64},{192,0},{1,193},{65,129},{129,65},{193,1... | collective-permute-start | bytes 196616 | tf_op jit(solution)/shard_map/ppermute | solution.py:382
  85.7 7.7 %collective-permute-start.31 = (bf16[288,128]{1,0:T(8,128)(2,1)S(1)}, bf16[288,128]{1,0:T(8,128)(2,1)S(1)}, u32[]{:S(2)}, u32[]{:S(2)}) collective-permute-start(bf16[288,128]{1,0:T(8,128)(2,1)S(1)} %get-tuple-element.183), channel_id=1, source_target_pairs={{0,24},{8,16},{16,8},{24,0},{1,25},{9,17},{17,9},{25,1},{2,26},{10... | collective-permute-start | bytes 221192 | tf_op jit(solution)/shard_map/ppermute | solution.py:382
  88.0 6.9 %collective-permute-start.32 = (bf16[288,128]{1,0:T(8,128)(2,1)S(1)}, bf16[288,128]{1,0:T(8,128)(2,1)S(1)}, u32[]{:S(2)}, u32[]{:S(2)}) collective-permute-start(bf16[288,128]{1,0:T(8,128)(2,1)S(1)} %get-tuple-element.185), channel_id=1, source_target_pairs={{0,192},{64,128},{128,64},{192,0},{1,193},{65,129},{129,65},{193,1... | collective-permute-start | bytes 221192 | tf_op jit(solution)/shard_map/ppermute | solution.py:382
  88.2 6.9 %collective-permute-start.33 = (bf16[288,128]{1,0:T(8,128)(2,1)S(1)}, bf16[288,128]{1,0:T(8,128)(2,1)S(1)}, u32[]{:S(2)}, u32[]{:S(2)}) collective-permute-start(bf16[288,128]{1,0:T(8,128)(2,1)S(1)} %get-tuple-element.187), channel_id=1, source_target_pairs={{0,64},{64,0},{128,192},{192,128},{1,65},{65,1},{129,193},{193,129... | collective-permute-start | bytes 221192 | tf_op jit(solution)/shard_map/ppermute | solution.py:382
  91.9 4.9 %collective-permute-start.35 = (bf16[64,256]{1,0:T(8,128)(2,1)S(1)}, bf16[64,256]{1,0:T(8,128)(2,1)S(1)}, u32[]{:S(2)}, u32[]{:S(2)}) collective-permute-start(bf16[64,256]{1,0:T(8,128)(2,1)S(1)} %get-tuple-element.193), channel_id=1, source_target_pairs={{0,64},{64,0},{128,192},{192,128},{1,65},{65,1},{129,193},{193,129... | collective-permute-start | bytes 98312 | tf_op jit(solution)/shard_map/ppermute | solution.py:382
  96.8 5.0 %collective-permute-start.36 = (bf16[496,128]{1,0:T(8,128)(2,1)S(1)}, bf16[496,128]{1,0:T(8,128)(2,1)S(1)}, u32[]{:S(2)}, u32[]{:S(2)}) collective-permute-start(bf16[496,128]{1,0:T(8,128)(2,1)S(1)} %get-tuple-element.196), channel_id=1, source_target_pairs={{0,32},{32,0},{1,33},{33,1},{2,34},{34,2},{3,35},{35,3},{4,36},{36... | collective-permute-start | bytes 380936 | tf_op jit(solution)/shard_map/ppermute | solution.py:382

commit v3 on v2

--- a/solution.py
+++ b/solution.py
@@ -146,12 +146,12 @@
 
 
 def forward_kernel(*refs):
-    o_ref, stat_ref, q_ref, qm_ref, kv_ref, km_ref = refs[8:14]
+    o_ref, stat_ref, q_ref, qm_ref, kv_ref, km_ref = refs[6:12]
     left, right = slice(0, DH), slice(DH, FEATS)
-    queries = [(ref, 0) for ref in refs[0:4]]
+    queries = pairs_of(refs[0:2], (0, 1, 3, 2), 0)
     assemble(queries, q_ref, 0, left)
     masks(queries, qm_ref, 0, True)
-    for base, parts in ((0, refs[4:6]), (NQ, refs[6:8])):
+    for base, parts in ((0, refs[2:4]), (NQ, refs[4:6])):
         keys = pairs_of(parts, (0, 1, 3, 2), 0)
         assemble(keys, kv_ref, base, left)
         assemble(pairs_of(parts, (0, 3, 1, 2), 2 * PAIR), kv_ref, base, right)
@@ -172,8 +172,8 @@
 
 
 def share_kernel(*refs):
-    o_ref, stat_ref, load_refs, da_ref, delta_ref = refs[4], refs[5], refs[6:10], refs[10], refs[11]
-    assemble([(ref, 0) for ref in refs[0:4]], da_ref, 0, slice(0, DH))
+    o_ref, stat_ref, load_refs, da_ref, delta_ref = refs[2], refs[3], refs[4:8], refs[8], refs[9]
+    assemble(pairs_of(refs[0:2], (0, 3, 1, 2), 0), da_ref, 0, slice(0, DH))
     lane = lax.broadcasted_iota(jnp.int32, (BLOCK, DH), 1)
     for block in range(NQ // BLOCK):
         rows = slice(block * BLOCK, (block + 1) * BLOCK)
@@ -407,28 +407,28 @@
     got = swapped(send, "e", 2, 1)
     dy, send = lax.optimization_barrier((dy, send))
     k, v, q = (jnp.concatenate([keep[i : i + PAD], got[i : i + PAD]], axis=0) for i in (0, PAD, 2 * PAD))
-    k = jnp.concatenate([k, swapped(k, "zr", 4, 1)], axis=0)
-    v = jnp.concatenate([v, swapped(v, "zr", 4, 3)], axis=0)
+    k_got, v_got = lax.optimization_barrier((swapped(k, "zr", 4, 1), swapped(v, "zr", 4, 3)))
+    k, v = jnp.concatenate([k, k_got], axis=0), jnp.concatenate([v, v_got], axis=0)
     dys = [dy, shifted(dy, "head", NH, 1), None, shifted(dy, "head", NH, 3)]
     dy_late, _ = lax.optimization_barrier((dy, got))
     dys[2] = shifted(dy_late, "head", NH, 2)
-    q_one, q_three = swapped(q, "x", 4, 1), swapped(q, "x", 4, 3)
-    k, v, dys = lax.optimization_barrier((k, v, dys))
+    q_got = swapped(q, "x", 4, 1)
+    _, _, dys, q_got = lax.optimization_barrier((k, v, dys, q_got))
     ks, vs = [k, swapped(k, "zr", 4, 3)], [v, swapped(v, "zr", 4, 1)]
-    dys, q_one, q_three = lax.optimization_barrier((dys, q_one, q_three))
     wo, _ = lax.optimization_barrier((wo, dy))
     at_head = lax.axis_index("head")
     wo = jnp.concatenate(
         [lax.dynamic_slice_in_dim(wo, lax.rem(at_head - s + NH, NH) * WIDE, WIDE, 1) for s in range(NH)], axis=1
     )
     keep, send = call(dattn_kernel, "dattn", [at, *dys, wo, ids], [shape((PAD, DH))] * 2, scalars=1)
-    q_late, send = lax.optimization_barrier((q, send))
-    q_two = swapped(q_late, "x", 4, 2)
+    q, send = lax.optimization_barrier((jnp.concatenate([q, q_got], axis=0), send))
+    qs = [q, swapped(q, "x", 4, 3)]
     da_got = swapped(send, "e", 2, 1)
-    ks[1], vs[1], da_got, q_two = lax.optimization_barrier((ks[1], vs[1], da_got, q_two))
-    qs = [q, q_one, q_two, q_three]
     da = jnp.concatenate([keep, da_got], axis=0)
-    das = [da] + [swapped(da, "x", 4, s) for s in (1, 2, 3)]
+    late = [ks[1], vs[1], swapped(da, "x", 4, 3), qs[1]]
+    ks[1], vs[1], da_got, qs[1] = lax.optimization_barrier(late)
+    da = jnp.concatenate([da, da_got], axis=0)
+    das = [da, swapped(da, "x", 4, 1)]
     kvs = [jnp.concatenate([ks[i], vs[i]], axis=0) for i in range(2)]
     kvs = kvs + [swapped(one, "c", 2, 1) for one in kvs]
 

time: 104 us -> 104 us (level)
  waiting for transfers between devices: 21.3 us -> 25.8 us
  starting transfers between devices: 58.4 us -> 54.2 us
    ppermute x29 -> x27, waiting for transfers between devices: 17.2 us -> 22.3 us  [swapped(): return lax.ppermute(value, axis, [(i, i ^ mask) for i in range(size)])]
    ppermute x29 -> x27, starting transfers between devices: 46.8 us -> 42.4 us  [swapped(): return lax.ppermute(value, axis, [(i, i ^ mask) for i in range(size)])]
    ppermute x6, waiting for transfers between devices: 3.91 us -> 2.18 us  [shifted(): lax.ppermute(value, axis, [(i, (i + by) % size) for i in range(size)])]
    ppermute x2, waiting for transfers between devices: 0.17 us -> 1.36 us  [by_core(): lax.ppermute(value, (axis, 'c'), [(i, (i // 2 ^ masks[i % 2]) * 2 + i % 2...]
  transfers between devices with their start and end apart: 37 -> 35, of which waited for: 14 -> 16; matrix products, arithmetic and copies ran while one was open for 1% -> 1% of each run, Pallas kernels for 15% -> 13%
where the time goes in v3:
time: 104 us
  starting transfers between devices  54.2 us (52%)
  waiting for transfers between devices  25.8 us (25%)
  Pallas kernels  19.4 us (19%)
  other arithmetic  2.73 us (3%)
    ppermute x27, starting transfers between devices, swapped(): return lax.ppermute(value, axis, [(i, i ^ mask) for i in range(size)])  42.4 us
    ppermute x27, waiting for transfers between devices, swapped(): return lax.ppermute(value, axis, [(i, i ^ mask) for i in range(size)])  22.3 us
    pallas_call x17, Pallas kernels, call(): pl.pallas_call(kernel, in_specs=[SMEM] * scalars + [VMEM] * (len(ins) - s...  19.4 us
    ppermute x6, starting transfers between devices, shifted(): lax.ppermute(value, axis, [(i, (i + by) % size) for i in range(size)])  8.8 us
    ppermute x2, starting transfers between devices, by_core(): lax.ppermute(value, (axis, 'c'), [(i, (i // 2 ^ masks[i % 2]) * 2 + i % 2...  3.06 us
    ppermute x6, waiting for transfers between devices, shifted(): lax.ppermute(value, axis, [(i, (i + by) % size) for i in range(size)])  2.18 us
  transfers between devices with their start and end apart: 35, of which 16 were waited for; matrix products, arithmetic and copies ran while one was open for 1% of the time, Pallas kernels for 13%

profile of v3, /device:TPU:8, one launch (start us, length us, event | category | flops | bytes accessed | tf_op | source)
XLA Modules:
  0.0 103.5 jit_solution(13854896961933788747)
XLA Ops:
  0.6 0.8 convert_bitcast_fusion.ids_ref.refs_5_
  1.4 1.0 %pad_maximum_fusion.1.all_ref = bf16[136,1280]{1,0:T(8,128)(2,1)S(1)} fusion(bf16[136,512]{1,0:T(8,128)(2,1)} %param.11, bf16[136,256]{1,0:T(8,128)(2,1)} %param.8, bf16[136,256]{1,0:T(8,128)(2,1)} %param.7, bf16[136,256]{1,0:T(8,128)(2,1)} %param.6), kind=kLoop, calls=%fused_computation.1 | loop fusion | flops 1392640 | bytes 696320 | tf_op jit(solution)/shard_map/concatenate | solution.py:403
  2.6 0.6 pack.1
  3.2 2.0 %collective-permute-start = (bf16[432,128]{1,0:T(8,128)(2,1)S(1)}, bf16[432,128]{1,0:T(8,128)(2,1)S(1)}, u32[]{:S(2)}, u32[]{:S(2)}) collective-permute-start(bf16[432,128]{1,0:T(8,128)(2,1)S(1)} %get-tuple-element.99), channel_id=1, source_target_pairs={{0,32},{32,0},{1,33},{33,1},{2,34},{34,2},{3,35},{35,3},{4,36},{36... | collective-permute-start | bytes 331784 | tf_op jit(solution)/shard_map/ppermute | solution.py:382
  5.2 0.4 collective-permute-start.5
  5.6 1.6 %collective-permute-start.3 = (bf16[136,512]{1,0:T(8,128)(2,1)S(1)}, bf16[136,512]{1,0:T(8,128)(2,1)S(1)}, u32[]{:S(2)}, u32[]{:S(2)}) collective-permute-start(bf16[136,512]{1,0:T(8,128)(2,1)S(1)} %get-tuple-element.105.refs_0_.dy0_ref), channel_id=1, source_target_pairs={{0,1},{1,2},{2,3},{3,0},{4,5},{5,6},{6,7},{7,4},{8,9},{9,10},{10,1... | collective-permute-start | bytes 417800 | tf_op jit(solution)/shard_map/ppermute | solution.py:378
  7.2 0.1 constant_dynamic-slice_fusion.3
  7.4 0.9 collective-permute-done
  8.3 3.4 %collective-permute-start.1 = (bf16[288,128]{1,0:T(8,128)(2,1)S(1)}, bf16[288,128]{1,0:T(8,128)(2,1)S(1)}, u32[]{:S(2)}, u32[]{:S(2)}) collective-permute-start(bf16[288,128]{1,0:T(8,128)(2,1)S(1)} %pad_maximum_fusion.5), channel_id=1, source_target_pairs={{0,64},{64,0},{128,192},{192,128},{1,65},{65,1},{129,193},{193,129... | collective-permute-start | bytes 221192 | tf_op jit(solution)/shard_map/ppermute | solution.py:382
  11.6 4.3 %collective-permute-start.2 = (bf16[288,128]{1,0:T(8,128)(2,1)S(1)}, bf16[288,128]{1,0:T(8,128)(2,1)S(1)}, u32[]{:S(2)}, u32[]{:S(2)}) collective-permute-start(bf16[288,128]{1,0:T(8,128)(2,1)S(1)} %pad_maximum_fusion.6), channel_id=1, source_target_pairs={{0,192},{64,128},{128,64},{192,0},{1,193},{65,129},{129,65},{193,1... | collective-permute-start | bytes 221192 | tf_op jit(solution)/shard_map/ppermute | solution.py:382
  15.9 0.1 pad_maximum_fusion.refs_4_.wo_ref
  16.1 2.4 %collective-permute-start.4 = (bf16[136,512]{1,0:T(8,128)(2,1)S(1)}, bf16[136,512]{1,0:T(8,128)(2,1)S(1)}, u32[]{:S(2)}, u32[]{:S(2)}) collective-permute-start(bf16[136,512]{1,0:T(8,128)(2,1)S(1)} %get-tuple-element.105.refs_0_.dy0_ref), channel_id=1, source_target_pairs={{0,2},{1,3},{2,0},{3,1},{4,6},{5,7},{6,4},{7,5},{8,10},{9,11},{10,... | collective-permute-start | bytes 417800 | tf_op jit(solution)/shard_map/ppermute | solution.py:378
  18.5 0.4 collective-permute-done.2
  18.9 1.6 %collective-permute-start.6 = (bf16[288,128]{1,0:T(8,128)(2,1)S(1)}, bf16[288,128]{1,0:T(8,128)(2,1)S(1)}, u32[]{:S(2)}, u32[]{:S(2)}) collective-permute-start(bf16[288,128]{1,0:T(8,128)(2,1)S(1)} %pad_maximum_fusion.7), channel_id=1, source_target_pairs={{0,8},{8,0},{16,24},{24,16},{1,9},{9,1},{17,25},{25,17},{2,10},{10... | collective-permute-start | bytes 221192 | tf_op jit(solution)/shard_map/ppermute | solution.py:382
  20.5 2.2 %collective-permute-done.4.refs_2_.dy2_ref = bf16[136,512]{1,0:T(8,128)(2,1)S(1)} collective-permute-done((bf16[136,512]{1,0:T(8,128)(2,1)S(1)}, bf16[136,512]{1,0:T(8,128)(2,1)S(1)}, u32[]{:S(2)}, u32[]{:S(2)}) %collective-permute-start.4) | collective-permute-done | bytes 139296 | tf_op jit(solution)/shard_map/ppermute | solution.py:378
  22.7 0.7 collective-permute-done.6
  23.4 1.0 dattn.1
  24.4 1.8 %collective-permute-start.7 = (bf16[144,128]{1,0:T(8,128)(2,1)S(1)}, bf16[144,128]{1,0:T(8,128)(2,1)S(1)}, u32[]{:S(2)}, u32[]{:S(2)}) collective-permute-start(bf16[144,128]{1,0:T(8,128)(2,1)S(1)} %get-tuple-element.113), channel_id=1, source_target_pairs={{0,32},{32,0},{1,33},{33,1},{2,34},{34,2},{3,35},{35,3},{4,36},{36... | collective-permute-start | bytes 110600 | tf_op jit(solution)/shard_map/ppermute | solution.py:382
  26.2 3.0 %collective-permute-start.8 = (bf16[576,128]{1,0:T(8,128)(2,1)S(1)}, bf16[576,128]{1,0:T(8,128)(2,1)S(1)}, u32[]{:S(2)}, u32[]{:S(2)}) collective-permute-start(bf16[576,128]{1,0:T(8,128)(2,1)S(1)} %pad_maximum_fusion.2), channel_id=1, source_target_pairs={{0,192},{64,128},{128,64},{192,0},{1,193},{65,129},{129,65},{193,1... | collective-permute-start | bytes 442376 | tf_op jit(solution)/shard_map/ppermute | solution.py:382
  29.2 2.2 %collective-permute-start.9 = (bf16[576,128]{1,0:T(8,128)(2,1)S(1)}, bf16[576,128]{1,0:T(8,128)(2,1)S(1)}, u32[]{:S(2)}, u32[]{:S(2)}) collective-permute-start(bf16[576,128]{1,0:T(8,128)(2,1)S(1)} %pad_maximum_fusion.3), channel_id=1, source_target_pairs={{0,64},{64,0},{128,192},{192,128},{1,65},{65,1},{129,193},{193,129... | collective-permute-start | bytes 442376 | tf_op jit(solution)/shard_map/ppermute | solution.py:382
  31.4 2.8 %collective-permute-start.11 = (bf16[576,128]{1,0:T(8,128)(2,1)S(1)}, bf16[576,128]{1,0:T(8,128)(2,1)S(1)}, u32[]{:S(2)}, u32[]{:S(2)}) collective-permute-start(bf16[576,128]{1,0:T(8,128)(2,1)S(1)} %pad_maximum_fusion.4.refs_0_), channel_id=1, source_target_pairs={{0,24},{8,16},{16,8},{24,0},{1,25},{9,17},{17,9},{25,1},{2,26},{10... | collective-permute-start | bytes 442376 | tf_op jit(solution)/shard_map/ppermute | solution.py:382
  34.1 0.6 collective-permute-start.10
  34.8 0.5 collective-permute-done.9
  35.3 4.4 %collective-permute-done.10 = bf16[288,128]{1,0:T(8,128)(2,1)S(1)} collective-permute-done((bf16[288,128]{1,0:T(8,128)(2,1)S(1)}, bf16[288,128]{1,0:T(8,128)(2,1)S(1)}, u32[]{:S(2)}, u32[]{:S(2)}) %collective-permute-start.10) | collective-permute-done | bytes 73760 | tf_op jit(solution)/shard_map/ppermute | solution.py:382
  40.0 0.3 collective-permute-start.12
  40.3 1.2 %collective-permute-done.14.refs_5_ = bf16[1152,128]{1,0:T(8,128)(2,1)S(1)} collective-permute-done((bf16[1152,128]{1,0:T(8,128)(2,1)S(1)}, bf16[1152,128]{1,0:T(8,128)(2,1)S(1)}, u32[]{:S(2)}, u32[]{:S(2)}) %collective-permute-start.14) | collective-permute-done | bytes 294944 | tf_op jit(solution)/shard_map/ppermute | solution.py:382
  41.5 5.0 %forward.1 = (f32[1152,128]{1,0:T(8,128)S(1)}, f32[8,1152]{1,0:T(8,128)S(1)}, bf16[1152,128]{1,0:T(8,128)(2,1)S(1)}, bf16[1152,128]{1,0:T(8,128)(2,1)S(1)}, bf16...) custom-call(bf16[576,128]{1,0:T(8,128)(2,1)S(1)} %pad_maximum_fusion.4.refs_0_, ...), custom_call_target="tpu_custom_call" | custom-call | flops 2038431744 | bytes 1048576 | tf_op jit(solution)/shard_map/forward/pallas_call | solution.py:47
  46.5 0.4 share.1
  46.9 0.9 collective-permute-start.15
  47.8 2.2 %collective-permute-start.16 = (bf16[368,128]{1,0:T(8,128)(2,1)S(1)}, bf16[368,128]{1,0:T(8,128)(2,1)S(1)}, u32[]{:S(2)}, u32[]{:S(2)}) collective-permute-start(bf16[368,128]{1,0:T(8,128)(2,1)S(1)} %get-tuple-element.123), channel_id=1, source_target_pairs={{0,16},{8,24},{16,0},{24,8},{1,17},{9,25},{17,1},{25,9},{2,18},{10... | collective-permute-start | bytes 282632 | tf_op jit(solution)/shard_map/ppermute | solution.py:382
  49.9 1.8 %collective-permute-start.17 = (bf16[368,128]{1,0:T(8,128)(2,1)S(1)}, bf16[368,128]{1,0:T(8,128)(2,1)S(1)}, u32[]{:S(2)}, u32[]{:S(2)}) collective-permute-start(bf16[368,128]{1,0:T(8,128)(2,1)S(1)} %get-tuple-element.124), channel_id=1, source_target_pairs={{0,24},{8,16},{16,8},{24,0},{1,25},{9,17},{17,9},{25,1},{2,26},{10... | collective-permute-start | bytes 282632 | tf_op jit(solution)/shard_map/ppermute | solution.py:382
  51.7 0.8 collective-permute-done.15.l1_ref
  52.5 2.2 %collective-permute-done.16.l2_ref = bf16[368,128]{1,0:T(8,128)(2,1)S(1)} collective-permute-done((bf16[368,128]{1,0:T(8,128)(2,1)S(1)}, bf16[368,128]{1,0:T(8,128)(2,1)S(1)}, u32[]{:S(2)}, u32[]{:S(2)}) %collective-permute-start.16) | collective-permute-done | bytes 94240 | tf_op jit(solution)/shard_map/ppermute | solution.py:382
  54.8 1.8 %collective-permute-done.17.l3_ref = bf16[368,128]{1,0:T(8,128)(2,1)S(1)} collective-permute-done((bf16[368,128]{1,0:T(8,128)(2,1)S(1)}, bf16[368,128]{1,0:T(8,128)(2,1)S(1)}, u32[]{:S(2)}, u32[]{:S(2)}) %collective-permute-start.17) | collective-permute-done | bytes 94240 | tf_op jit(solution)/shard_map/ppermute | solution.py:382
  56.6 0.9 merge.1
  57.5 0.4 collective-permute-start.18
  58.0 2.8 %backward_one.1 = (bf16[768,256]{1,0:T(8,128)(2,1)S(1)}, f32[1152,128]{1,0:T(8,128)S(1)}) custom-call(bf16[1152,128]{1,0:T(8,128)(2,1)S(1)} %get-tuple-element.128.q_ref, bf16[1152,128]{1,0:T(8,128)(2,1)S(1)} %get-tuple-element.129.qm_ref, bf16[1152,128]{1,0:T(8,128)(2,1)S(1)} %get-tuple-element.130.da_ref, bf16[2304,256]{1,0:T(8,128)(2,1)S(1)} %get-tuple-element.131.kv_ref, ...), custom_call_target="tpu_custom_call" | custom-call | flops 1358954496 | bytes 1048576 | tf_op jit(solution)/shard_map/backward_one/pallas_call | solution.py:47
  60.8 0.8 collective-permute-done.18.other_ref
  61.6 1.2 %project.1 = (bf16[136,512]{1,0:T(8,128)(2,1)S(1)}, bf16[136,512]{1,0:T(8,128)(2,1)S(1)}, bf16[136,512]{1,0:T(8,128)(2,1)S(1)}, bf16[136,512]{1,0:T(8,128)(2,1)S...) custom-call(s32[5]{0:T(128)S(1)} %stack.23.at_ref, ...), custom_call_target="tpu_custom_call" | custom-call | tf_op jit(solution)/shard_map/project/pallas_call | solution.py:47
  62.8 0.3 collective-permute-start.19
  63.2 1.6 %backward_two.1 = (bf16[8,288,128]{2,1,0:T(8,128)(2,1)S(1)}, f32[1152,128]{1,0:T(8,128)S(1)}) custom-call(bf16[1152,128]{1,0:T(8,128)(2,1)S(1)} %get-tuple-element.128.q_ref, bf16[1152,128]{1,0:T(8,128)(2,1)S(1)} %get-tuple-element.129.qm_ref, bf16[1152,128]{1,0:T(8,128)(2,1)S(1)} %get-tuple-element.130.da_ref, ...), custom_call_target="tpu_custom_call" | custom-call | flops 679477248 | bytes 1048576 | tf_op jit(solution)/shard_map/backward_two/pallas_call | solution.py:47
  64.7 0.6 collective-permute-start.21
  65.3 0.1 dwo.1
  65.4 1.8 %collective-permute-start.20 = (bf16[512,256]{1,0:T(8,128)(2,1)S(1)}, bf16[512,256]{1,0:T(8,128)(2,1)S(1)}, u32[]{:S(2)}, u32[]{:S(2)}) collective-permute-start(bf16[512,256]{1,0:T(8,128)(2,1)S(1)} %get-tuple-element.147), channel_id=1, source_target_pairs={{0,24},{4,12},{8,16},{12,4},{16,8},{20,28},{24,0},{28,20},{1,25},{... | collective-permute-start | bytes 786440 | tf_op jit(solution)/shard_map/ppermute | solution.py:387
  67.2 4.1 %backward_three.1 = (bf16[8,288,128]{2,1,0:T(8,128)(2,1)S(1)}, f32[576,128]{1,0:T(8,128)S(1)}, bf16[576,128]{1,0:T(8,128)(2,1)S(1)}) custom-call(bf16[1152,128]{1,0:T(8,128)(2,1)S(1)} %get-tuple-element.128.q_ref, bf16[1152,128]{1,0:T(8,128)(2,1)S(1)} %get-tuple-element.129.qm_ref, bf16[1152,128]{1,0:T(8,128)(2,1)S(1)} %get-tuple-element.130.da_ref, ...), custom_call_target="tpu_custom_call" | custom-call | flops 2038431744 | bytes 1048576 | tf_op jit(solution)/shard_map/backward_three/pallas_call | solution.py:47
  71.5 0.2 core.1
  71.7 1.4 %collective-permute-done.20.refs_1_ = bf16[512,256]{1,0:T(8,128)(2,1)S(1)} collective-permute-done((bf16[512,256]{1,0:T(8,128)(2,1)S(1)}, bf16[512,256]{1,0:T(8,128)(2,1)S(1)}, u32[]{:S(2)}, u32[]{:S(2)}) %collective-permute-start.20) | collective-permute-done | bytes 262176 | tf_op jit(solution)/shard_map/ppermute | solution.py:387
  73.1 1.3 %collective-permute-start.22 = (bf16[576,128]{1,0:T(8,128)(2,1)S(1)}, bf16[576,128]{1,0:T(8,128)(2,1)S(1)}, u32[]{:S(2)}, u32[]{:S(2)}) collective-permute-start(bf16[576,128]{1,0:T(8,128)(2,1)S(1)} %get-tuple-element.152), channel_id=1, source_target_pairs={{0,64},{64,0},{128,192},{192,128},{1,65},{65,1},{129,193},{193,129... | collective-permute-start | bytes 442376 | tf_op jit(solution)/shard_map/ppermute | solution.py:382
  74.5 1.7 %collective-permute-start.26 = (bf16[136,512]{1,0:T(8,128)(2,1)S(1)}, bf16[136,512]{1,0:T(8,128)(2,1)S(1)}, u32[]{:S(2)}, u32[]{:S(2)}) collective-permute-start(bf16[136,512]{1,0:T(8,128)(2,1)S(1)} %get-tuple-element.161), channel_id=1, source_target_pairs={{0,1},{1,2},{2,3},{3,0},{4,5},{5,6},{6,7},{7,4},{8,9},{9,10},{10,1... | collective-permute-start | bytes 417800 | tf_op jit(solution)/shard_map/ppermute | solution.py:378
  76.1 0.4 collective-permute-start.27
  76.6 1.2 %collective-permute-start.25 = (bf16[256,256]{1,0:T(8,128)(2,1)S(1)}, bf16[256,256]{1,0:T(8,128)(2,1)S(1)}, u32[]{:S(2)}, u32[]{:S(2)}) collective-permute-start(bf16[256,256]{1,0:T(8,128)(2,1)S(1)} %get-tuple-element.160), channel_id=1, source_target_pairs={{0,8},{4,28},{8,0},{12,20},{16,24},{20,12},{24,16},{28,4},{1,9},{5... | collective-permute-start | bytes 393224 | tf_op jit(solution)/shard_map/ppermute | solution.py:387
  77.8 2.5 %collective-permute-done.23.refs_3_ = bf16[576,128]{1,0:T(8,128)(2,1)S(1)} collective-permute-done((bf16[576,128]{1,0:T(8,128)(2,1)S(1)}, bf16[576,128]{1,0:T(8,128)(2,1)S(1)}, u32[]{:S(2)}, u32[]{:S(2)}) %collective-permute-start.23) | collective-permute-done | bytes 147488 | tf_op jit(solution)/shard_map/ppermute | solution.py:382
  80.4 2.3 %collective-permute-start.28 = (bf16[136,512]{1,0:T(8,128)(2,1)S(1)}, bf16[136,512]{1,0:T(8,128)(2,1)S(1)}, u32[]{:S(2)}, u32[]{:S(2)}) collective-permute-start(bf16[136,512]{1,0:T(8,128)(2,1)S(1)} %get-tuple-element.164), channel_id=1, source_target_pairs={{0,2},{1,3},{2,0},{3,1},{4,6},{5,7},{6,4},{7,5},{8,10},{9,11},{10,... | collective-permute-start | bytes 417800 | tf_op jit(solution)/shard_map/ppermute | solution.py:378
  82.7 2.6 %collective-permute-start.32 = (bf16[128,256]{1,0:T(8,128)(2,1)S(1)}, bf16[128,256]{1,0:T(8,128)(2,1)S(1)}, u32[]{:S(2)}, u32[]{:S(2)}) collective-permute-start(bf16[128,256]{1,0:T(8,128)(2,1)S(1)} %get-tuple-element.181), channel_id=1, source_target_pairs={{0,192},{64,128},{128,64},{192,0},{1,193},{65,129},{129,65},{193,1... | collective-permute-start | bytes 196616 | tf_op jit(solution)/shard_map/ppermute | solution.py:382
  85.4 1.8 %collective-permute-start.29 = (bf16[288,128]{1,0:T(8,128)(2,1)S(1)}, bf16[288,128]{1,0:T(8,128)(2,1)S(1)}, u32[]{:S(2)}, u32[]{:S(2)}) collective-permute-start(bf16[288,128]{1,0:T(8,128)(2,1)S(1)} %get-tuple-element.173), channel_id=1, source_target_pairs={{0,24},{8,16},{16,8},{24,0},{1,25},{9,17},{17,9},{25,1},{2,26},{10... | collective-permute-start | bytes 221192 | tf_op jit(solution)/shard_map/ppermute | solution.py:382
  87.2 1.9 %collective-permute-start.30 = (bf16[288,128]{1,0:T(8,128)(2,1)S(1)}, bf16[288,128]{1,0:T(8,128)(2,1)S(1)}, u32[]{:S(2)}, u32[]{:S(2)}) collective-permute-start(bf16[288,128]{1,0:T(8,128)(2,1)S(1)} %get-tuple-element.175), channel_id=1, source_target_pairs={{0,192},{64,128},{128,64},{192,0},{1,193},{65,129},{129,65},{193,1... | collective-permute-start | bytes 221192 | tf_op jit(solution)/shard_map/ppermute | solution.py:382
  89.1 3.1 %collective-permute-start.31 = (bf16[288,128]{1,0:T(8,128)(2,1)S(1)}, bf16[288,128]{1,0:T(8,128)(2,1)S(1)}, u32[]{:S(2)}, u32[]{:S(2)}) collective-permute-start(bf16[288,128]{1,0:T(8,128)(2,1)S(1)} %get-tuple-element.177), channel_id=1, source_target_pairs={{0,64},{64,0},{128,192},{192,128},{1,65},{65,1},{129,193},{193,129... | collective-permute-start | bytes 221192 | tf_op jit(solution)/shard_map/ppermute | solution.py:382
  92.3 1.9 %collective-permute-start.33 = (bf16[64,256]{1,0:T(8,128)(2,1)S(1)}, bf16[64,256]{1,0:T(8,128)(2,1)S(1)}, u32[]{:S(2)}, u32[]{:S(2)}) collective-permute-start(bf16[64,256]{1,0:T(8,128)(2,1)S(1)} %get-tuple-element.183), channel_id=1, source_target_pairs={{0,64},{64,0},{128,192},{192,128},{1,65},{65,1},{129,193},{193,129... | collective-permute-start | bytes 98312 | tf_op jit(solution)/shard_map/ppermute | solution.py:382
  94.2 2.6 %collective-permute-done.31.refs_5_ = bf16[288,128]{1,0:T(8,128)(2,1)S(1)} collective-permute-done((bf16[288,128]{1,0:T(8,128)(2,1)S(1)}, bf16[288,128]{1,0:T(8,128)(2,1)S(1)}, u32[]{:S(2)}, u32[]{:S(2)}) %collective-permute-start.31) | collective-permute-done | bytes 73760 | tf_op jit(solution)/shard_map/ppermute | solution.py:382
  96.8 0.4 collective-permute-done.33.refs_7_
  97.2 1.5 %collective-permute-start.34 = (bf16[496,128]{1,0:T(8,128)(2,1)S(1)}, bf16[496,128]{1,0:T(8,128)(2,1)S(1)}, u32[]{:S(2)}, u32[]{:S(2)}) collective-permute-start(bf16[496,128]{1,0:T(8,128)(2,1)S(1)} %get-tuple-element.186), channel_id=1, source_target_pairs={{0,32},{32,0},{1,33},{33,1},{2,34},{34,2},{3,35},{35,3},{4,36},{36... | collective-permute-start | bytes 380936 | tf_op jit(solution)/shard_map/ppermute | solution.py:382
  98.7 0.7 add_convert_fusion
  99.4 2.8 %collective-permute-done.34.got_ref = bf16[496,128]{1,0:T(8,128)(2,1)S(1)} collective-permute-done((bf16[496,128]{1,0:T(8,128)(2,1)S(1)}, bf16[496,128]{1,0:T(8,128)(2,1)S(1)}, u32[]{:S(2)}, u32[]{:S(2)}) %collective-permute-start.34) | collective-permute-done | bytes 127008 | tf_op jit(solution)/shard_map/ppermute | solution.py:382
  102.3 1.3 %place.1 = (bf16[136,256]{1,0:T(8,128)(2,1)}, bf16[136,256]{1,0:T(8,128)(2,1)}, bf16[136,256]{1,0:T(8,128)(2,1)}, f32[32,256]{1,0:T(8,128)}) custom-call(s32[5]{0:T(128)S(1)} %stack.23.at_ref, bf16[144,384]{1,0:T(8,128)(2,1)S(1)} %get-tuple-element.184.mine_ref, f32[32,256]{1,0:T(8,128)S(1)} %get-tuple-element.185.wmine_ref, ...), custom_call_target="tpu_custom_call" | custom-call | tf_op jit(solution)/shard_map/place/pallas_call | solution.py:47
  (49 shorter events, 1.0 us)
Async XLA Ops:
  0.6 6.6 %copy-start = (bf16[256,2048]{1,0:T(8,128)(2,1)S(1)}, bf16[256,2048]{1,0:T(8,128)(2,1)}, u32[]{:S(2)}) copy-start(bf16[256,2048]{1,0:T(8,128)(2,1)} %param.10) | copy-start | bytes 3145732
  3.2 5.1 %collective-permute-start = (bf16[432,128]{1,0:T(8,128)(2,1)S(1)}, bf16[432,128]{1,0:T(8,128)(2,1)S(1)}, u32[]{:S(2)}, u32[]{:S(2)}) collective-permute-start(bf16[432,128]{1,0:T(8,128)(2,1)S(1)} %get-tuple-element.99), channel_id=1, source_target_pairs={{0,32},{32,0},{1,33},{33,1},{2,34},{34,2},{3,35},{35,3},{4,36},{36... | collective-permute-start | bytes 331784 | tf_op jit(solution)/shard_map/ppermute | solution.py:382
  5.2 15.4 %collective-permute-start.5 = (bf16[136,512]{1,0:T(8,128)(2,1)S(1)}, bf16[136,512]{1,0:T(8,128)(2,1)S(1)}, u32[]{:S(2)}, u32[]{:S(2)}) collective-permute-start(bf16[136,512]{1,0:T(8,128)(2,1)S(1)} %get-tuple-element.105.refs_0_.dy0_ref), channel_id=1, source_target_pairs={{0,3},{1,0},{2,1},{3,2},{4,7},{5,4},{6,5},{7,6},{8,11},{9,8},{10,9... | collective-permute-start | bytes 417800 | tf_op jit(solution)/shard_map/ppermute | solution.py:378
  5.6 14.9 %collective-permute-start.3 = (bf16[136,512]{1,0:T(8,128)(2,1)S(1)}, bf16[136,512]{1,0:T(8,128)(2,1)S(1)}, u32[]{:S(2)}, u32[]{:S(2)}) collective-permute-start(bf16[136,512]{1,0:T(8,128)(2,1)S(1)} %get-tuple-element.105.refs_0_.dy0_ref), channel_id=1, source_target_pairs={{0,1},{1,2},{2,3},{3,0},{4,5},{5,6},{6,7},{7,4},{8,9},{9,10},{10,1... | collective-permute-start | bytes 417800 | tf_op jit(solution)/shard_map/ppermute | solution.py:378
  8.3 10.2 %collective-permute-start.1 = (bf16[288,128]{1,0:T(8,128)(2,1)S(1)}, bf16[288,128]{1,0:T(8,128)(2,1)S(1)}, u32[]{:S(2)}, u32[]{:S(2)}) collective-permute-start(bf16[288,128]{1,0:T(8,128)(2,1)S(1)} %pad_maximum_fusion.5), channel_id=1, source_target_pairs={{0,64},{64,0},{128,192},{192,128},{1,65},{65,1},{129,193},{193,129... | collective-permute-start | bytes 221192 | tf_op jit(solution)/shard_map/ppermute | solution.py:382
  11.6 7.2 %collective-permute-start.2 = (bf16[288,128]{1,0:T(8,128)(2,1)S(1)}, bf16[288,128]{1,0:T(8,128)(2,1)S(1)}, u32[]{:S(2)}, u32[]{:S(2)}) collective-permute-start(bf16[288,128]{1,0:T(8,128)(2,1)S(1)} %pad_maximum_fusion.6), channel_id=1, source_target_pairs={{0,192},{64,128},{128,64},{192,0},{1,193},{65,129},{129,65},{193,1... | collective-permute-start | bytes 221192 | tf_op jit(solution)/shard_map/ppermute | solution.py:382
  16.1 6.6 %collective-permute-start.4 = (bf16[136,512]{1,0:T(8,128)(2,1)S(1)}, bf16[136,512]{1,0:T(8,128)(2,1)S(1)}, u32[]{:S(2)}, u32[]{:S(2)}) collective-permute-start(bf16[136,512]{1,0:T(8,128)(2,1)S(1)} %get-tuple-element.105.refs_0_.dy0_ref), channel_id=1, source_target_pairs={{0,2},{1,3},{2,0},{3,1},{4,6},{5,7},{6,4},{7,5},{8,10},{9,11},{10,... | collective-permute-start | bytes 417800 | tf_op jit(solution)/shard_map/ppermute | solution.py:378
  18.9 4.4 %collective-permute-start.6 = (bf16[288,128]{1,0:T(8,128)(2,1)S(1)}, bf16[288,128]{1,0:T(8,128)(2,1)S(1)}, u32[]{:S(2)}, u32[]{:S(2)}) collective-permute-start(bf16[288,128]{1,0:T(8,128)(2,1)S(1)} %pad_maximum_fusion.7), channel_id=1, source_target_pairs={{0,8},{8,0},{16,24},{24,16},{1,9},{9,1},{17,25},{25,17},{2,10},{10... | collective-permute-start | bytes 221192 | tf_op jit(solution)/shard_map/ppermute | solution.py:382
  24.4 9.7 %collective-permute-start.7 = (bf16[144,128]{1,0:T(8,128)(2,1)S(1)}, bf16[144,128]{1,0:T(8,128)(2,1)S(1)}, u32[]{:S(2)}, u32[]{:S(2)}) collective-permute-start(bf16[144,128]{1,0:T(8,128)(2,1)S(1)} %get-tuple-element.113), channel_id=1, source_target_pairs={{0,32},{32,0},{1,33},{33,1},{2,34},{34,2},{3,35},{35,3},{4,36},{36... | collective-permute-start | bytes 110600 | tf_op jit(solution)/shard_map/ppermute | solution.py:382
  26.2 8.6 %collective-permute-start.8 = (bf16[576,128]{1,0:T(8,128)(2,1)S(1)}, bf16[576,128]{1,0:T(8,128)(2,1)S(1)}, u32[]{:S(2)}, u32[]{:S(2)}) collective-permute-start(bf16[576,128]{1,0:T(8,128)(2,1)S(1)} %pad_maximum_fusion.2), channel_id=1, source_target_pairs={{0,192},{64,128},{128,64},{192,0},{1,193},{65,129},{129,65},{193,1... | collective-permute-start | bytes 442376 | tf_op jit(solution)/shard_map/ppermute | solution.py:382
  29.2 6.1 %collective-permute-start.9 = (bf16[576,128]{1,0:T(8,128)(2,1)S(1)}, bf16[576,128]{1,0:T(8,128)(2,1)S(1)}, u32[]{:S(2)}, u32[]{:S(2)}) collective-permute-start(bf16[576,128]{1,0:T(8,128)(2,1)S(1)} %pad_maximum_fusion.3), channel_id=1, source_target_pairs={{0,64},{64,0},{128,192},{192,128},{1,65},{65,1},{129,193},{193,129... | collective-permute-start | bytes 442376 | tf_op jit(solution)/shard_map/ppermute | solution.py:382
  31.4 8.4 %collective-permute-start.11 = (bf16[576,128]{1,0:T(8,128)(2,1)S(1)}, bf16[576,128]{1,0:T(8,128)(2,1)S(1)}, u32[]{:S(2)}, u32[]{:S(2)}) collective-permute-start(bf16[576,128]{1,0:T(8,128)(2,1)S(1)} %pad_maximum_fusion.4.refs_0_), channel_id=1, source_target_pairs={{0,24},{8,16},{16,8},{24,0},{1,25},{9,17},{17,9},{25,1},{2,26},{10... | collective-permute-start | bytes 442376 | tf_op jit(solution)/shard_map/ppermute | solution.py:382
  34.1 5.7 %collective-permute-start.10 = (bf16[288,128]{1,0:T(8,128)(2,1)S(1)}, bf16[288,128]{1,0:T(8,128)(2,1)S(1)}, u32[]{:S(2)}, u32[]{:S(2)}) collective-permute-start(bf16[288,128]{1,0:T(8,128)(2,1)S(1)} %pad_maximum_fusion.8), channel_id=1, source_target_pairs={{0,24},{8,16},{16,8},{24,0},{1,25},{9,17},{17,9},{25,1},{2,26},{10... | collective-permute-start | bytes 221192 | tf_op jit(solution)/shard_map/ppermute | solution.py:382
  34.7 5.6 %collective-permute-start.13 = (bf16[1152,128]{1,0:T(8,128)(2,1)S(1)}, bf16[1152,128]{1,0:T(8,128)(2,1)S(1)}, u32[]{:S(2)}, u32[]{:S(2)}) collective-permute-start(bf16[1152,128]{1,0:T(8,128)(2,1)S(1)} %constant_dynamic-update-slice_fusion.3.refs_2_), channel_id=1, source_target_pairs={{0,4},{4,0},{1,5},{5,1},{2,6},{6,2},{3,7},{7,3},{8,12},{12,8},{9,1... | collective-permute-start | bytes 884744 | tf_op jit(solution)/shard_map/ppermute | solution.py:382
  39.8 1.7 %collective-permute-start.14 = (bf16[1152,128]{1,0:T(8,128)(2,1)S(1)}, bf16[1152,128]{1,0:T(8,128)(2,1)S(1)}, u32[]{:S(2)}, u32[]{:S(2)}) collective-permute-start(bf16[1152,128]{1,0:T(8,128)(2,1)S(1)} %constant_dynamic-update-slice_fusion.9.refs_3_), channel_id=1, source_target_pairs={{0,4},{4,0},{1,5},{5,1},{2,6},{6,2},{3,7},{7,3},{8,12},{12,8},{9,1... | collective-permute-start | bytes 884744 | tf_op jit(solution)/shard_map/ppermute | solution.py:382
  40.0 6.5 %collective-permute-start.12 = (bf16[576,128]{1,0:T(8,128)(2,1)S(1)}, bf16[576,128]{1,0:T(8,128)(2,1)S(1)}, u32[]{:S(2)}, u32[]{:S(2)}) collective-permute-start(bf16[576,128]{1,0:T(8,128)(2,1)S(1)} %constant_dynamic-update-slice_fusion.refs_0_), channel_id=1, source_target_pairs={{0,8},{8,0},{16,24},{24,16},{1,9},{9,1},{17,25},{25,17},{2,10},{10... | collective-permute-start | bytes 442376 | tf_op jit(solution)/shard_map/ppermute | solution.py:382
  46.9 5.6 %collective-permute-start.15 = (bf16[368,128]{1,0:T(8,128)(2,1)S(1)}, bf16[368,128]{1,0:T(8,128)(2,1)S(1)}, u32[]{:S(2)}, u32[]{:S(2)}) collective-permute-start(bf16[368,128]{1,0:T(8,128)(2,1)S(1)} %get-tuple-element.122), channel_id=1, source_target_pairs={{0,8},{8,0},{16,24},{24,16},{1,9},{9,1},{17,25},{25,17},{2,10},{10... | collective-permute-start | bytes 282632 | tf_op jit(solution)/shard_map/ppermute | solution.py:382
  47.8 7.0 %collective-permute-start.16 = (bf16[368,128]{1,0:T(8,128)(2,1)S(1)}, bf16[368,128]{1,0:T(8,128)(2,1)S(1)}, u32[]{:S(2)}, u32[]{:S(2)}) collective-permute-start(bf16[368,128]{1,0:T(8,128)(2,1)S(1)} %get-tuple-element.123), channel_id=1, source_target_pairs={{0,16},{8,24},{16,0},{24,8},{1,17},{9,25},{17,1},{25,9},{2,18},{10... | collective-permute-start | bytes 282632 | tf_op jit(solution)/shard_map/ppermute | solution.py:382
  49.9 6.7 %collective-permute-start.17 = (bf16[368,128]{1,0:T(8,128)(2,1)S(1)}, bf16[368,128]{1,0:T(8,128)(2,1)S(1)}, u32[]{:S(2)}, u32[]{:S(2)}) collective-permute-start(bf16[368,128]{1,0:T(8,128)(2,1)S(1)} %get-tuple-element.124), channel_id=1, source_target_pairs={{0,24},{8,16},{16,8},{24,0},{1,25},{9,17},{17,9},{25,1},{2,26},{10... | collective-permute-start | bytes 282632 | tf_op jit(solution)/shard_map/ppermute | solution.py:382
  57.5 4.0 %collective-permute-start.18 = (bf16[144,128]{1,0:T(8,128)(2,1)S(1)}, bf16[144,128]{1,0:T(8,128)(2,1)S(1)}, u32[]{:S(2)}, u32[]{:S(2)}) collective-permute-start(bf16[144,128]{1,0:T(8,128)(2,1)S(1)} %get-tuple-element.126), channel_id=1, source_target_pairs={{0,32},{32,0},{1,33},{33,1},{2,34},{34,2},{3,35},{35,3},{4,36},{36... | collective-permute-start | bytes 110600 | tf_op jit(solution)/shard_map/ppermute | solution.py:382
  62.8 2.5 %collective-permute-start.19 = (bf16[4,256,256]{2,1,0:T(8,128)(2,1)S(1)}, bf16[4,256,256]{2,1,0:T(8,128)(2,1)S(1)}, u32[]{:S(2)}, u32[]{:S(2)}) collective-permute-start(bf16[4,256,256]{2,1,0:T(8,128)(2,1)S(1)} %get-tuple-element.140), channel_id=1, source_target_pairs={{0,4},{4,0},{1,5},{5,1},{2,6},{6,2},{3,7},{7,3},{8,12},{12,8},{9,1... | collective-permute-start | bytes 1572872 | tf_op jit(solution)/shard_map/ppermute | solution.py:382
  64.7 6.7 %collective-permute-start.21 = (bf16[8,288,128]{2,1,0:T(8,128)(2,1)S(1)}, bf16[8,288,128]{2,1,0:T(8,128)(2,1)S(1)}, u32[]{:S(2)}, u32[]{:S(2)}) collective-permute-start(bf16[8,288,128]{2,1,0:T(8,128)(2,1)S(1)} %get-tuple-element.150), channel_id=1, source_target_pairs={{0,4},{4,0},{1,5},{5,1},{2,6},{6,2},{3,7},{7,3},{8,12},{12,8},{9,1... | collective-permute-start | bytes 1769480 | tf_op jit(solution)/shard_map/ppermute | solution.py:382
  65.4 7.7 %collective-permute-start.20 = (bf16[512,256]{1,0:T(8,128)(2,1)S(1)}, bf16[512,256]{1,0:T(8,128)(2,1)S(1)}, u32[]{:S(2)}, u32[]{:S(2)}) collective-permute-start(bf16[512,256]{1,0:T(8,128)(2,1)S(1)} %get-tuple-element.147), channel_id=1, source_target_pairs={{0,24},{4,12},{8,16},{12,4},{16,8},{20,28},{24,0},{28,20},{1,25},{... | collective-permute-start | bytes 786440 | tf_op jit(solution)/shard_map/ppermute | solution.py:387
  71.4 5.2 %collective-permute-start.24 = (bf16[576,128]{1,0:T(8,128)(2,1)S(1)}, bf16[576,128]{1,0:T(8,128)(2,1)S(1)}, u32[]{:S(2)}, u32[]{:S(2)}) collective-permute-start(bf16[576,128]{1,0:T(8,128)(2,1)S(1)} %get-tuple-element.154), channel_id=1, source_target_pairs={{0,8},{8,0},{16,24},{24,16},{1,9},{9,1},{17,25},{25,17},{2,10},{10... | collective-permute-start | bytes 442376 | tf_op jit(solution)/shard_map/ppermute | solution.py:382
  71.6 8.7 %collective-permute-start.23 = (bf16[576,128]{1,0:T(8,128)(2,1)S(1)}, bf16[576,128]{1,0:T(8,128)(2,1)S(1)}, u32[]{:S(2)}, u32[]{:S(2)}) collective-permute-start(bf16[576,128]{1,0:T(8,128)(2,1)S(1)} %get-tuple-element.153), channel_id=1, source_target_pairs={{0,192},{64,128},{128,64},{192,0},{1,193},{65,129},{129,65},{193,1... | collective-permute-start | bytes 442376 | tf_op jit(solution)/shard_map/ppermute | solution.py:382
  73.1 9.6 %collective-permute-start.22 = (bf16[576,128]{1,0:T(8,128)(2,1)S(1)}, bf16[576,128]{1,0:T(8,128)(2,1)S(1)}, u32[]{:S(2)}, u32[]{:S(2)}) collective-permute-start(bf16[576,128]{1,0:T(8,128)(2,1)S(1)} %get-tuple-element.152), channel_id=1, source_target_pairs={{0,64},{64,0},{128,192},{192,128},{1,65},{65,1},{129,193},{193,129... | collective-permute-start | bytes 442376 | tf_op jit(solution)/shard_map/ppermute | solution.py:382
  74.5 8.2 %collective-permute-start.26 = (bf16[136,512]{1,0:T(8,128)(2,1)S(1)}, bf16[136,512]{1,0:T(8,128)(2,1)S(1)}, u32[]{:S(2)}, u32[]{:S(2)}) collective-permute-start(bf16[136,512]{1,0:T(8,128)(2,1)S(1)} %get-tuple-element.161), channel_id=1, source_target_pairs={{0,1},{1,2},{2,3},{3,0},{4,5},{5,6},{6,7},{7,4},{8,9},{9,10},{10,1... | collective-permute-start | bytes 417800 | tf_op jit(solution)/shard_map/ppermute | solution.py:378
  76.1 6.5 %collective-permute-start.27 = (bf16[136,512]{1,0:T(8,128)(2,1)S(1)}, bf16[136,512]{1,0:T(8,128)(2,1)S(1)}, u32[]{:S(2)}, u32[]{:S(2)}) collective-permute-start(bf16[136,512]{1,0:T(8,128)(2,1)S(1)} %get-tuple-element.162), channel_id=1, source_target_pairs={{0,3},{1,0},{2,1},{3,2},{4,7},{5,4},{6,5},{7,6},{8,11},{9,8},{10,9... | collective-permute-start | bytes 417800 | tf_op jit(solution)/shard_map/ppermute | solution.py:378
  76.6 6.1 %collective-permute-start.25 = (bf16[256,256]{1,0:T(8,128)(2,1)S(1)}, bf16[256,256]{1,0:T(8,128)(2,1)S(1)}, u32[]{:S(2)}, u32[]{:S(2)}) collective-permute-start(bf16[256,256]{1,0:T(8,128)(2,1)S(1)} %get-tuple-element.160), channel_id=1, source_target_pairs={{0,8},{4,28},{8,0},{12,20},{16,24},{20,12},{24,16},{28,4},{1,9},{5... | collective-permute-start | bytes 393224 | tf_op jit(solution)/shard_map/ppermute | solution.py:387
  80.4 18.3 %collective-permute-start.28 = (bf16[136,512]{1,0:T(8,128)(2,1)S(1)}, bf16[136,512]{1,0:T(8,128)(2,1)S(1)}, u32[]{:S(2)}, u32[]{:S(2)}) collective-permute-start(bf16[136,512]{1,0:T(8,128)(2,1)S(1)} %get-tuple-element.164), channel_id=1, source_target_pairs={{0,2},{1,3},{2,0},{3,1},{4,6},{5,7},{6,4},{7,5},{8,10},{9,11},{10,... | collective-permute-start | bytes 417800 | tf_op jit(solution)/shard_map/ppermute | solution.py:378
  82.7 9.6 %collective-permute-start.32 = (bf16[128,256]{1,0:T(8,128)(2,1)S(1)}, bf16[128,256]{1,0:T(8,128)(2,1)S(1)}, u32[]{:S(2)}, u32[]{:S(2)}) collective-permute-start(bf16[128,256]{1,0:T(8,128)(2,1)S(1)} %get-tuple-element.181), channel_id=1, source_target_pairs={{0,192},{64,128},{128,64},{192,0},{1,193},{65,129},{129,65},{193,1... | collective-permute-start | bytes 196616 | tf_op jit(solution)/shard_map/ppermute | solution.py:382
  85.4 8.8 %collective-permute-start.29 = (bf16[288,128]{1,0:T(8,128)(2,1)S(1)}, bf16[288,128]{1,0:T(8,128)(2,1)S(1)}, u32[]{:S(2)}, u32[]{:S(2)}) collective-permute-start(bf16[288,128]{1,0:T(8,128)(2,1)S(1)} %get-tuple-element.173), channel_id=1, source_target_pairs={{0,24},{8,16},{16,8},{24,0},{1,25},{9,17},{17,9},{25,1},{2,26},{10... | collective-permute-start | bytes 221192 | tf_op jit(solution)/shard_map/ppermute | solution.py:382
  87.2 7.0 %collective-permute-start.30 = (bf16[288,128]{1,0:T(8,128)(2,1)S(1)}, bf16[288,128]{1,0:T(8,128)(2,1)S(1)}, u32[]{:S(2)}, u32[]{:S(2)}) collective-permute-start(bf16[288,128]{1,0:T(8,128)(2,1)S(1)} %get-tuple-element.175), channel_id=1, source_target_pairs={{0,192},{64,128},{128,64},{192,0},{1,193},{65,129},{129,65},{193,1... | collective-permute-start | bytes 221192 | tf_op jit(solution)/shard_map/ppermute | solution.py:382
  89.1 7.7 %collective-permute-start.31 = (bf16[288,128]{1,0:T(8,128)(2,1)S(1)}, bf16[288,128]{1,0:T(8,128)(2,1)S(1)}, u32[]{:S(2)}, u32[]{:S(2)}) collective-permute-start(bf16[288,128]{1,0:T(8,128)(2,1)S(1)} %get-tuple-element.177), channel_id=1, source_target_pairs={{0,64},{64,0},{128,192},{192,128},{1,65},{65,1},{129,193},{193,129... | collective-permute-start | bytes 221192 | tf_op jit(solution)/shard_map/ppermute | solution.py:382
  92.3 4.9 %collective-permute-start.33 = (bf16[64,256]{1,0:T(8,128)(2,1)S(1)}, bf16[64,256]{1,0:T(8,128)(2,1)S(1)}, u32[]{:S(2)}, u32[]{:S(2)}) collective-permute-start(bf16[64,256]{1,0:T(8,128)(2,1)S(1)} %get-tuple-element.183), channel_id=1, source_target_pairs={{0,64},{64,0},{128,192},{192,128},{1,65},{65,1},{129,193},{193,129... | collective-permute-start | bytes 98312 | tf_op jit(solution)/shard_map/ppermute | solution.py:382
  97.2 5.0 %collective-permute-start.34 = (bf16[496,128]{1,0:T(8,128)(2,1)S(1)}, bf16[496,128]{1,0:T(8,128)(2,1)S(1)}, u32[]{:S(2)}, u32[]{:S(2)}) collective-permute-start(bf16[496,128]{1,0:T(8,128)(2,1)S(1)} %get-tuple-element.186), channel_id=1, source_target_pairs={{0,32},{32,0},{1,33},{33,1},{2,34},{34,2},{3,35},{35,3},{4,36},{36... | collective-permute-start | bytes 380936 | tf_op jit(solution)/shard_map/ppermute | solution.py:382

commit v4 on v3

--- a/solution.py
+++ b/solution.py
@@ -172,8 +172,8 @@
 
 
 def share_kernel(*refs):
-    o_ref, stat_ref, load_refs, da_ref, delta_ref = refs[2], refs[3], refs[4:8], refs[8], refs[9]
-    assemble(pairs_of(refs[0:2], (0, 3, 1, 2), 0), da_ref, 0, slice(0, DH))
+    o_ref, stat_ref, load_refs, da_ref, delta_ref = refs[4], refs[5], refs[6:10], refs[10], refs[11]
+    assemble([(ref, 0) for ref in refs[0:4]], da_ref, 0, slice(0, DH))
     lane = lax.broadcasted_iota(jnp.int32, (BLOCK, DH), 1)
     for block in range(NQ // BLOCK):
         rows = slice(block * BLOCK, (block + 1) * BLOCK)
@@ -424,11 +424,9 @@
     q, send = lax.optimization_barrier((jnp.concatenate([q, q_got], axis=0), send))
     qs = [q, swapped(q, "x", 4, 3)]
     da_got = swapped(send, "e", 2, 1)
+    ks[1], vs[1], da_got, qs[1] = lax.optimization_barrier((ks[1], vs[1], da_got, qs[1]))
     da = jnp.concatenate([keep, da_got], axis=0)
-    late = [ks[1], vs[1], swapped(da, "x", 4, 3), qs[1]]
-    ks[1], vs[1], da_got, qs[1] = lax.optimization_barrier(late)
-    da = jnp.concatenate([da, da_got], axis=0)
-    das = [da, swapped(da, "x", 4, 1)]
+    das = [da] + [swapped(da, "x", 4, s) for s in (1, 2, 3)]
     kvs = [jnp.concatenate([ks[i], vs[i]], axis=0) for i in range(2)]
     kvs = kvs + [swapped(one, "c", 2, 1) for one in kvs]
 

time: 104 us -> 100 us (0.962)
  waiting for transfers between devices: 25.8 us -> 16.7 us
  starting transfers between devices: 54.2 us -> 59.6 us
    ppermute x27 -> x28, waiting for transfers between devices: 22.3 us -> 16.7 us  [swapped(): return lax.ppermute(value, axis, [(i, i ^ mask) for i in range(size)])]
    ppermute x27 -> x28, starting transfers between devices: 42.4 us -> 47.7 us  [swapped(): return lax.ppermute(value, axis, [(i, i ^ mask) for i in range(size)])]
    ppermute x6, waiting for transfers between devices: 2.18 us -> 0.02 us  [shifted(): lax.ppermute(value, axis, [(i, (i + by) % size) for i in range(size)])]
    ppermute x2, waiting for transfers between devices: 1.36 us -> 0.01 us  [by_core(): lax.ppermute(value, (axis, 'c'), [(i, (i // 2 ^ masks[i % 2]) * 2 + i % 2...]
  transfers between devices with their start and end apart: 35 -> 36, of which waited for: 16 -> 13; matrix products, arithmetic and copies ran while one was open for 1% -> 1% of each run, Pallas kernels for 13% -> 15%
where the time goes in v4:
time: 100 us; the launch traced here: 99.8 us
  starting transfers between devices  59.6 us (60%)
  Pallas kernels  19.4 us (19%)
  waiting for transfers between devices  16.7 us (17%)
  other arithmetic  2.73 us (3%)
    ppermute x28, starting transfers between devices, swapped(): return lax.ppermute(value, axis, [(i, i ^ mask) for i in range(size)])  47.7 us
    pallas_call x17, Pallas kernels, call(): pl.pallas_call(kernel, in_specs=[SMEM] * scalars + [VMEM] * (len(ins) - s...  19.4 us
    ppermute x28, waiting for transfers between devices, swapped(): return lax.ppermute(value, axis, [(i, i ^ mask) for i in range(size)])  16.7 us
    ppermute x6, starting transfers between devices, shifted(): lax.ppermute(value, axis, [(i, (i + by) % size) for i in range(size)])  8.81 us
    ppermute x2, starting transfers between devices, by_core(): lax.ppermute(value, (axis, 'c'), [(i, (i // 2 ^ masks[i % 2]) * 2 + i % 2...  3.14 us
  transfers between devices with their start and end apart: 36, of which 13 were waited for; matrix products, arithmetic and copies ran while one was open for 1% of the time, Pallas kernels for 15%

profile of v4, /device:TPU:8, one launch (start us, length us, event | category | flops | bytes accessed | tf_op | source)
XLA Modules:
  0.0 99.8 jit_solution(3366761972377210232)
XLA Ops:
  0.6 0.8 convert_bitcast_fusion.ids_ref.refs_5_
  1.4 1.0 %pad_maximum_fusion.1.all_ref = bf16[136,1280]{1,0:T(8,128)(2,1)S(1)} fusion(bf16[136,512]{1,0:T(8,128)(2,1)} %param.11, bf16[136,256]{1,0:T(8,128)(2,1)} %param.8, bf16[136,256]{1,0:T(8,128)(2,1)} %param.7, bf16[136,256]{1,0:T(8,128)(2,1)} %param.6), kind=kLoop, calls=%fused_computation.1 | loop fusion | flops 1392640 | bytes 696320 | tf_op jit(solution)/shard_map/concatenate | solution.py:403
  2.6 0.6 pack.1
  3.2 2.0 %collective-permute-start = (bf16[432,128]{1,0:T(8,128)(2,1)S(1)}, bf16[432,128]{1,0:T(8,128)(2,1)S(1)}, u32[]{:S(2)}, u32[]{:S(2)}) collective-permute-start(bf16[432,128]{1,0:T(8,128)(2,1)S(1)} %get-tuple-element.99), channel_id=1, source_target_pairs={{0,32},{32,0},{1,33},{33,1},{2,34},{34,2},{3,35},{35,3},{4,36},{36... | collective-permute-start | bytes 331784 | tf_op jit(solution)/shard_map/ppermute | solution.py:382
  5.2 0.4 collective-permute-start.5
  5.6 1.6 %collective-permute-start.3 = (bf16[136,512]{1,0:T(8,128)(2,1)S(1)}, bf16[136,512]{1,0:T(8,128)(2,1)S(1)}, u32[]{:S(2)}, u32[]{:S(2)}) collective-permute-start(bf16[136,512]{1,0:T(8,128)(2,1)S(1)} %get-tuple-element.105.refs_0_.dy0_ref), channel_id=1, source_target_pairs={{0,1},{1,2},{2,3},{3,0},{4,5},{5,6},{6,7},{7,4},{8,9},{9,10},{10,1... | collective-permute-start | bytes 417800 | tf_op jit(solution)/shard_map/ppermute | solution.py:378
  7.2 0.1 constant_dynamic-slice_fusion.3
  7.4 0.9 collective-permute-done
  8.3 3.4 %collective-permute-start.1 = (bf16[288,128]{1,0:T(8,128)(2,1)S(1)}, bf16[288,128]{1,0:T(8,128)(2,1)S(1)}, u32[]{:S(2)}, u32[]{:S(2)}) collective-permute-start(bf16[288,128]{1,0:T(8,128)(2,1)S(1)} %pad_maximum_fusion.5), channel_id=1, source_target_pairs={{0,64},{64,0},{128,192},{192,128},{1,65},{65,1},{129,193},{193,129... | collective-permute-start | bytes 221192 | tf_op jit(solution)/shard_map/ppermute | solution.py:382
  11.6 4.3 %collective-permute-start.2 = (bf16[288,128]{1,0:T(8,128)(2,1)S(1)}, bf16[288,128]{1,0:T(8,128)(2,1)S(1)}, u32[]{:S(2)}, u32[]{:S(2)}) collective-permute-start(bf16[288,128]{1,0:T(8,128)(2,1)S(1)} %pad_maximum_fusion.6), channel_id=1, source_target_pairs={{0,192},{64,128},{128,64},{192,0},{1,193},{65,129},{129,65},{193,1... | collective-permute-start | bytes 221192 | tf_op jit(solution)/shard_map/ppermute | solution.py:382
  15.9 0.1 pad_maximum_fusion.refs_4_.wo_ref
  16.1 2.4 %collective-permute-start.4 = (bf16[136,512]{1,0:T(8,128)(2,1)S(1)}, bf16[136,512]{1,0:T(8,128)(2,1)S(1)}, u32[]{:S(2)}, u32[]{:S(2)}) collective-permute-start(bf16[136,512]{1,0:T(8,128)(2,1)S(1)} %get-tuple-element.105.refs_0_.dy0_ref), channel_id=1, source_target_pairs={{0,2},{1,3},{2,0},{3,1},{4,6},{5,7},{6,4},{7,5},{8,10},{9,11},{10,... | collective-permute-start | bytes 417800 | tf_op jit(solution)/shard_map/ppermute | solution.py:378
  18.5 0.4 collective-permute-done.2
  18.9 1.6 %collective-permute-start.6 = (bf16[288,128]{1,0:T(8,128)(2,1)S(1)}, bf16[288,128]{1,0:T(8,128)(2,1)S(1)}, u32[]{:S(2)}, u32[]{:S(2)}) collective-permute-start(bf16[288,128]{1,0:T(8,128)(2,1)S(1)} %pad_maximum_fusion.7), channel_id=1, source_target_pairs={{0,8},{8,0},{16,24},{24,16},{1,9},{9,1},{17,25},{25,17},{2,10},{10... | collective-permute-start | bytes 221192 | tf_op jit(solution)/shard_map/ppermute | solution.py:382
  20.5 4.3 %collective-permute-start.7 = (bf16[576,128]{1,0:T(8,128)(2,1)S(1)}, bf16[576,128]{1,0:T(8,128)(2,1)S(1)}, u32[]{:S(2)}, u32[]{:S(2)}) collective-permute-start(bf16[576,128]{1,0:T(8,128)(2,1)S(1)} %pad_maximum_fusion.2), channel_id=1, source_target_pairs={{0,192},{64,128},{128,64},{192,0},{1,193},{65,129},{129,65},{193,1... | collective-permute-start | bytes 442376 | tf_op jit(solution)/shard_map/ppermute | solution.py:382
  24.9 0.9 collective-permute-start.8
  25.8 1.0 %dattn.1 = (bf16[144,128]{1,0:T(8,128)(2,1)S(1)}, bf16[144,128]{1,0:T(8,128)(2,1)S(1)}) custom-call(s32[5]{0:T(128)S(1)} %stack.23.at_ref, bf16[136,512]{1,0:T(8,128)(2,1)S(1)} %get-tuple-element.105.refs_0_.dy0_ref, bf16[136,512]{1,0:T(8,128)(2,1)S(1)} %collective-permute-done.3.refs_1_.dy1_ref, ...), custom_call_target="tpu_custom_call" | custom-call | tf_op jit(solution)/shard_map/dattn/pallas_call | solution.py:47
  26.8 2.2 %collective-permute-start.10 = (bf16[576,128]{1,0:T(8,128)(2,1)S(1)}, bf16[576,128]{1,0:T(8,128)(2,1)S(1)}, u32[]{:S(2)}, u32[]{:S(2)}) collective-permute-start(bf16[576,128]{1,0:T(8,128)(2,1)S(1)} %pad_maximum_fusion.4.refs_0_), channel_id=1, source_target_pairs={{0,24},{8,16},{16,8},{24,0},{1,25},{9,17},{17,9},{25,1},{2,26},{10... | collective-permute-start | bytes 442376 | tf_op jit(solution)/shard_map/ppermute | solution.py:382
  29.0 1.7 %collective-permute-start.9 = (bf16[144,128]{1,0:T(8,128)(2,1)S(1)}, bf16[144,128]{1,0:T(8,128)(2,1)S(1)}, u32[]{:S(2)}, u32[]{:S(2)}) collective-permute-start(bf16[144,128]{1,0:T(8,128)(2,1)S(1)} %get-tuple-element.113), channel_id=1, source_target_pairs={{0,32},{32,0},{1,33},{33,1},{2,34},{34,2},{3,35},{35,3},{4,36},{36... | collective-permute-start | bytes 110600 | tf_op jit(solution)/shard_map/ppermute | solution.py:382
  30.8 2.1 %collective-permute-done.9 = bf16[144,128]{1,0:T(8,128)(2,1)S(1)} collective-permute-done((bf16[144,128]{1,0:T(8,128)(2,1)S(1)}, bf16[144,128]{1,0:T(8,128)(2,1)S(1)}, u32[]{:S(2)}, u32[]{:S(2)}) %collective-permute-start.9) | collective-permute-done | bytes 36896 | tf_op jit(solution)/shard_map/ppermute | solution.py:382
  33.0 0.3 collective-permute-done.10.refs_1_
  33.3 0.1 collective-permute-start.15
  33.4 2.2 %collective-permute-start.13 = (bf16[288,128]{1,0:T(8,128)(2,1)S(1)}, bf16[288,128]{1,0:T(8,128)(2,1)S(1)}, u32[]{:S(2)}, u32[]{:S(2)}) collective-permute-start(bf16[288,128]{1,0:T(8,128)(2,1)S(1)} %constant_dynamic-update-slice_fusion.refs_0_), channel_id=1, source_target_pairs={{0,24},{8,16},{16,8},{24,0},{1,25},{9,17},{17,9},{25,1},{2,26},{10... | collective-permute-start | bytes 221192 | tf_op jit(solution)/shard_map/ppermute | solution.py:382
  35.6 0.3 collective-permute-start.12
  35.9 1.7 %collective-permute-start.11 = (bf16[288,128]{1,0:T(8,128)(2,1)S(1)}, bf16[288,128]{1,0:T(8,128)(2,1)S(1)}, u32[]{:S(2)}, u32[]{:S(2)}) collective-permute-start(bf16[288,128]{1,0:T(8,128)(2,1)S(1)} %constant_dynamic-update-slice_fusion.refs_0_), channel_id=1, source_target_pairs={{0,8},{8,0},{16,24},{24,16},{1,9},{9,1},{17,25},{25,17},{2,10},{10... | collective-permute-start | bytes 221192 | tf_op jit(solution)/shard_map/ppermute | solution.py:382
  37.6 5.0 %forward.1 = (f32[1152,128]{1,0:T(8,128)S(1)}, f32[8,1152]{1,0:T(8,128)S(1)}, bf16[1152,128]{1,0:T(8,128)(2,1)S(1)}, bf16[1152,128]{1,0:T(8,128)(2,1)S(1)}, bf16...) custom-call(bf16[576,128]{1,0:T(8,128)(2,1)S(1)} %pad_maximum_fusion.4.refs_0_, ...), custom_call_target="tpu_custom_call" | custom-call | flops 2038431744 | bytes 1048576 | tf_op jit(solution)/shard_map/forward/pallas_call | solution.py:47
  42.7 0.4 share.1
  43.1 0.4 collective-permute-start.16
  43.5 3.3 %collective-permute-start.17 = (bf16[368,128]{1,0:T(8,128)(2,1)S(1)}, bf16[368,128]{1,0:T(8,128)(2,1)S(1)}, u32[]{:S(2)}, u32[]{:S(2)}) collective-permute-start(bf16[368,128]{1,0:T(8,128)(2,1)S(1)} %get-tuple-element.123), channel_id=1, source_target_pairs={{0,16},{8,24},{16,0},{24,8},{1,17},{9,25},{17,1},{25,9},{2,18},{10... | collective-permute-start | bytes 282632 | tf_op jit(solution)/shard_map/ppermute | solution.py:382
  46.7 1.1 %collective-permute-start.18 = (bf16[368,128]{1,0:T(8,128)(2,1)S(1)}, bf16[368,128]{1,0:T(8,128)(2,1)S(1)}, u32[]{:S(2)}, u32[]{:S(2)}) collective-permute-start(bf16[368,128]{1,0:T(8,128)(2,1)S(1)} %get-tuple-element.124), channel_id=1, source_target_pairs={{0,24},{8,16},{16,8},{24,0},{1,25},{9,17},{17,9},{25,1},{2,26},{10... | collective-permute-start | bytes 282632 | tf_op jit(solution)/shard_map/ppermute | solution.py:382
  47.9 0.7 collective-permute-done.16.l1_ref
  48.5 2.6 %collective-permute-done.17.l2_ref = bf16[368,128]{1,0:T(8,128)(2,1)S(1)} collective-permute-done((bf16[368,128]{1,0:T(8,128)(2,1)S(1)}, bf16[368,128]{1,0:T(8,128)(2,1)S(1)}, u32[]{:S(2)}, u32[]{:S(2)}) %collective-permute-start.17) | collective-permute-done | bytes 94240 | tf_op jit(solution)/shard_map/ppermute | solution.py:382
  51.1 1.6 %collective-permute-done.18.l3_ref = bf16[368,128]{1,0:T(8,128)(2,1)S(1)} collective-permute-done((bf16[368,128]{1,0:T(8,128)(2,1)S(1)}, bf16[368,128]{1,0:T(8,128)(2,1)S(1)}, u32[]{:S(2)}, u32[]{:S(2)}) %collective-permute-start.18) | collective-permute-done | bytes 94240 | tf_op jit(solution)/shard_map/ppermute | solution.py:382
  52.7 0.9 merge.1
  53.6 1.8 %collective-permute-start.19 = (bf16[144,128]{1,0:T(8,128)(2,1)S(1)}, bf16[144,128]{1,0:T(8,128)(2,1)S(1)}, u32[]{:S(2)}, u32[]{:S(2)}) collective-permute-start(bf16[144,128]{1,0:T(8,128)(2,1)S(1)} %get-tuple-element.126), channel_id=1, source_target_pairs={{0,32},{32,0},{1,33},{33,1},{2,34},{34,2},{3,35},{35,3},{4,36},{36... | collective-permute-start | bytes 110600 | tf_op jit(solution)/shard_map/ppermute | solution.py:382
  55.4 2.8 %backward_one.1 = (bf16[768,256]{1,0:T(8,128)(2,1)S(1)}, f32[1152,128]{1,0:T(8,128)S(1)}) custom-call(bf16[1152,128]{1,0:T(8,128)(2,1)S(1)} %get-tuple-element.128.q_ref, bf16[1152,128]{1,0:T(8,128)(2,1)S(1)} %get-tuple-element.129.qm_ref, bf16[1152,128]{1,0:T(8,128)(2,1)S(1)} %get-tuple-element.130.da_ref, bf16[2304,256]{1,0:T(8,128)(2,1)S(1)} %get-tuple-element.131.kv_ref, ...), custom_call_target="tpu_custom_call" | custom-call | flops 1358954496 | bytes 1048576 | tf_op jit(solution)/shard_map/backward_one/pallas_call | solution.py:47
  58.2 1.2 %project.1 = (bf16[136,512]{1,0:T(8,128)(2,1)S(1)}, bf16[136,512]{1,0:T(8,128)(2,1)S(1)}, bf16[136,512]{1,0:T(8,128)(2,1)S(1)}, bf16[136,512]{1,0:T(8,128)(2,1)S...) custom-call(s32[5]{0:T(128)S(1)} %stack.23.at_ref, ...), custom_call_target="tpu_custom_call" | custom-call | tf_op jit(solution)/shard_map/project/pallas_call | solution.py:47
  59.4 0.3 collective-permute-start.20
  59.7 1.6 %backward_two.1 = (bf16[8,288,128]{2,1,0:T(8,128)(2,1)S(1)}, f32[1152,128]{1,0:T(8,128)S(1)}) custom-call(bf16[1152,128]{1,0:T(8,128)(2,1)S(1)} %get-tuple-element.128.q_ref, bf16[1152,128]{1,0:T(8,128)(2,1)S(1)} %get-tuple-element.129.qm_ref, bf16[1152,128]{1,0:T(8,128)(2,1)S(1)} %get-tuple-element.130.da_ref, ...), custom_call_target="tpu_custom_call" | custom-call | flops 679477248 | bytes 1048576 | tf_op jit(solution)/shard_map/backward_two/pallas_call | solution.py:47
  61.3 0.6 collective-permute-start.22
  61.9 0.1 dwo.1
  62.0 1.3 %collective-permute-start.21 = (bf16[512,256]{1,0:T(8,128)(2,1)S(1)}, bf16[512,256]{1,0:T(8,128)(2,1)S(1)}, u32[]{:S(2)}, u32[]{:S(2)}) collective-permute-start(bf16[512,256]{1,0:T(8,128)(2,1)S(1)} %get-tuple-element.147), channel_id=1, source_target_pairs={{0,24},{4,12},{8,16},{12,4},{16,8},{20,28},{24,0},{28,20},{1,25},{... | collective-permute-start | bytes 786440 | tf_op jit(solution)/shard_map/ppermute | solution.py:387
  63.2 4.1 %backward_three.1 = (bf16[8,288,128]{2,1,0:T(8,128)(2,1)S(1)}, f32[576,128]{1,0:T(8,128)S(1)}, bf16[576,128]{1,0:T(8,128)(2,1)S(1)}) custom-call(bf16[1152,128]{1,0:T(8,128)(2,1)S(1)} %get-tuple-element.128.q_ref, bf16[1152,128]{1,0:T(8,128)(2,1)S(1)} %get-tuple-element.129.qm_ref, bf16[1152,128]{1,0:T(8,128)(2,1)S(1)} %get-tuple-element.130.da_ref, ...), custom_call_target="tpu_custom_call" | custom-call | flops 2038431744 | bytes 1048576 | tf_op jit(solution)/shard_map/backward_three/pallas_call | solution.py:47
  67.5 0.2 core.1
  67.6 2.1 %collective-permute-start.24 = (bf16[576,128]{1,0:T(8,128)(2,1)S(1)}, bf16[576,128]{1,0:T(8,128)(2,1)S(1)}, u32[]{:S(2)}, u32[]{:S(2)}) collective-permute-start(bf16[576,128]{1,0:T(8,128)(2,1)S(1)} %get-tuple-element.153), channel_id=1, source_target_pairs={{0,192},{64,128},{128,64},{192,0},{1,193},{65,129},{129,65},{193,1... | collective-permute-start | bytes 442376 | tf_op jit(solution)/shard_map/ppermute | solution.py:382
  69.8 1.5 %collective-permute-start.23 = (bf16[576,128]{1,0:T(8,128)(2,1)S(1)}, bf16[576,128]{1,0:T(8,128)(2,1)S(1)}, u32[]{:S(2)}, u32[]{:S(2)}) collective-permute-start(bf16[576,128]{1,0:T(8,128)(2,1)S(1)} %get-tuple-element.152), channel_id=1, source_target_pairs={{0,64},{64,0},{128,192},{192,128},{1,65},{65,1},{129,193},{193,129... | collective-permute-start | bytes 442376 | tf_op jit(solution)/shard_map/ppermute | solution.py:382
  71.3 1.7 %collective-permute-start.27 = (bf16[136,512]{1,0:T(8,128)(2,1)S(1)}, bf16[136,512]{1,0:T(8,128)(2,1)S(1)}, u32[]{:S(2)}, u32[]{:S(2)}) collective-permute-start(bf16[136,512]{1,0:T(8,128)(2,1)S(1)} %get-tuple-element.161), channel_id=1, source_target_pairs={{0,1},{1,2},{2,3},{3,0},{4,5},{5,6},{6,7},{7,4},{8,9},{9,10},{10,1... | collective-permute-start | bytes 417800 | tf_op jit(solution)/shard_map/ppermute | solution.py:378
  73.0 0.4 collective-permute-start.28
  73.4 1.9 %collective-permute-start.26 = (bf16[256,256]{1,0:T(8,128)(2,1)S(1)}, bf16[256,256]{1,0:T(8,128)(2,1)S(1)}, u32[]{:S(2)}, u32[]{:S(2)}) collective-permute-start(bf16[256,256]{1,0:T(8,128)(2,1)S(1)} %get-tuple-element.160), channel_id=1, source_target_pairs={{0,8},{4,28},{8,0},{12,20},{16,24},{20,12},{24,16},{28,4},{1,9},{5... | collective-permute-start | bytes 393224 | tf_op jit(solution)/shard_map/ppermute | solution.py:387
  75.3 1.3 %collective-permute-done.24.refs_3_ = bf16[576,128]{1,0:T(8,128)(2,1)S(1)} collective-permute-done((bf16[576,128]{1,0:T(8,128)(2,1)S(1)}, bf16[576,128]{1,0:T(8,128)(2,1)S(1)}, u32[]{:S(2)}, u32[]{:S(2)}) %collective-permute-start.24) | collective-permute-done | bytes 147488 | tf_op jit(solution)/shard_map/ppermute | solution.py:382
  76.6 2.3 %collective-permute-start.29 = (bf16[136,512]{1,0:T(8,128)(2,1)S(1)}, bf16[136,512]{1,0:T(8,128)(2,1)S(1)}, u32[]{:S(2)}, u32[]{:S(2)}) collective-permute-start(bf16[136,512]{1,0:T(8,128)(2,1)S(1)} %get-tuple-element.164), channel_id=1, source_target_pairs={{0,2},{1,3},{2,0},{3,1},{4,6},{5,7},{6,4},{7,5},{8,10},{9,11},{10,... | collective-permute-start | bytes 417800 | tf_op jit(solution)/shard_map/ppermute | solution.py:378
  78.9 0.7 collective-permute-done.23.refs_1_
  79.6 4.0 %collective-permute-start.33 = (bf16[128,256]{1,0:T(8,128)(2,1)S(1)}, bf16[128,256]{1,0:T(8,128)(2,1)S(1)}, u32[]{:S(2)}, u32[]{:S(2)}) collective-permute-start(bf16[128,256]{1,0:T(8,128)(2,1)S(1)} %get-tuple-element.181), channel_id=1, source_target_pairs={{0,192},{64,128},{128,64},{192,0},{1,193},{65,129},{129,65},{193,1... | collective-permute-start | bytes 196616 | tf_op jit(solution)/shard_map/ppermute | solution.py:382
  83.7 1.2 %collective-permute-start.30 = (bf16[288,128]{1,0:T(8,128)(2,1)S(1)}, bf16[288,128]{1,0:T(8,128)(2,1)S(1)}, u32[]{:S(2)}, u32[]{:S(2)}) collective-permute-start(bf16[288,128]{1,0:T(8,128)(2,1)S(1)} %get-tuple-element.173), channel_id=1, source_target_pairs={{0,24},{8,16},{16,8},{24,0},{1,25},{9,17},{17,9},{25,1},{2,26},{10... | collective-permute-start | bytes 221192 | tf_op jit(solution)/shard_map/ppermute | solution.py:382
  84.9 0.3 collective-permute-start.31
  85.2 3.3 %collective-permute-start.32 = (bf16[288,128]{1,0:T(8,128)(2,1)S(1)}, bf16[288,128]{1,0:T(8,128)(2,1)S(1)}, u32[]{:S(2)}, u32[]{:S(2)}) collective-permute-start(bf16[288,128]{1,0:T(8,128)(2,1)S(1)} %get-tuple-element.177), channel_id=1, source_target_pairs={{0,64},{64,0},{128,192},{192,128},{1,65},{65,1},{129,193},{193,129... | collective-permute-start | bytes 221192 | tf_op jit(solution)/shard_map/ppermute | solution.py:382
  88.6 1.7 %collective-permute-start.34 = (bf16[64,256]{1,0:T(8,128)(2,1)S(1)}, bf16[64,256]{1,0:T(8,128)(2,1)S(1)}, u32[]{:S(2)}, u32[]{:S(2)}) collective-permute-start(bf16[64,256]{1,0:T(8,128)(2,1)S(1)} %get-tuple-element.183), channel_id=1, source_target_pairs={{0,64},{64,0},{128,192},{192,128},{1,65},{65,1},{129,193},{193,129... | collective-permute-start | bytes 98312 | tf_op jit(solution)/shard_map/ppermute | solution.py:382
  90.3 1.1 %collective-permute-done.31.refs_3_ = bf16[288,128]{1,0:T(8,128)(2,1)S(1)} collective-permute-done((bf16[288,128]{1,0:T(8,128)(2,1)S(1)}, bf16[288,128]{1,0:T(8,128)(2,1)S(1)}, u32[]{:S(2)}, u32[]{:S(2)}) %collective-permute-start.31) | collective-permute-done | bytes 73760 | tf_op jit(solution)/shard_map/ppermute | solution.py:382
  91.4 0.5 collective-permute-done.32.refs_5_
  91.9 1.6 %collective-permute-done.34.refs_7_ = bf16[64,256]{1,0:T(8,128)(2,1)S(1)} collective-permute-done((bf16[64,256]{1,0:T(8,128)(2,1)S(1)}, bf16[64,256]{1,0:T(8,128)(2,1)S(1)}, u32[]{:S(2)}, u32[]{:S(2)}) %collective-permute-start.34) | collective-permute-done | bytes 32800 | tf_op jit(solution)/shard_map/ppermute | solution.py:382
  93.5 1.3 %collective-permute-start.35 = (bf16[496,128]{1,0:T(8,128)(2,1)S(1)}, bf16[496,128]{1,0:T(8,128)(2,1)S(1)}, u32[]{:S(2)}, u32[]{:S(2)}) collective-permute-start(bf16[496,128]{1,0:T(8,128)(2,1)S(1)} %get-tuple-element.186), channel_id=1, source_target_pairs={{0,32},{32,0},{1,33},{33,1},{2,34},{34,2},{3,35},{35,3},{4,36},{36... | collective-permute-start | bytes 380936 | tf_op jit(solution)/shard_map/ppermute | solution.py:382
  94.8 0.7 add_convert_fusion
  95.5 3.0 %collective-permute-done.35.got_ref = bf16[496,128]{1,0:T(8,128)(2,1)S(1)} collective-permute-done((bf16[496,128]{1,0:T(8,128)(2,1)S(1)}, bf16[496,128]{1,0:T(8,128)(2,1)S(1)}, u32[]{:S(2)}, u32[]{:S(2)}) %collective-permute-start.35) | collective-permute-done | bytes 127008 | tf_op jit(solution)/shard_map/ppermute | solution.py:382
  98.5 1.3 %place.1 = (bf16[136,256]{1,0:T(8,128)(2,1)}, bf16[136,256]{1,0:T(8,128)(2,1)}, bf16[136,256]{1,0:T(8,128)(2,1)}, f32[32,256]{1,0:T(8,128)}) custom-call(s32[5]{0:T(128)S(1)} %stack.23.at_ref, bf16[144,384]{1,0:T(8,128)(2,1)S(1)} %get-tuple-element.184.mine_ref, f32[32,256]{1,0:T(8,128)S(1)} %get-tuple-element.185.wmine_ref, ...), custom_call_target="tpu_custom_call" | custom-call | tf_op jit(solution)/shard_map/place/pallas_call | solution.py:47
  (49 shorter events, 0.8 us)
Async XLA Ops:
  0.6 6.6 %copy-start = (bf16[256,2048]{1,0:T(8,128)(2,1)S(1)}, bf16[256,2048]{1,0:T(8,128)(2,1)}, u32[]{:S(2)}) copy-start(bf16[256,2048]{1,0:T(8,128)(2,1)} %param.10) | copy-start | bytes 3145732
  3.2 5.1 %collective-permute-start = (bf16[432,128]{1,0:T(8,128)(2,1)S(1)}, bf16[432,128]{1,0:T(8,128)(2,1)S(1)}, u32[]{:S(2)}, u32[]{:S(2)}) collective-permute-start(bf16[432,128]{1,0:T(8,128)(2,1)S(1)} %get-tuple-element.99), channel_id=1, source_target_pairs={{0,32},{32,0},{1,33},{33,1},{2,34},{34,2},{3,35},{35,3},{4,36},{36... | collective-permute-start | bytes 331784 | tf_op jit(solution)/shard_map/ppermute | solution.py:382
  5.2 19.7 %collective-permute-start.5 = (bf16[136,512]{1,0:T(8,128)(2,1)S(1)}, bf16[136,512]{1,0:T(8,128)(2,1)S(1)}, u32[]{:S(2)}, u32[]{:S(2)}) collective-permute-start(bf16[136,512]{1,0:T(8,128)(2,1)S(1)} %get-tuple-element.105.refs_0_.dy0_ref), channel_id=1, source_target_pairs={{0,3},{1,0},{2,1},{3,2},{4,7},{5,4},{6,5},{7,6},{8,11},{9,8},{10,9... | collective-permute-start | bytes 417800 | tf_op jit(solution)/shard_map/ppermute | solution.py:378
  5.6 20.1 %collective-permute-start.3 = (bf16[136,512]{1,0:T(8,128)(2,1)S(1)}, bf16[136,512]{1,0:T(8,128)(2,1)S(1)}, u32[]{:S(2)}, u32[]{:S(2)}) collective-permute-start(bf16[136,512]{1,0:T(8,128)(2,1)S(1)} %get-tuple-element.105.refs_0_.dy0_ref), channel_id=1, source_target_pairs={{0,1},{1,2},{2,3},{3,0},{4,5},{5,6},{6,7},{7,4},{8,9},{9,10},{10,1... | collective-permute-start | bytes 417800 | tf_op jit(solution)/shard_map/ppermute | solution.py:378
  8.3 10.2 %collective-permute-start.1 = (bf16[288,128]{1,0:T(8,128)(2,1)S(1)}, bf16[288,128]{1,0:T(8,128)(2,1)S(1)}, u32[]{:S(2)}, u32[]{:S(2)}) collective-permute-start(bf16[288,128]{1,0:T(8,128)(2,1)S(1)} %pad_maximum_fusion.5), channel_id=1, source_target_pairs={{0,64},{64,0},{128,192},{192,128},{1,65},{65,1},{129,193},{193,129... | collective-permute-start | bytes 221192 | tf_op jit(solution)/shard_map/ppermute | solution.py:382
  11.6 7.2 %collective-permute-start.2 = (bf16[288,128]{1,0:T(8,128)(2,1)S(1)}, bf16[288,128]{1,0:T(8,128)(2,1)S(1)}, u32[]{:S(2)}, u32[]{:S(2)}) collective-permute-start(bf16[288,128]{1,0:T(8,128)(2,1)S(1)} %pad_maximum_fusion.6), channel_id=1, source_target_pairs={{0,192},{64,128},{128,64},{192,0},{1,193},{65,129},{129,65},{193,1... | collective-permute-start | bytes 221192 | tf_op jit(solution)/shard_map/ppermute | solution.py:382
  16.1 9.7 %collective-permute-start.4 = (bf16[136,512]{1,0:T(8,128)(2,1)S(1)}, bf16[136,512]{1,0:T(8,128)(2,1)S(1)}, u32[]{:S(2)}, u32[]{:S(2)}) collective-permute-start(bf16[136,512]{1,0:T(8,128)(2,1)S(1)} %get-tuple-element.105.refs_0_.dy0_ref), channel_id=1, source_target_pairs={{0,2},{1,3},{2,0},{3,1},{4,6},{5,7},{6,4},{7,5},{8,10},{9,11},{10,... | collective-permute-start | bytes 417800 | tf_op jit(solution)/shard_map/ppermute | solution.py:378
  18.9 6.8 %collective-permute-start.6 = (bf16[288,128]{1,0:T(8,128)(2,1)S(1)}, bf16[288,128]{1,0:T(8,128)(2,1)S(1)}, u32[]{:S(2)}, u32[]{:S(2)}) collective-permute-start(bf16[288,128]{1,0:T(8,128)(2,1)S(1)} %pad_maximum_fusion.7), channel_id=1, source_target_pairs={{0,8},{8,0},{16,24},{24,16},{1,9},{9,1},{17,25},{25,17},{2,10},{10... | collective-permute-start | bytes 221192 | tf_op jit(solution)/shard_map/ppermute | solution.py:382
  20.5 12.5 %collective-permute-start.7 = (bf16[576,128]{1,0:T(8,128)(2,1)S(1)}, bf16[576,128]{1,0:T(8,128)(2,1)S(1)}, u32[]{:S(2)}, u32[]{:S(2)}) collective-permute-start(bf16[576,128]{1,0:T(8,128)(2,1)S(1)} %pad_maximum_fusion.2), channel_id=1, source_target_pairs={{0,192},{64,128},{128,64},{192,0},{1,193},{65,129},{129,65},{193,1... | collective-permute-start | bytes 442376 | tf_op jit(solution)/shard_map/ppermute | solution.py:382
  24.9 8.1 %collective-permute-start.8 = (bf16[576,128]{1,0:T(8,128)(2,1)S(1)}, bf16[576,128]{1,0:T(8,128)(2,1)S(1)}, u32[]{:S(2)}, u32[]{:S(2)}) collective-permute-start(bf16[576,128]{1,0:T(8,128)(2,1)S(1)} %pad_maximum_fusion.3), channel_id=1, source_target_pairs={{0,64},{64,0},{128,192},{192,128},{1,65},{65,1},{129,193},{193,129... | collective-permute-start | bytes 442376 | tf_op jit(solution)/shard_map/ppermute | solution.py:382
  26.8 6.4 %collective-permute-start.10 = (bf16[576,128]{1,0:T(8,128)(2,1)S(1)}, bf16[576,128]{1,0:T(8,128)(2,1)S(1)}, u32[]{:S(2)}, u32[]{:S(2)}) collective-permute-start(bf16[576,128]{1,0:T(8,128)(2,1)S(1)} %pad_maximum_fusion.4.refs_0_), channel_id=1, source_target_pairs={{0,24},{8,16},{16,8},{24,0},{1,25},{9,17},{17,9},{25,1},{2,26},{10... | collective-permute-start | bytes 442376 | tf_op jit(solution)/shard_map/ppermute | solution.py:382
  29.0 4.0 %collective-permute-start.9 = (bf16[144,128]{1,0:T(8,128)(2,1)S(1)}, bf16[144,128]{1,0:T(8,128)(2,1)S(1)}, u32[]{:S(2)}, u32[]{:S(2)}) collective-permute-start(bf16[144,128]{1,0:T(8,128)(2,1)S(1)} %get-tuple-element.113), channel_id=1, source_target_pairs={{0,32},{32,0},{1,33},{33,1},{2,34},{34,2},{3,35},{35,3},{4,36},{36... | collective-permute-start | bytes 110600 | tf_op jit(solution)/shard_map/ppermute | solution.py:382
  30.7 6.9 %collective-permute-start.14 = (bf16[1152,128]{1,0:T(8,128)(2,1)S(1)}, bf16[1152,128]{1,0:T(8,128)(2,1)S(1)}, u32[]{:S(2)}, u32[]{:S(2)}) collective-permute-start(bf16[1152,128]{1,0:T(8,128)(2,1)S(1)} %constant_dynamic-update-slice_fusion.2.refs_2_), channel_id=1, source_target_pairs={{0,4},{4,0},{1,5},{5,1},{2,6},{6,2},{3,7},{7,3},{8,12},{12,8},{9,1... | collective-permute-start | bytes 884744 | tf_op jit(solution)/shard_map/ppermute | solution.py:382
  33.3 4.3 %collective-permute-start.15 = (bf16[1152,128]{1,0:T(8,128)(2,1)S(1)}, bf16[1152,128]{1,0:T(8,128)(2,1)S(1)}, u32[]{:S(2)}, u32[]{:S(2)}) collective-permute-start(bf16[1152,128]{1,0:T(8,128)(2,1)S(1)} %constant_dynamic-update-slice_fusion.8.refs_3_), channel_id=1, source_target_pairs={{0,4},{4,0},{1,5},{5,1},{2,6},{6,2},{3,7},{7,3},{8,12},{12,8},{9,1... | collective-permute-start | bytes 884744 | tf_op jit(solution)/shard_map/ppermute | solution.py:382
  33.4 9.2 %collective-permute-start.13 = (bf16[288,128]{1,0:T(8,128)(2,1)S(1)}, bf16[288,128]{1,0:T(8,128)(2,1)S(1)}, u32[]{:S(2)}, u32[]{:S(2)}) collective-permute-start(bf16[288,128]{1,0:T(8,128)(2,1)S(1)} %constant_dynamic-update-slice_fusion.refs_0_), channel_id=1, source_target_pairs={{0,24},{8,16},{16,8},{24,0},{1,25},{9,17},{17,9},{25,1},{2,26},{10... | collective-permute-start | bytes 221192 | tf_op jit(solution)/shard_map/ppermute | solution.py:382
  35.6 7.0 %collective-permute-start.12 = (bf16[288,128]{1,0:T(8,128)(2,1)S(1)}, bf16[288,128]{1,0:T(8,128)(2,1)S(1)}, u32[]{:S(2)}, u32[]{:S(2)}) collective-permute-start(bf16[288,128]{1,0:T(8,128)(2,1)S(1)} %constant_dynamic-update-slice_fusion.refs_0_), channel_id=1, source_target_pairs={{0,16},{8,24},{16,0},{24,8},{1,17},{9,25},{17,1},{25,9},{2,18},{10... | collective-permute-start | bytes 221192 | tf_op jit(solution)/shard_map/ppermute | solution.py:382
  35.9 6.8 %collective-permute-start.11 = (bf16[288,128]{1,0:T(8,128)(2,1)S(1)}, bf16[288,128]{1,0:T(8,128)(2,1)S(1)}, u32[]{:S(2)}, u32[]{:S(2)}) collective-permute-start(bf16[288,128]{1,0:T(8,128)(2,1)S(1)} %constant_dynamic-update-slice_fusion.refs_0_), channel_id=1, source_target_pairs={{0,8},{8,0},{16,24},{24,16},{1,9},{9,1},{17,25},{25,17},{2,10},{10... | collective-permute-start | bytes 221192 | tf_op jit(solution)/shard_map/ppermute | solution.py:382
  43.1 5.4 %collective-permute-start.16 = (bf16[368,128]{1,0:T(8,128)(2,1)S(1)}, bf16[368,128]{1,0:T(8,128)(2,1)S(1)}, u32[]{:S(2)}, u32[]{:S(2)}) collective-permute-start(bf16[368,128]{1,0:T(8,128)(2,1)S(1)} %get-tuple-element.122), channel_id=1, source_target_pairs={{0,8},{8,0},{16,24},{24,16},{1,9},{9,1},{17,25},{25,17},{2,10},{10... | collective-permute-start | bytes 282632 | tf_op jit(solution)/shard_map/ppermute | solution.py:382
  43.5 7.6 %collective-permute-start.17 = (bf16[368,128]{1,0:T(8,128)(2,1)S(1)}, bf16[368,128]{1,0:T(8,128)(2,1)S(1)}, u32[]{:S(2)}, u32[]{:S(2)}) collective-permute-start(bf16[368,128]{1,0:T(8,128)(2,1)S(1)} %get-tuple-element.123), channel_id=1, source_target_pairs={{0,16},{8,24},{16,0},{24,8},{1,17},{9,25},{17,1},{25,9},{2,18},{10... | collective-permute-start | bytes 282632 | tf_op jit(solution)/shard_map/ppermute | solution.py:382
  46.7 5.9 %collective-permute-start.18 = (bf16[368,128]{1,0:T(8,128)(2,1)S(1)}, bf16[368,128]{1,0:T(8,128)(2,1)S(1)}, u32[]{:S(2)}, u32[]{:S(2)}) collective-permute-start(bf16[368,128]{1,0:T(8,128)(2,1)S(1)} %get-tuple-element.124), channel_id=1, source_target_pairs={{0,24},{8,16},{16,8},{24,0},{1,25},{9,17},{17,9},{25,1},{2,26},{10... | collective-permute-start | bytes 282632 | tf_op jit(solution)/shard_map/ppermute | solution.py:382
  53.6 4.6 %collective-permute-start.19 = (bf16[144,128]{1,0:T(8,128)(2,1)S(1)}, bf16[144,128]{1,0:T(8,128)(2,1)S(1)}, u32[]{:S(2)}, u32[]{:S(2)}) collective-permute-start(bf16[144,128]{1,0:T(8,128)(2,1)S(1)} %get-tuple-element.126), channel_id=1, source_target_pairs={{0,32},{32,0},{1,33},{33,1},{2,34},{34,2},{3,35},{35,3},{4,36},{36... | collective-permute-start | bytes 110600 | tf_op jit(solution)/shard_map/ppermute | solution.py:382
  59.4 2.5 %collective-permute-start.20 = (bf16[4,256,256]{2,1,0:T(8,128)(2,1)S(1)}, bf16[4,256,256]{2,1,0:T(8,128)(2,1)S(1)}, u32[]{:S(2)}, u32[]{:S(2)}) collective-permute-start(bf16[4,256,256]{2,1,0:T(8,128)(2,1)S(1)} %get-tuple-element.140), channel_id=1, source_target_pairs={{0,4},{4,0},{1,5},{5,1},{2,6},{6,2},{3,7},{7,3},{8,12},{12,8},{9,1... | collective-permute-start | bytes 1572872 | tf_op jit(solution)/shard_map/ppermute | solution.py:382
  61.3 6.2 %collective-permute-start.22 = (bf16[8,288,128]{2,1,0:T(8,128)(2,1)S(1)}, bf16[8,288,128]{2,1,0:T(8,128)(2,1)S(1)}, u32[]{:S(2)}, u32[]{:S(2)}) collective-permute-start(bf16[8,288,128]{2,1,0:T(8,128)(2,1)S(1)} %get-tuple-element.150), channel_id=1, source_target_pairs={{0,4},{4,0},{1,5},{5,1},{2,6},{6,2},{3,7},{7,3},{8,12},{12,8},{9,1... | collective-permute-start | bytes 1769480 | tf_op jit(solution)/shard_map/ppermute | solution.py:382
  62.0 7.8 %collective-permute-start.21 = (bf16[512,256]{1,0:T(8,128)(2,1)S(1)}, bf16[512,256]{1,0:T(8,128)(2,1)S(1)}, u32[]{:S(2)}, u32[]{:S(2)}) collective-permute-start(bf16[512,256]{1,0:T(8,128)(2,1)S(1)} %get-tuple-element.147), channel_id=1, source_target_pairs={{0,24},{4,12},{8,16},{12,4},{16,8},{20,28},{24,0},{28,20},{1,25},{... | collective-permute-start | bytes 786440 | tf_op jit(solution)/shard_map/ppermute | solution.py:387
  67.4 6.0 %collective-permute-start.25 = (bf16[576,128]{1,0:T(8,128)(2,1)S(1)}, bf16[576,128]{1,0:T(8,128)(2,1)S(1)}, u32[]{:S(2)}, u32[]{:S(2)}) collective-permute-start(bf16[576,128]{1,0:T(8,128)(2,1)S(1)} %get-tuple-element.154), channel_id=1, source_target_pairs={{0,8},{8,0},{16,24},{24,16},{1,9},{9,1},{17,25},{25,17},{2,10},{10... | collective-permute-start | bytes 442376 | tf_op jit(solution)/shard_map/ppermute | solution.py:382
  67.6 9.0 %collective-permute-start.24 = (bf16[576,128]{1,0:T(8,128)(2,1)S(1)}, bf16[576,128]{1,0:T(8,128)(2,1)S(1)}, u32[]{:S(2)}, u32[]{:S(2)}) collective-permute-start(bf16[576,128]{1,0:T(8,128)(2,1)S(1)} %get-tuple-element.153), channel_id=1, source_target_pairs={{0,192},{64,128},{128,64},{192,0},{1,193},{65,129},{129,65},{193,1... | collective-permute-start | bytes 442376 | tf_op jit(solution)/shard_map/ppermute | solution.py:382
  69.8 9.8 %collective-permute-start.23 = (bf16[576,128]{1,0:T(8,128)(2,1)S(1)}, bf16[576,128]{1,0:T(8,128)(2,1)S(1)}, u32[]{:S(2)}, u32[]{:S(2)}) collective-permute-start(bf16[576,128]{1,0:T(8,128)(2,1)S(1)} %get-tuple-element.152), channel_id=1, source_target_pairs={{0,64},{64,0},{128,192},{192,128},{1,65},{65,1},{129,193},{193,129... | collective-permute-start | bytes 442376 | tf_op jit(solution)/shard_map/ppermute | solution.py:382
  71.3 7.6 %collective-permute-start.27 = (bf16[136,512]{1,0:T(8,128)(2,1)S(1)}, bf16[136,512]{1,0:T(8,128)(2,1)S(1)}, u32[]{:S(2)}, u32[]{:S(2)}) collective-permute-start(bf16[136,512]{1,0:T(8,128)(2,1)S(1)} %get-tuple-element.161), channel_id=1, source_target_pairs={{0,1},{1,2},{2,3},{3,0},{4,5},{5,6},{6,7},{7,4},{8,9},{9,10},{10,1... | collective-permute-start | bytes 417800 | tf_op jit(solution)/shard_map/ppermute | solution.py:378
  73.0 6.0 %collective-permute-start.28 = (bf16[136,512]{1,0:T(8,128)(2,1)S(1)}, bf16[136,512]{1,0:T(8,128)(2,1)S(1)}, u32[]{:S(2)}, u32[]{:S(2)}) collective-permute-start(bf16[136,512]{1,0:T(8,128)(2,1)S(1)} %get-tuple-element.162), channel_id=1, source_target_pairs={{0,3},{1,0},{2,1},{3,2},{4,7},{5,4},{6,5},{7,6},{8,11},{9,8},{10,9... | collective-permute-start | bytes 417800 | tf_op jit(solution)/shard_map/ppermute | solution.py:378
  73.4 5.5 %collective-permute-start.26 = (bf16[256,256]{1,0:T(8,128)(2,1)S(1)}, bf16[256,256]{1,0:T(8,128)(2,1)S(1)}, u32[]{:S(2)}, u32[]{:S(2)}) collective-permute-start(bf16[256,256]{1,0:T(8,128)(2,1)S(1)} %get-tuple-element.160), channel_id=1, source_target_pairs={{0,8},{4,28},{8,0},{12,20},{16,24},{20,12},{24,16},{28,4},{1,9},{5... | collective-permute-start | bytes 393224 | tf_op jit(solution)/shard_map/ppermute | solution.py:387
  76.6 18.2 %collective-permute-start.29 = (bf16[136,512]{1,0:T(8,128)(2,1)S(1)}, bf16[136,512]{1,0:T(8,128)(2,1)S(1)}, u32[]{:S(2)}, u32[]{:S(2)}) collective-permute-start(bf16[136,512]{1,0:T(8,128)(2,1)S(1)} %get-tuple-element.164), channel_id=1, source_target_pairs={{0,2},{1,3},{2,0},{3,1},{4,6},{5,7},{6,4},{7,5},{8,10},{9,11},{10,... | collective-permute-start | bytes 417800 | tf_op jit(solution)/shard_map/ppermute | solution.py:378
  79.6 8.9 %collective-permute-start.33 = (bf16[128,256]{1,0:T(8,128)(2,1)S(1)}, bf16[128,256]{1,0:T(8,128)(2,1)S(1)}, u32[]{:S(2)}, u32[]{:S(2)}) collective-permute-start(bf16[128,256]{1,0:T(8,128)(2,1)S(1)} %get-tuple-element.181), channel_id=1, source_target_pairs={{0,192},{64,128},{128,64},{192,0},{1,193},{65,129},{129,65},{193,1... | collective-permute-start | bytes 196616 | tf_op jit(solution)/shard_map/ppermute | solution.py:382
  83.7 6.6 %collective-permute-start.30 = (bf16[288,128]{1,0:T(8,128)(2,1)S(1)}, bf16[288,128]{1,0:T(8,128)(2,1)S(1)}, u32[]{:S(2)}, u32[]{:S(2)}) collective-permute-start(bf16[288,128]{1,0:T(8,128)(2,1)S(1)} %get-tuple-element.173), channel_id=1, source_target_pairs={{0,24},{8,16},{16,8},{24,0},{1,25},{9,17},{17,9},{25,1},{2,26},{10... | collective-permute-start | bytes 221192 | tf_op jit(solution)/shard_map/ppermute | solution.py:382
  84.9 6.5 %collective-permute-start.31 = (bf16[288,128]{1,0:T(8,128)(2,1)S(1)}, bf16[288,128]{1,0:T(8,128)(2,1)S(1)}, u32[]{:S(2)}, u32[]{:S(2)}) collective-permute-start(bf16[288,128]{1,0:T(8,128)(2,1)S(1)} %get-tuple-element.175), channel_id=1, source_target_pairs={{0,192},{64,128},{128,64},{192,0},{1,193},{65,129},{129,65},{193,1... | collective-permute-start | bytes 221192 | tf_op jit(solution)/shard_map/ppermute | solution.py:382
  85.2 6.7 %collective-permute-start.32 = (bf16[288,128]{1,0:T(8,128)(2,1)S(1)}, bf16[288,128]{1,0:T(8,128)(2,1)S(1)}, u32[]{:S(2)}, u32[]{:S(2)}) collective-permute-start(bf16[288,128]{1,0:T(8,128)(2,1)S(1)} %get-tuple-element.177), channel_id=1, source_target_pairs={{0,64},{64,0},{128,192},{192,128},{1,65},{65,1},{129,193},{193,129... | collective-permute-start | bytes 221192 | tf_op jit(solution)/shard_map/ppermute | solution.py:382
  88.6 4.9 %collective-permute-start.34 = (bf16[64,256]{1,0:T(8,128)(2,1)S(1)}, bf16[64,256]{1,0:T(8,128)(2,1)S(1)}, u32[]{:S(2)}, u32[]{:S(2)}) collective-permute-start(bf16[64,256]{1,0:T(8,128)(2,1)S(1)} %get-tuple-element.183), channel_id=1, source_target_pairs={{0,64},{64,0},{128,192},{192,128},{1,65},{65,1},{129,193},{193,129... | collective-permute-start | bytes 98312 | tf_op jit(solution)/shard_map/ppermute | solution.py:382
  93.5 5.0 %collective-permute-start.35 = (bf16[496,128]{1,0:T(8,128)(2,1)S(1)}, bf16[496,128]{1,0:T(8,128)(2,1)S(1)}, u32[]{:S(2)}, u32[]{:S(2)}) collective-permute-start(bf16[496,128]{1,0:T(8,128)(2,1)S(1)} %get-tuple-element.186), channel_id=1, source_target_pairs={{0,32},{32,0},{1,33},{33,1},{2,34},{34,2},{3,35},{35,3},{4,36},{36... | collective-permute-start | bytes 380936 | tf_op jit(solution)/shard_map/ppermute | solution.py:382

commit v5 on v4

--- a/solution.py
+++ b/solution.py
@@ -511,10 +511,11 @@
         [dk_keep, dk_got, dv_keep, dv_got, dq_keep, dq_got],
         [shape(pair, F32), shape(pair)] * 3,
     )
-    wgot, dq_got = swapped(wsend, "zr", 4, 3), swapped(dq_send, "x", 4, 3)
+    wgot, out_two = lax.optimization_barrier((swapped(wsend, "zr", 4, 3), shifted(outs[2], "head", NH, 2)))
     dk_got, dv_got = swapped(dk_send, "zr", 4, 3), swapped(dv_send, "zr", 4, 1)
     wkeep, wsend = call(half_kernel, "half", [wkeep, wgot], [shape((64, FEATS), F32), shape((64, FEATS))])
-    out_two = shifted(outs[2], "head", NH, 2)
+    wsend, dq_send = lax.optimization_barrier((wsend, dq_send))
+    dq_got = swapped(dq_send, "x", 4, 3)
     block_out = sum(one.astype(F32) for one in (outs[0], out_one, out_two, out_three)).astype(BF16)
     keep, wkeep, send = call(
         total_kernel,

time: 100 us -> 102 us (1.020)
  starting transfers between devices: 59.6 us -> 62.9 us
  waiting for transfers between devices: 16.7 us -> 14.6 us
    ppermute x28, starting transfers between devices: 47.7 us -> 50.9 us  [swapped(): return lax.ppermute(value, axis, [(i, i ^ mask) for i in range(size)])]
    ppermute x28, waiting for transfers between devices: 16.7 us -> 14.6 us  [swapped(): return lax.ppermute(value, axis, [(i, i ^ mask) for i in range(size)])]
  transfers between devices with their start and end apart: 36 -> 36, of which waited for: 13 -> 11; matrix products, arithmetic and copies ran while one was open for 1% -> 1% of each run, Pallas kernels for 15% -> 15%
where the time goes in v5:
time: 102 us; the launch traced here: 101 us
  starting transfers between devices  62.9 us (62%)
  Pallas kernels  19.4 us (19%)
  waiting for transfers between devices  14.6 us (14%)
  other arithmetic  2.73 us (3%)
    ppermute x28, starting transfers between devices, swapped(): return lax.ppermute(value, axis, [(i, i ^ mask) for i in range(size)])  50.9 us
    pallas_call x17, Pallas kernels, call(): pl.pallas_call(kernel, in_specs=[SMEM] * scalars + [VMEM] * (len(ins) - s...  19.4 us
    ppermute x28, waiting for transfers between devices, swapped(): return lax.ppermute(value, axis, [(i, i ^ mask) for i in range(size)])  14.6 us
    ppermute x6, starting transfers between devices, shifted(): lax.ppermute(value, axis, [(i, (i + by) % size) for i in range(size)])  8.81 us
    ppermute x2, starting transfers between devices, by_core(): lax.ppermute(value, (axis, 'c'), [(i, (i // 2 ^ masks[i % 2]) * 2 + i % 2...  3.14 us
  transfers between devices with their start and end apart: 36, of which 11 were waited for; matrix products, arithmetic and copies ran while one was open for 1% of the time, Pallas kernels for 15%

profile of v5, /device:TPU:8, one launch (start us, length us, event | category | flops | bytes accessed | tf_op | source)
XLA Modules:
  0.0 100.9 jit_solution(16423339575473833684)
XLA Ops:
  0.6 0.8 convert_bitcast_fusion.ids_ref.refs_5_
  1.4 1.0 %pad_maximum_fusion.1.all_ref = bf16[136,1280]{1,0:T(8,128)(2,1)S(1)} fusion(bf16[136,512]{1,0:T(8,128)(2,1)} %param.11, bf16[136,256]{1,0:T(8,128)(2,1)} %param.8, bf16[136,256]{1,0:T(8,128)(2,1)} %param.7, bf16[136,256]{1,0:T(8,128)(2,1)} %param.6), kind=kLoop, calls=%fused_computation.1 | loop fusion | flops 1392640 | bytes 696320 | tf_op jit(solution)/shard_map/concatenate | solution.py:403
  2.6 0.6 pack.1
  3.2 2.0 %collective-permute-start = (bf16[432,128]{1,0:T(8,128)(2,1)S(1)}, bf16[432,128]{1,0:T(8,128)(2,1)S(1)}, u32[]{:S(2)}, u32[]{:S(2)}) collective-permute-start(bf16[432,128]{1,0:T(8,128)(2,1)S(1)} %get-tuple-element.103), channel_id=1, source_target_pairs={{0,32},{32,0},{1,33},{33,1},{2,34},{34,2},{3,35},{35,3},{4,36},{36... | collective-permute-start | bytes 331784 | tf_op jit(solution)/shard_map/ppermute | solution.py:382
  5.2 0.4 collective-permute-start.5
  5.6 1.6 %collective-permute-start.3 = (bf16[136,512]{1,0:T(8,128)(2,1)S(1)}, bf16[136,512]{1,0:T(8,128)(2,1)S(1)}, u32[]{:S(2)}, u32[]{:S(2)}) collective-permute-start(bf16[136,512]{1,0:T(8,128)(2,1)S(1)} %get-tuple-element.109.refs_0_.dy0_ref), channel_id=1, source_target_pairs={{0,1},{1,2},{2,3},{3,0},{4,5},{5,6},{6,7},{7,4},{8,9},{9,10},{10,1... | collective-permute-start | bytes 417800 | tf_op jit(solution)/shard_map/ppermute | solution.py:378
  7.2 0.1 constant_dynamic-slice_fusion.3
  7.4 0.9 collective-permute-done
  8.3 3.4 %collective-permute-start.1 = (bf16[288,128]{1,0:T(8,128)(2,1)S(1)}, bf16[288,128]{1,0:T(8,128)(2,1)S(1)}, u32[]{:S(2)}, u32[]{:S(2)}) collective-permute-start(bf16[288,128]{1,0:T(8,128)(2,1)S(1)} %pad_maximum_fusion.5), channel_id=1, source_target_pairs={{0,64},{64,0},{128,192},{192,128},{1,65},{65,1},{129,193},{193,129... | collective-permute-start | bytes 221192 | tf_op jit(solution)/shard_map/ppermute | solution.py:382
  11.6 4.3 %collective-permute-start.2 = (bf16[288,128]{1,0:T(8,128)(2,1)S(1)}, bf16[288,128]{1,0:T(8,128)(2,1)S(1)}, u32[]{:S(2)}, u32[]{:S(2)}) collective-permute-start(bf16[288,128]{1,0:T(8,128)(2,1)S(1)} %pad_maximum_fusion.6), channel_id=1, source_target_pairs={{0,192},{64,128},{128,64},{192,0},{1,193},{65,129},{129,65},{193,1... | collective-permute-start | bytes 221192 | tf_op jit(solution)/shard_map/ppermute | solution.py:382
  15.9 0.1 pad_maximum_fusion.refs_4_.wo_ref
  16.1 2.4 %collective-permute-start.4 = (bf16[136,512]{1,0:T(8,128)(2,1)S(1)}, bf16[136,512]{1,0:T(8,128)(2,1)S(1)}, u32[]{:S(2)}, u32[]{:S(2)}) collective-permute-start(bf16[136,512]{1,0:T(8,128)(2,1)S(1)} %get-tuple-element.109.refs_0_.dy0_ref), channel_id=1, source_target_pairs={{0,2},{1,3},{2,0},{3,1},{4,6},{5,7},{6,4},{7,5},{8,10},{9,11},{10,... | collective-permute-start | bytes 417800 | tf_op jit(solution)/shard_map/ppermute | solution.py:378
  18.5 0.4 collective-permute-done.2
  18.9 1.6 %collective-permute-start.6 = (bf16[288,128]{1,0:T(8,128)(2,1)S(1)}, bf16[288,128]{1,0:T(8,128)(2,1)S(1)}, u32[]{:S(2)}, u32[]{:S(2)}) collective-permute-start(bf16[288,128]{1,0:T(8,128)(2,1)S(1)} %pad_maximum_fusion.7), channel_id=1, source_target_pairs={{0,8},{8,0},{16,24},{24,16},{1,9},{9,1},{17,25},{25,17},{2,10},{10... | collective-permute-start | bytes 221192 | tf_op jit(solution)/shard_map/ppermute | solution.py:382
  20.5 4.3 %collective-permute-start.7 = (bf16[576,128]{1,0:T(8,128)(2,1)S(1)}, bf16[576,128]{1,0:T(8,128)(2,1)S(1)}, u32[]{:S(2)}, u32[]{:S(2)}) collective-permute-start(bf16[576,128]{1,0:T(8,128)(2,1)S(1)} %pad_maximum_fusion.2), channel_id=1, source_target_pairs={{0,192},{64,128},{128,64},{192,0},{1,193},{65,129},{129,65},{193,1... | collective-permute-start | bytes 442376 | tf_op jit(solution)/shard_map/ppermute | solution.py:382
  24.9 0.9 collective-permute-start.8
  25.8 1.0 %dattn.1 = (bf16[144,128]{1,0:T(8,128)(2,1)S(1)}, bf16[144,128]{1,0:T(8,128)(2,1)S(1)}) custom-call(s32[5]{0:T(128)S(1)} %stack.23.at_ref, bf16[136,512]{1,0:T(8,128)(2,1)S(1)} %get-tuple-element.109.refs_0_.dy0_ref, bf16[136,512]{1,0:T(8,128)(2,1)S(1)} %collective-permute-done.3.refs_1_.dy1_ref, ...), custom_call_target="tpu_custom_call" | custom-call | tf_op jit(solution)/shard_map/dattn/pallas_call | solution.py:47
  26.8 2.2 %collective-permute-start.10 = (bf16[576,128]{1,0:T(8,128)(2,1)S(1)}, bf16[576,128]{1,0:T(8,128)(2,1)S(1)}, u32[]{:S(2)}, u32[]{:S(2)}) collective-permute-start(bf16[576,128]{1,0:T(8,128)(2,1)S(1)} %pad_maximum_fusion.4.refs_0_), channel_id=1, source_target_pairs={{0,24},{8,16},{16,8},{24,0},{1,25},{9,17},{17,9},{25,1},{2,26},{10... | collective-permute-start | bytes 442376 | tf_op jit(solution)/shard_map/ppermute | solution.py:382
  29.0 1.7 %collective-permute-start.9 = (bf16[144,128]{1,0:T(8,128)(2,1)S(1)}, bf16[144,128]{1,0:T(8,128)(2,1)S(1)}, u32[]{:S(2)}, u32[]{:S(2)}) collective-permute-start(bf16[144,128]{1,0:T(8,128)(2,1)S(1)} %get-tuple-element.117), channel_id=1, source_target_pairs={{0,32},{32,0},{1,33},{33,1},{2,34},{34,2},{3,35},{35,3},{4,36},{36... | collective-permute-start | bytes 110600 | tf_op jit(solution)/shard_map/ppermute | solution.py:382
  30.7 0.1 collective-permute-start.14
  30.8 2.1 %collective-permute-done.9 = bf16[144,128]{1,0:T(8,128)(2,1)S(1)} collective-permute-done((bf16[144,128]{1,0:T(8,128)(2,1)S(1)}, bf16[144,128]{1,0:T(8,128)(2,1)S(1)}, u32[]{:S(2)}, u32[]{:S(2)}) %collective-permute-start.9) | collective-permute-done | bytes 36896 | tf_op jit(solution)/shard_map/ppermute | solution.py:382
  33.0 0.3 collective-permute-done.10.refs_1_
  33.3 0.1 collective-permute-start.15
  33.4 2.2 %collective-permute-start.13 = (bf16[288,128]{1,0:T(8,128)(2,1)S(1)}, bf16[288,128]{1,0:T(8,128)(2,1)S(1)}, u32[]{:S(2)}, u32[]{:S(2)}) collective-permute-start(bf16[288,128]{1,0:T(8,128)(2,1)S(1)} %constant_dynamic-update-slice_fusion.refs_0_), channel_id=1, source_target_pairs={{0,24},{8,16},{16,8},{24,0},{1,25},{9,17},{17,9},{25,1},{2,26},{10... | collective-permute-start | bytes 221192 | tf_op jit(solution)/shard_map/ppermute | solution.py:382
  35.6 0.3 collective-permute-start.12
  35.9 1.7 %collective-permute-start.11 = (bf16[288,128]{1,0:T(8,128)(2,1)S(1)}, bf16[288,128]{1,0:T(8,128)(2,1)S(1)}, u32[]{:S(2)}, u32[]{:S(2)}) collective-permute-start(bf16[288,128]{1,0:T(8,128)(2,1)S(1)} %constant_dynamic-update-slice_fusion.refs_0_), channel_id=1, source_target_pairs={{0,8},{8,0},{16,24},{24,16},{1,9},{9,1},{17,25},{25,17},{2,10},{10... | collective-permute-start | bytes 221192 | tf_op jit(solution)/shard_map/ppermute | solution.py:382
  37.6 5.0 %forward.1 = (f32[1152,128]{1,0:T(8,128)S(1)}, f32[8,1152]{1,0:T(8,128)S(1)}, bf16[1152,128]{1,0:T(8,128)(2,1)S(1)}, bf16[1152,128]{1,0:T(8,128)(2,1)S(1)}, bf16...) custom-call(bf16[576,128]{1,0:T(8,128)(2,1)S(1)} %pad_maximum_fusion.4.refs_0_, ...), custom_call_target="tpu_custom_call" | custom-call | flops 2038431744 | bytes 1048576 | tf_op jit(solution)/shard_map/forward/pallas_call | solution.py:47
  42.7 0.4 share.1
  43.1 0.4 collective-permute-start.16
  43.5 3.3 %collective-permute-start.17 = (bf16[368,128]{1,0:T(8,128)(2,1)S(1)}, bf16[368,128]{1,0:T(8,128)(2,1)S(1)}, u32[]{:S(2)}, u32[]{:S(2)}) collective-permute-start(bf16[368,128]{1,0:T(8,128)(2,1)S(1)} %get-tuple-element.127), channel_id=1, source_target_pairs={{0,16},{8,24},{16,0},{24,8},{1,17},{9,25},{17,1},{25,9},{2,18},{10... | collective-permute-start | bytes 282632 | tf_op jit(solution)/shard_map/ppermute | solution.py:382
  46.7 1.1 %collective-permute-start.18 = (bf16[368,128]{1,0:T(8,128)(2,1)S(1)}, bf16[368,128]{1,0:T(8,128)(2,1)S(1)}, u32[]{:S(2)}, u32[]{:S(2)}) collective-permute-start(bf16[368,128]{1,0:T(8,128)(2,1)S(1)} %get-tuple-element.128), channel_id=1, source_target_pairs={{0,24},{8,16},{16,8},{24,0},{1,25},{9,17},{17,9},{25,1},{2,26},{10... | collective-permute-start | bytes 282632 | tf_op jit(solution)/shard_map/ppermute | solution.py:382
  47.9 0.7 collective-permute-done.16.l1_ref
  48.5 2.6 %collective-permute-done.17.l2_ref = bf16[368,128]{1,0:T(8,128)(2,1)S(1)} collective-permute-done((bf16[368,128]{1,0:T(8,128)(2,1)S(1)}, bf16[368,128]{1,0:T(8,128)(2,1)S(1)}, u32[]{:S(2)}, u32[]{:S(2)}) %collective-permute-start.17) | collective-permute-done | bytes 94240 | tf_op jit(solution)/shard_map/ppermute | solution.py:382
  51.1 1.6 %collective-permute-done.18.l3_ref = bf16[368,128]{1,0:T(8,128)(2,1)S(1)} collective-permute-done((bf16[368,128]{1,0:T(8,128)(2,1)S(1)}, bf16[368,128]{1,0:T(8,128)(2,1)S(1)}, u32[]{:S(2)}, u32[]{:S(2)}) %collective-permute-start.18) | collective-permute-done | bytes 94240 | tf_op jit(solution)/shard_map/ppermute | solution.py:382
  52.7 0.9 merge.1
  53.6 1.8 %collective-permute-start.19 = (bf16[144,128]{1,0:T(8,128)(2,1)S(1)}, bf16[144,128]{1,0:T(8,128)(2,1)S(1)}, u32[]{:S(2)}, u32[]{:S(2)}) collective-permute-start(bf16[144,128]{1,0:T(8,128)(2,1)S(1)} %get-tuple-element.130), channel_id=1, source_target_pairs={{0,32},{32,0},{1,33},{33,1},{2,34},{34,2},{3,35},{35,3},{4,36},{36... | collective-permute-start | bytes 110600 | tf_op jit(solution)/shard_map/ppermute | solution.py:382
  55.4 2.8 %backward_one.1 = (bf16[768,256]{1,0:T(8,128)(2,1)S(1)}, f32[1152,128]{1,0:T(8,128)S(1)}) custom-call(bf16[1152,128]{1,0:T(8,128)(2,1)S(1)} %get-tuple-element.132.q_ref, bf16[1152,128]{1,0:T(8,128)(2,1)S(1)} %get-tuple-element.133.qm_ref, bf16[1152,128]{1,0:T(8,128)(2,1)S(1)} %get-tuple-element.134.da_ref, bf16[2304,256]{1,0:T(8,128)(2,1)S(1)} %get-tuple-element.135.kv_ref, ...), custom_call_target="tpu_custom_call" | custom-call | flops 1358954496 | bytes 1048576 | tf_op jit(solution)/shard_map/backward_one/pallas_call | solution.py:47
  58.2 1.2 %project.1 = (bf16[136,512]{1,0:T(8,128)(2,1)S(1)}, bf16[136,512]{1,0:T(8,128)(2,1)S(1)}, bf16[136,512]{1,0:T(8,128)(2,1)S(1)}, bf16[136,512]{1,0:T(8,128)(2,1)S...) custom-call(s32[5]{0:T(128)S(1)} %stack.23.at_ref, ...), custom_call_target="tpu_custom_call" | custom-call | tf_op jit(solution)/shard_map/project/pallas_call | solution.py:47
  59.4 0.3 collective-permute-start.20
  59.7 1.6 %backward_two.1 = (bf16[8,288,128]{2,1,0:T(8,128)(2,1)S(1)}, f32[1152,128]{1,0:T(8,128)S(1)}) custom-call(bf16[1152,128]{1,0:T(8,128)(2,1)S(1)} %get-tuple-element.132.q_ref, bf16[1152,128]{1,0:T(8,128)(2,1)S(1)} %get-tuple-element.133.qm_ref, bf16[1152,128]{1,0:T(8,128)(2,1)S(1)} %get-tuple-element.134.da_ref, ...), custom_call_target="tpu_custom_call" | custom-call | flops 679477248 | bytes 1048576 | tf_op jit(solution)/shard_map/backward_two/pallas_call | solution.py:47
  61.3 0.6 collective-permute-start.22
  61.9 0.1 dwo.1
  62.0 1.3 %collective-permute-start.21 = (bf16[512,256]{1,0:T(8,128)(2,1)S(1)}, bf16[512,256]{1,0:T(8,128)(2,1)S(1)}, u32[]{:S(2)}, u32[]{:S(2)}) collective-permute-start(bf16[512,256]{1,0:T(8,128)(2,1)S(1)} %get-tuple-element.151), channel_id=1, source_target_pairs={{0,24},{4,12},{8,16},{12,4},{16,8},{20,28},{24,0},{28,20},{1,25},{... | collective-permute-start | bytes 786440 | tf_op jit(solution)/shard_map/ppermute | solution.py:387
  63.2 4.1 %backward_three.1 = (bf16[8,288,128]{2,1,0:T(8,128)(2,1)S(1)}, f32[576,128]{1,0:T(8,128)S(1)}, bf16[576,128]{1,0:T(8,128)(2,1)S(1)}) custom-call(bf16[1152,128]{1,0:T(8,128)(2,1)S(1)} %get-tuple-element.132.q_ref, bf16[1152,128]{1,0:T(8,128)(2,1)S(1)} %get-tuple-element.133.qm_ref, bf16[1152,128]{1,0:T(8,128)(2,1)S(1)} %get-tuple-element.134.da_ref, ...), custom_call_target="tpu_custom_call" | custom-call | flops 2038431744 | bytes 1048576 | tf_op jit(solution)/shard_map/backward_three/pallas_call | solution.py:47
  67.4 0.1 collective-permute-start.25
  67.5 0.2 core.1
  67.6 2.1 %collective-permute-start.24 = (bf16[576,128]{1,0:T(8,128)(2,1)S(1)}, bf16[576,128]{1,0:T(8,128)(2,1)S(1)}, u32[]{:S(2)}, u32[]{:S(2)}) collective-permute-start(bf16[576,128]{1,0:T(8,128)(2,1)S(1)} %get-tuple-element.157), channel_id=1, source_target_pairs={{0,192},{64,128},{128,64},{192,0},{1,193},{65,129},{129,65},{193,1... | collective-permute-start | bytes 442376 | tf_op jit(solution)/shard_map/ppermute | solution.py:382
  69.8 1.5 %collective-permute-start.23 = (bf16[576,128]{1,0:T(8,128)(2,1)S(1)}, bf16[576,128]{1,0:T(8,128)(2,1)S(1)}, u32[]{:S(2)}, u32[]{:S(2)}) collective-permute-start(bf16[576,128]{1,0:T(8,128)(2,1)S(1)} %get-tuple-element.156), channel_id=1, source_target_pairs={{0,64},{64,0},{128,192},{192,128},{1,65},{65,1},{129,193},{193,129... | collective-permute-start | bytes 442376 | tf_op jit(solution)/shard_map/ppermute | solution.py:382
  71.3 1.7 %collective-permute-start.27 = (bf16[136,512]{1,0:T(8,128)(2,1)S(1)}, bf16[136,512]{1,0:T(8,128)(2,1)S(1)}, u32[]{:S(2)}, u32[]{:S(2)}) collective-permute-start(bf16[136,512]{1,0:T(8,128)(2,1)S(1)} %get-tuple-element.165), channel_id=1, source_target_pairs={{0,1},{1,2},{2,3},{3,0},{4,5},{5,6},{6,7},{7,4},{8,9},{9,10},{10,1... | collective-permute-start | bytes 417800 | tf_op jit(solution)/shard_map/ppermute | solution.py:378
  73.0 0.4 collective-permute-start.28
  73.4 1.9 %collective-permute-start.26 = (bf16[256,256]{1,0:T(8,128)(2,1)S(1)}, bf16[256,256]{1,0:T(8,128)(2,1)S(1)}, u32[]{:S(2)}, u32[]{:S(2)}) collective-permute-start(bf16[256,256]{1,0:T(8,128)(2,1)S(1)} %get-tuple-element.164), channel_id=1, source_target_pairs={{0,8},{4,28},{8,0},{12,20},{16,24},{20,12},{24,16},{28,4},{1,9},{5... | collective-permute-start | bytes 393224 | tf_op jit(solution)/shard_map/ppermute | solution.py:387
  75.3 1.3 %collective-permute-done.24.refs_3_ = bf16[576,128]{1,0:T(8,128)(2,1)S(1)} collective-permute-done((bf16[576,128]{1,0:T(8,128)(2,1)S(1)}, bf16[576,128]{1,0:T(8,128)(2,1)S(1)}, u32[]{:S(2)}, u32[]{:S(2)}) %collective-permute-start.24) | collective-permute-done | bytes 147488 | tf_op jit(solution)/shard_map/ppermute | solution.py:382
  76.6 2.3 %collective-permute-start.30 = (bf16[136,512]{1,0:T(8,128)(2,1)S(1)}, bf16[136,512]{1,0:T(8,128)(2,1)S(1)}, u32[]{:S(2)}, u32[]{:S(2)}) collective-permute-start(bf16[136,512]{1,0:T(8,128)(2,1)S(1)} %get-tuple-element.171), channel_id=1, source_target_pairs={{0,2},{1,3},{2,0},{3,1},{4,6},{5,7},{6,4},{7,5},{8,10},{9,11},{10,... | collective-permute-start | bytes 417800 | tf_op jit(solution)/shard_map/ppermute | solution.py:378
  78.9 0.7 collective-permute-done.23.refs_1_
  79.6 3.9 %collective-permute-start.29 = (bf16[128,256]{1,0:T(8,128)(2,1)S(1)}, bf16[128,256]{1,0:T(8,128)(2,1)S(1)}, u32[]{:S(2)}, u32[]{:S(2)}) collective-permute-start(bf16[128,256]{1,0:T(8,128)(2,1)S(1)} %get-tuple-element.170), channel_id=1, source_target_pairs={{0,192},{64,128},{128,64},{192,0},{1,193},{65,129},{129,65},{193,1... | collective-permute-start | bytes 196616 | tf_op jit(solution)/shard_map/ppermute | solution.py:382
  83.7 0.4 collective-permute-start.32
  84.0 3.3 %collective-permute-start.33 = (bf16[288,128]{1,0:T(8,128)(2,1)S(1)}, bf16[288,128]{1,0:T(8,128)(2,1)S(1)}, u32[]{:S(2)}, u32[]{:S(2)}) collective-permute-start(bf16[288,128]{1,0:T(8,128)(2,1)S(1)} %get-tuple-element.189), channel_id=1, source_target_pairs={{0,64},{64,0},{128,192},{192,128},{1,65},{65,1},{129,193},{193,129... | collective-permute-start | bytes 221192 | tf_op jit(solution)/shard_map/ppermute | solution.py:382
  87.4 1.2 %collective-permute-start.31 = (bf16[288,128]{1,0:T(8,128)(2,1)S(1)}, bf16[288,128]{1,0:T(8,128)(2,1)S(1)}, u32[]{:S(2)}, u32[]{:S(2)}) collective-permute-start(bf16[288,128]{1,0:T(8,128)(2,1)S(1)} %get-tuple-element.185), channel_id=1, source_target_pairs={{0,24},{8,16},{16,8},{24,0},{1,25},{9,17},{17,9},{25,1},{2,26},{10... | collective-permute-start | bytes 221192 | tf_op jit(solution)/shard_map/ppermute | solution.py:382
  88.6 3.3 %collective-permute-start.34 = (bf16[64,256]{1,0:T(8,128)(2,1)S(1)}, bf16[64,256]{1,0:T(8,128)(2,1)S(1)}, u32[]{:S(2)}, u32[]{:S(2)}) collective-permute-start(bf16[64,256]{1,0:T(8,128)(2,1)S(1)} %get-tuple-element.191), channel_id=1, source_target_pairs={{0,64},{64,0},{128,192},{192,128},{1,65},{65,1},{129,193},{193,129... | collective-permute-start | bytes 98312 | tf_op jit(solution)/shard_map/ppermute | solution.py:382
  92.0 1.9 %collective-permute-done.34.refs_7_ = bf16[64,256]{1,0:T(8,128)(2,1)S(1)} collective-permute-done((bf16[64,256]{1,0:T(8,128)(2,1)S(1)}, bf16[64,256]{1,0:T(8,128)(2,1)S(1)}, u32[]{:S(2)}, u32[]{:S(2)}) %collective-permute-start.34) | collective-permute-done | bytes 32800 | tf_op jit(solution)/shard_map/ppermute | solution.py:382
  93.9 2.9 %collective-permute-start.35 = (bf16[496,128]{1,0:T(8,128)(2,1)S(1)}, bf16[496,128]{1,0:T(8,128)(2,1)S(1)}, u32[]{:S(2)}, u32[]{:S(2)}) collective-permute-start(bf16[496,128]{1,0:T(8,128)(2,1)S(1)} %get-tuple-element.194), channel_id=1, source_target_pairs={{0,32},{32,0},{1,33},{33,1},{2,34},{34,2},{3,35},{35,3},{4,36},{36... | collective-permute-start | bytes 380936 | tf_op jit(solution)/shard_map/ppermute | solution.py:382
  96.8 0.7 add_convert_fusion
  97.5 2.2 %collective-permute-done.35.got_ref = bf16[496,128]{1,0:T(8,128)(2,1)S(1)} collective-permute-done((bf16[496,128]{1,0:T(8,128)(2,1)S(1)}, bf16[496,128]{1,0:T(8,128)(2,1)S(1)}, u32[]{:S(2)}, u32[]{:S(2)}) %collective-permute-start.35) | collective-permute-done | bytes 127008 | tf_op jit(solution)/shard_map/ppermute | solution.py:382
  99.7 1.3 %place.1 = (bf16[136,256]{1,0:T(8,128)(2,1)}, bf16[136,256]{1,0:T(8,128)(2,1)}, bf16[136,256]{1,0:T(8,128)(2,1)}, f32[32,256]{1,0:T(8,128)}) custom-call(s32[5]{0:T(128)S(1)} %stack.23.at_ref, bf16[144,384]{1,0:T(8,128)(2,1)S(1)} %get-tuple-element.192.mine_ref, f32[32,256]{1,0:T(8,128)S(1)} %get-tuple-element.193.wmine_ref, ...), custom_call_target="tpu_custom_call" | custom-call | tf_op jit(solution)/shard_map/place/pallas_call | solution.py:47
  (49 shorter events, 0.6 us)
Async XLA Ops:
  0.6 6.6 %copy-start = (bf16[256,2048]{1,0:T(8,128)(2,1)S(1)}, bf16[256,2048]{1,0:T(8,128)(2,1)}, u32[]{:S(2)}) copy-start(bf16[256,2048]{1,0:T(8,128)(2,1)} %param.10) | copy-start | bytes 3145732
  3.2 5.1 %collective-permute-start = (bf16[432,128]{1,0:T(8,128)(2,1)S(1)}, bf16[432,128]{1,0:T(8,128)(2,1)S(1)}, u32[]{:S(2)}, u32[]{:S(2)}) collective-permute-start(bf16[432,128]{1,0:T(8,128)(2,1)S(1)} %get-tuple-element.103), channel_id=1, source_target_pairs={{0,32},{32,0},{1,33},{33,1},{2,34},{34,2},{3,35},{35,3},{4,36},{36... | collective-permute-start | bytes 331784 | tf_op jit(solution)/shard_map/ppermute | solution.py:382
  5.2 19.7 %collective-permute-start.5 = (bf16[136,512]{1,0:T(8,128)(2,1)S(1)}, bf16[136,512]{1,0:T(8,128)(2,1)S(1)}, u32[]{:S(2)}, u32[]{:S(2)}) collective-permute-start(bf16[136,512]{1,0:T(8,128)(2,1)S(1)} %get-tuple-element.109.refs_0_.dy0_ref), channel_id=1, source_target_pairs={{0,3},{1,0},{2,1},{3,2},{4,7},{5,4},{6,5},{7,6},{8,11},{9,8},{10,9... | collective-permute-start | bytes 417800 | tf_op jit(solution)/shard_map/ppermute | solution.py:378
  5.6 20.1 %collective-permute-start.3 = (bf16[136,512]{1,0:T(8,128)(2,1)S(1)}, bf16[136,512]{1,0:T(8,128)(2,1)S(1)}, u32[]{:S(2)}, u32[]{:S(2)}) collective-permute-start(bf16[136,512]{1,0:T(8,128)(2,1)S(1)} %get-tuple-element.109.refs_0_.dy0_ref), channel_id=1, source_target_pairs={{0,1},{1,2},{2,3},{3,0},{4,5},{5,6},{6,7},{7,4},{8,9},{9,10},{10,1... | collective-permute-start | bytes 417800 | tf_op jit(solution)/shard_map/ppermute | solution.py:378
  8.3 10.2 %collective-permute-start.1 = (bf16[288,128]{1,0:T(8,128)(2,1)S(1)}, bf16[288,128]{1,0:T(8,128)(2,1)S(1)}, u32[]{:S(2)}, u32[]{:S(2)}) collective-permute-start(bf16[288,128]{1,0:T(8,128)(2,1)S(1)} %pad_maximum_fusion.5), channel_id=1, source_target_pairs={{0,64},{64,0},{128,192},{192,128},{1,65},{65,1},{129,193},{193,129... | collective-permute-start | bytes 221192 | tf_op jit(solution)/shard_map/ppermute | solution.py:382
  11.6 7.2 %collective-permute-start.2 = (bf16[288,128]{1,0:T(8,128)(2,1)S(1)}, bf16[288,128]{1,0:T(8,128)(2,1)S(1)}, u32[]{:S(2)}, u32[]{:S(2)}) collective-permute-start(bf16[288,128]{1,0:T(8,128)(2,1)S(1)} %pad_maximum_fusion.6), channel_id=1, source_target_pairs={{0,192},{64,128},{128,64},{192,0},{1,193},{65,129},{129,65},{193,1... | collective-permute-start | bytes 221192 | tf_op jit(solution)/shard_map/ppermute | solution.py:382
  16.1 9.7 %collective-permute-start.4 = (bf16[136,512]{1,0:T(8,128)(2,1)S(1)}, bf16[136,512]{1,0:T(8,128)(2,1)S(1)}, u32[]{:S(2)}, u32[]{:S(2)}) collective-permute-start(bf16[136,512]{1,0:T(8,128)(2,1)S(1)} %get-tuple-element.109.refs_0_.dy0_ref), channel_id=1, source_target_pairs={{0,2},{1,3},{2,0},{3,1},{4,6},{5,7},{6,4},{7,5},{8,10},{9,11},{10,... | collective-permute-start | bytes 417800 | tf_op jit(solution)/shard_map/ppermute | solution.py:378
  18.9 6.8 %collective-permute-start.6 = (bf16[288,128]{1,0:T(8,128)(2,1)S(1)}, bf16[288,128]{1,0:T(8,128)(2,1)S(1)}, u32[]{:S(2)}, u32[]{:S(2)}) collective-permute-start(bf16[288,128]{1,0:T(8,128)(2,1)S(1)} %pad_maximum_fusion.7), channel_id=1, source_target_pairs={{0,8},{8,0},{16,24},{24,16},{1,9},{9,1},{17,25},{25,17},{2,10},{10... | collective-permute-start | bytes 221192 | tf_op jit(solution)/shard_map/ppermute | solution.py:382
  20.5 12.5 %collective-permute-start.7 = (bf16[576,128]{1,0:T(8,128)(2,1)S(1)}, bf16[576,128]{1,0:T(8,128)(2,1)S(1)}, u32[]{:S(2)}, u32[]{:S(2)}) collective-permute-start(bf16[576,128]{1,0:T(8,128)(2,1)S(1)} %pad_maximum_fusion.2), channel_id=1, source_target_pairs={{0,192},{64,128},{128,64},{192,0},{1,193},{65,129},{129,65},{193,1... | collective-permute-start | bytes 442376 | tf_op jit(solution)/shard_map/ppermute | solution.py:382
  24.9 8.1 %collective-permute-start.8 = (bf16[576,128]{1,0:T(8,128)(2,1)S(1)}, bf16[576,128]{1,0:T(8,128)(2,1)S(1)}, u32[]{:S(2)}, u32[]{:S(2)}) collective-permute-start(bf16[576,128]{1,0:T(8,128)(2,1)S(1)} %pad_maximum_fusion.3), channel_id=1, source_target_pairs={{0,64},{64,0},{128,192},{192,128},{1,65},{65,1},{129,193},{193,129... | collective-permute-start | bytes 442376 | tf_op jit(solution)/shard_map/ppermute | solution.py:382
  26.8 6.4 %collective-permute-start.10 = (bf16[576,128]{1,0:T(8,128)(2,1)S(1)}, bf16[576,128]{1,0:T(8,128)(2,1)S(1)}, u32[]{:S(2)}, u32[]{:S(2)}) collective-permute-start(bf16[576,128]{1,0:T(8,128)(2,1)S(1)} %pad_maximum_fusion.4.refs_0_), channel_id=1, source_target_pairs={{0,24},{8,16},{16,8},{24,0},{1,25},{9,17},{17,9},{25,1},{2,26},{10... | collective-permute-start | bytes 442376 | tf_op jit(solution)/shard_map/ppermute | solution.py:382
  29.0 4.0 %collective-permute-start.9 = (bf16[144,128]{1,0:T(8,128)(2,1)S(1)}, bf16[144,128]{1,0:T(8,128)(2,1)S(1)}, u32[]{:S(2)}, u32[]{:S(2)}) collective-permute-start(bf16[144,128]{1,0:T(8,128)(2,1)S(1)} %get-tuple-element.117), channel_id=1, source_target_pairs={{0,32},{32,0},{1,33},{33,1},{2,34},{34,2},{3,35},{35,3},{4,36},{36... | collective-permute-start | bytes 110600 | tf_op jit(solution)/shard_map/ppermute | solution.py:382
  30.7 6.9 %collective-permute-start.14 = (bf16[1152,128]{1,0:T(8,128)(2,1)S(1)}, bf16[1152,128]{1,0:T(8,128)(2,1)S(1)}, u32[]{:S(2)}, u32[]{:S(2)}) collective-permute-start(bf16[1152,128]{1,0:T(8,128)(2,1)S(1)} %constant_dynamic-update-slice_fusion.2.refs_2_), channel_id=1, source_target_pairs={{0,4},{4,0},{1,5},{5,1},{2,6},{6,2},{3,7},{7,3},{8,12},{12,8},{9,1... | collective-permute-start | bytes 884744 | tf_op jit(solution)/shard_map/ppermute | solution.py:382
  33.3 4.3 %collective-permute-start.15 = (bf16[1152,128]{1,0:T(8,128)(2,1)S(1)}, bf16[1152,128]{1,0:T(8,128)(2,1)S(1)}, u32[]{:S(2)}, u32[]{:S(2)}) collective-permute-start(bf16[1152,128]{1,0:T(8,128)(2,1)S(1)} %constant_dynamic-update-slice_fusion.8.refs_3_), channel_id=1, source_target_pairs={{0,4},{4,0},{1,5},{5,1},{2,6},{6,2},{3,7},{7,3},{8,12},{12,8},{9,1... | collective-permute-start | bytes 884744 | tf_op jit(solution)/shard_map/ppermute | solution.py:382
  33.4 9.2 %collective-permute-start.13 = (bf16[288,128]{1,0:T(8,128)(2,1)S(1)}, bf16[288,128]{1,0:T(8,128)(2,1)S(1)}, u32[]{:S(2)}, u32[]{:S(2)}) collective-permute-start(bf16[288,128]{1,0:T(8,128)(2,1)S(1)} %constant_dynamic-update-slice_fusion.refs_0_), channel_id=1, source_target_pairs={{0,24},{8,16},{16,8},{24,0},{1,25},{9,17},{17,9},{25,1},{2,26},{10... | collective-permute-start | bytes 221192 | tf_op jit(solution)/shard_map/ppermute | solution.py:382
  35.6 7.0 %collective-permute-start.12 = (bf16[288,128]{1,0:T(8,128)(2,1)S(1)}, bf16[288,128]{1,0:T(8,128)(2,1)S(1)}, u32[]{:S(2)}, u32[]{:S(2)}) collective-permute-start(bf16[288,128]{1,0:T(8,128)(2,1)S(1)} %constant_dynamic-update-slice_fusion.refs_0_), channel_id=1, source_target_pairs={{0,16},{8,24},{16,0},{24,8},{1,17},{9,25},{17,1},{25,9},{2,18},{10... | collective-permute-start | bytes 221192 | tf_op jit(solution)/shard_map/ppermute | solution.py:382
  35.9 6.8 %collective-permute-start.11 = (bf16[288,128]{1,0:T(8,128)(2,1)S(1)}, bf16[288,128]{1,0:T(8,128)(2,1)S(1)}, u32[]{:S(2)}, u32[]{:S(2)}) collective-permute-start(bf16[288,128]{1,0:T(8,128)(2,1)S(1)} %constant_dynamic-update-slice_fusion.refs_0_), channel_id=1, source_target_pairs={{0,8},{8,0},{16,24},{24,16},{1,9},{9,1},{17,25},{25,17},{2,10},{10... | collective-permute-start | bytes 221192 | tf_op jit(solution)/shard_map/ppermute | solution.py:382
  43.1 5.4 %collective-permute-start.16 = (bf16[368,128]{1,0:T(8,128)(2,1)S(1)}, bf16[368,128]{1,0:T(8,128)(2,1)S(1)}, u32[]{:S(2)}, u32[]{:S(2)}) collective-permute-start(bf16[368,128]{1,0:T(8,128)(2,1)S(1)} %get-tuple-element.126), channel_id=1, source_target_pairs={{0,8},{8,0},{16,24},{24,16},{1,9},{9,1},{17,25},{25,17},{2,10},{10... | collective-permute-start | bytes 282632 | tf_op jit(solution)/shard_map/ppermute | solution.py:382
  43.5 7.6 %collective-permute-start.17 = (bf16[368,128]{1,0:T(8,128)(2,1)S(1)}, bf16[368,128]{1,0:T(8,128)(2,1)S(1)}, u32[]{:S(2)}, u32[]{:S(2)}) collective-permute-start(bf16[368,128]{1,0:T(8,128)(2,1)S(1)} %get-tuple-element.127), channel_id=1, source_target_pairs={{0,16},{8,24},{16,0},{24,8},{1,17},{9,25},{17,1},{25,9},{2,18},{10... | collective-permute-start | bytes 282632 | tf_op jit(solution)/shard_map/ppermute | solution.py:382
  46.7 5.9 %collective-permute-start.18 = (bf16[368,128]{1,0:T(8,128)(2,1)S(1)}, bf16[368,128]{1,0:T(8,128)(2,1)S(1)}, u32[]{:S(2)}, u32[]{:S(2)}) collective-permute-start(bf16[368,128]{1,0:T(8,128)(2,1)S(1)} %get-tuple-element.128), channel_id=1, source_target_pairs={{0,24},{8,16},{16,8},{24,0},{1,25},{9,17},{17,9},{25,1},{2,26},{10... | collective-permute-start | bytes 282632 | tf_op jit(solution)/shard_map/ppermute | solution.py:382
  53.6 4.6 %collective-permute-start.19 = (bf16[144,128]{1,0:T(8,128)(2,1)S(1)}, bf16[144,128]{1,0:T(8,128)(2,1)S(1)}, u32[]{:S(2)}, u32[]{:S(2)}) collective-permute-start(bf16[144,128]{1,0:T(8,128)(2,1)S(1)} %get-tuple-element.130), channel_id=1, source_target_pairs={{0,32},{32,0},{1,33},{33,1},{2,34},{34,2},{3,35},{35,3},{4,36},{36... | collective-permute-start | bytes 110600 | tf_op jit(solution)/shard_map/ppermute | solution.py:382
  59.4 2.5 %collective-permute-start.20 = (bf16[4,256,256]{2,1,0:T(8,128)(2,1)S(1)}, bf16[4,256,256]{2,1,0:T(8,128)(2,1)S(1)}, u32[]{:S(2)}, u32[]{:S(2)}) collective-permute-start(bf16[4,256,256]{2,1,0:T(8,128)(2,1)S(1)} %get-tuple-element.144), channel_id=1, source_target_pairs={{0,4},{4,0},{1,5},{5,1},{2,6},{6,2},{3,7},{7,3},{8,12},{12,8},{9,1... | collective-permute-start | bytes 1572872 | tf_op jit(solution)/shard_map/ppermute | solution.py:382
  61.3 6.2 %collective-permute-start.22 = (bf16[8,288,128]{2,1,0:T(8,128)(2,1)S(1)}, bf16[8,288,128]{2,1,0:T(8,128)(2,1)S(1)}, u32[]{:S(2)}, u32[]{:S(2)}) collective-permute-start(bf16[8,288,128]{2,1,0:T(8,128)(2,1)S(1)} %get-tuple-element.154), channel_id=1, source_target_pairs={{0,4},{4,0},{1,5},{5,1},{2,6},{6,2},{3,7},{7,3},{8,12},{12,8},{9,1... | collective-permute-start | bytes 1769480 | tf_op jit(solution)/shard_map/ppermute | solution.py:382
  62.0 7.8 %collective-permute-start.21 = (bf16[512,256]{1,0:T(8,128)(2,1)S(1)}, bf16[512,256]{1,0:T(8,128)(2,1)S(1)}, u32[]{:S(2)}, u32[]{:S(2)}) collective-permute-start(bf16[512,256]{1,0:T(8,128)(2,1)S(1)} %get-tuple-element.151), channel_id=1, source_target_pairs={{0,24},{4,12},{8,16},{12,4},{16,8},{20,28},{24,0},{28,20},{1,25},{... | collective-permute-start | bytes 786440 | tf_op jit(solution)/shard_map/ppermute | solution.py:387
  67.4 6.0 %collective-permute-start.25 = (bf16[576,128]{1,0:T(8,128)(2,1)S(1)}, bf16[576,128]{1,0:T(8,128)(2,1)S(1)}, u32[]{:S(2)}, u32[]{:S(2)}) collective-permute-start(bf16[576,128]{1,0:T(8,128)(2,1)S(1)} %get-tuple-element.158), channel_id=1, source_target_pairs={{0,8},{8,0},{16,24},{24,16},{1,9},{9,1},{17,25},{25,17},{2,10},{10... | collective-permute-start | bytes 442376 | tf_op jit(solution)/shard_map/ppermute | solution.py:382
  67.6 9.0 %collective-permute-start.24 = (bf16[576,128]{1,0:T(8,128)(2,1)S(1)}, bf16[576,128]{1,0:T(8,128)(2,1)S(1)}, u32[]{:S(2)}, u32[]{:S(2)}) collective-permute-start(bf16[576,128]{1,0:T(8,128)(2,1)S(1)} %get-tuple-element.157), channel_id=1, source_target_pairs={{0,192},{64,128},{128,64},{192,0},{1,193},{65,129},{129,65},{193,1... | collective-permute-start | bytes 442376 | tf_op jit(solution)/shard_map/ppermute | solution.py:382
  69.8 9.8 %collective-permute-start.23 = (bf16[576,128]{1,0:T(8,128)(2,1)S(1)}, bf16[576,128]{1,0:T(8,128)(2,1)S(1)}, u32[]{:S(2)}, u32[]{:S(2)}) collective-permute-start(bf16[576,128]{1,0:T(8,128)(2,1)S(1)} %get-tuple-element.156), channel_id=1, source_target_pairs={{0,64},{64,0},{128,192},{192,128},{1,65},{65,1},{129,193},{193,129... | collective-permute-start | bytes 442376 | tf_op jit(solution)/shard_map/ppermute | solution.py:382
  71.3 7.6 %collective-permute-start.27 = (bf16[136,512]{1,0:T(8,128)(2,1)S(1)}, bf16[136,512]{1,0:T(8,128)(2,1)S(1)}, u32[]{:S(2)}, u32[]{:S(2)}) collective-permute-start(bf16[136,512]{1,0:T(8,128)(2,1)S(1)} %get-tuple-element.165), channel_id=1, source_target_pairs={{0,1},{1,2},{2,3},{3,0},{4,5},{5,6},{6,7},{7,4},{8,9},{9,10},{10,1... | collective-permute-start | bytes 417800 | tf_op jit(solution)/shard_map/ppermute | solution.py:378
  73.0 6.0 %collective-permute-start.28 = (bf16[136,512]{1,0:T(8,128)(2,1)S(1)}, bf16[136,512]{1,0:T(8,128)(2,1)S(1)}, u32[]{:S(2)}, u32[]{:S(2)}) collective-permute-start(bf16[136,512]{1,0:T(8,128)(2,1)S(1)} %get-tuple-element.166), channel_id=1, source_target_pairs={{0,3},{1,0},{2,1},{3,2},{4,7},{5,4},{6,5},{7,6},{8,11},{9,8},{10,9... | collective-permute-start | bytes 417800 | tf_op jit(solution)/shard_map/ppermute | solution.py:378
  73.4 5.5 %collective-permute-start.26 = (bf16[256,256]{1,0:T(8,128)(2,1)S(1)}, bf16[256,256]{1,0:T(8,128)(2,1)S(1)}, u32[]{:S(2)}, u32[]{:S(2)}) collective-permute-start(bf16[256,256]{1,0:T(8,128)(2,1)S(1)} %get-tuple-element.164), channel_id=1, source_target_pairs={{0,8},{4,28},{8,0},{12,20},{16,24},{20,12},{24,16},{28,4},{1,9},{5... | collective-permute-start | bytes 393224 | tf_op jit(solution)/shard_map/ppermute | solution.py:387
  76.6 10.8 %collective-permute-start.30 = (bf16[136,512]{1,0:T(8,128)(2,1)S(1)}, bf16[136,512]{1,0:T(8,128)(2,1)S(1)}, u32[]{:S(2)}, u32[]{:S(2)}) collective-permute-start(bf16[136,512]{1,0:T(8,128)(2,1)S(1)} %get-tuple-element.171), channel_id=1, source_target_pairs={{0,2},{1,3},{2,0},{3,1},{4,6},{5,7},{6,4},{7,5},{8,10},{9,11},{10,... | collective-permute-start | bytes 417800 | tf_op jit(solution)/shard_map/ppermute | solution.py:378
  79.6 7.7 %collective-permute-start.29 = (bf16[128,256]{1,0:T(8,128)(2,1)S(1)}, bf16[128,256]{1,0:T(8,128)(2,1)S(1)}, u32[]{:S(2)}, u32[]{:S(2)}) collective-permute-start(bf16[128,256]{1,0:T(8,128)(2,1)S(1)} %get-tuple-element.170), channel_id=1, source_target_pairs={{0,192},{64,128},{128,64},{192,0},{1,193},{65,129},{129,65},{193,1... | collective-permute-start | bytes 196616 | tf_op jit(solution)/shard_map/ppermute | solution.py:382
  83.7 8.3 %collective-permute-start.32 = (bf16[288,128]{1,0:T(8,128)(2,1)S(1)}, bf16[288,128]{1,0:T(8,128)(2,1)S(1)}, u32[]{:S(2)}, u32[]{:S(2)}) collective-permute-start(bf16[288,128]{1,0:T(8,128)(2,1)S(1)} %get-tuple-element.187), channel_id=1, source_target_pairs={{0,192},{64,128},{128,64},{192,0},{1,193},{65,129},{129,65},{193,1... | collective-permute-start | bytes 221192 | tf_op jit(solution)/shard_map/ppermute | solution.py:382
  84.0 7.9 %collective-permute-start.33 = (bf16[288,128]{1,0:T(8,128)(2,1)S(1)}, bf16[288,128]{1,0:T(8,128)(2,1)S(1)}, u32[]{:S(2)}, u32[]{:S(2)}) collective-permute-start(bf16[288,128]{1,0:T(8,128)(2,1)S(1)} %get-tuple-element.189), channel_id=1, source_target_pairs={{0,64},{64,0},{128,192},{192,128},{1,65},{65,1},{129,193},{193,129... | collective-permute-start | bytes 221192 | tf_op jit(solution)/shard_map/ppermute | solution.py:382
  87.4 6.4 %collective-permute-start.31 = (bf16[288,128]{1,0:T(8,128)(2,1)S(1)}, bf16[288,128]{1,0:T(8,128)(2,1)S(1)}, u32[]{:S(2)}, u32[]{:S(2)}) collective-permute-start(bf16[288,128]{1,0:T(8,128)(2,1)S(1)} %get-tuple-element.185), channel_id=1, source_target_pairs={{0,24},{8,16},{16,8},{24,0},{1,25},{9,17},{17,9},{25,1},{2,26},{10... | collective-permute-start | bytes 221192 | tf_op jit(solution)/shard_map/ppermute | solution.py:382
  88.6 5.2 %collective-permute-start.34 = (bf16[64,256]{1,0:T(8,128)(2,1)S(1)}, bf16[64,256]{1,0:T(8,128)(2,1)S(1)}, u32[]{:S(2)}, u32[]{:S(2)}) collective-permute-start(bf16[64,256]{1,0:T(8,128)(2,1)S(1)} %get-tuple-element.191), channel_id=1, source_target_pairs={{0,64},{64,0},{128,192},{192,128},{1,65},{65,1},{129,193},{193,129... | collective-permute-start | bytes 98312 | tf_op jit(solution)/shard_map/ppermute | solution.py:382
  93.9 5.8 %collective-permute-start.35 = (bf16[496,128]{1,0:T(8,128)(2,1)S(1)}, bf16[496,128]{1,0:T(8,128)(2,1)S(1)}, u32[]{:S(2)}, u32[]{:S(2)}) collective-permute-start(bf16[496,128]{1,0:T(8,128)(2,1)S(1)} %get-tuple-element.194), channel_id=1, source_target_pairs={{0,32},{32,0},{1,33},{33,1},{2,34},{34,2},{3,35},{35,3},{4,36},{36... | collective-permute-start | bytes 380936 | tf_op jit(solution)/shard_map/ppermute | solution.py:382
